TPU v7x, 128 devices: a whole 4x4x4 slice. The times are simulated.
128 devices in a mesh: ctx: 32 (over x, y_hi, z), fsdp: 4 (over y_lo, core).
Axes of the slice: x: 4, y: 4 (y_hi: 2, y_lo: 2; y = y_hi * 2 + y_lo), z: 4, core: 2. Of those that a mesh axis runs over, the one named last changes fastest.
Arguments:
- query: bfloat16 [4, 8192, 4096], P('fsdp', None, 'ctx'), may hold values from -6 to 6
- gated: bfloat16 [4, 8192, 4096], P('fsdp', None, 'ctx'), may hold values from -6 to 6
- grad_out: bfloat16 [4, 8192, 4096], P('fsdp', None, 'ctx'), may hold values from -6 to 6
- filters: float32 [512, 128], P('fsdp'), may hold values from -0.5 to 0.5
Outputs:
- grad_query: bfloat16 [4, 8192, 4096], P('fsdp', None, 'ctx')
- grad_gated: bfloat16 [4, 8192, 4096], P('fsdp', None, 'ctx')
- grad_filters: float32 [512, 128], P('fsdp')
All inputs are finite; a program needn't handle non-finite values.
Results may differ from a plain program's by a relative error of at most 0.0058.
Values may be sent and summed in bfloat16 or wider, within the bound.
No kernel may reach another device: no remote copies, remote signals or barrier semaphores. Data moves between devices by JAX's collectives and lax.ppermute only.
A program may use at most 384 MiB of HBM per device.

v0:
```python
import math

import jax
import jax.numpy as jnp
from jax import lax
from jax.sharding import PartitionSpec as P

FLEN = 128
GROUP_CH = 16


def shifted(block, axis, distance):
    devices = range(lax.axis_size(axis))
    route = [(i - distance, i) for i in devices if i - distance in devices]
    return lax.ppermute(block, axis, route)


def build_band(taps):
    groups, length = taps.shape
    row = jnp.concatenate([taps[:, ::-1], jnp.zeros((groups, length + 1), taps.dtype)], axis=1)
    flat = jnp.tile(row, (1, length))
    flat = jnp.concatenate([jnp.zeros((groups, 1), taps.dtype), flat], axis=1)[
        :, : length * 2 * length
    ]
    return flat.reshape(groups, length, 2 * length)


def fold_taps(outer):
    groups, length = (outer.shape[0], outer.shape[1])
    flat = outer.reshape(groups, length * 2 * length)
    flat = jnp.concatenate([flat, jnp.zeros((groups, length + 1), outer.dtype)], axis=1)
    skewed = flat[:, 1 : 1 + length * (2 * length + 1)].reshape(groups, length, 2 * length + 1)[
        :, :, :length
    ]
    return jnp.sum(skewed, axis=1)[:, ::-1]


def per_device(query, gated, grad_out, filters):
    query = query[0]
    gated = gated[0]
    grad_out = grad_out[0]
    width, rows = gated.shape
    groups = width // GROUP_CH
    nblocks = rows // FLEN
    taps = lax.all_gather(filters.astype(jnp.bfloat16), "fsdp", axis=0, tiled=True)
    band = build_band(taps)
    grad_core = (grad_out.astype(jnp.float32) * query).astype(jnp.bfloat16)
    below = shifted(gated, "ctx", 1)
    above = shifted(grad_core, "ctx", -1)
    stacked = jnp.concatenate([below[:, None], gated.reshape(width, nblocks, FLEN)], axis=1)
    windows = jnp.concatenate([stacked[:, :-1], stacked[:, 1:]], axis=2).reshape(
        groups, GROUP_CH, nblocks, 2 * FLEN
    )
    conv = jnp.einsum("gim,gcnm->gcni", band, windows, preferred_element_type=jnp.float32).reshape(
        width, rows
    )
    grad_query = (grad_out.astype(jnp.float32) * conv).astype(jnp.bfloat16)
    core_blocks = grad_core.reshape(groups, GROUP_CH, nblocks, FLEN)
    spread = jnp.einsum("gim,gcni->gcnm", band, core_blocks, preferred_element_type=jnp.float32)
    tail = jnp.einsum(
        "gim,gci->gcm",
        band[:, :, :FLEN],
        above.reshape(groups, GROUP_CH, FLEN),
        preferred_element_type=jnp.float32,
    )
    later = jnp.concatenate([spread[:, :, 1:, :FLEN], tail[:, :, None]], axis=2)
    grad_gated = (spread[:, :, :, FLEN:] + later).reshape(width, rows).astype(jnp.bfloat16)
    outer = jnp.einsum("gcni,gcnm->gim", core_blocks, windows, preferred_element_type=jnp.float32)
    partial_taps = fold_taps(outer)
    summed = lax.psum(partial_taps, "ctx")
    tap_sums = lax.psum_scatter(summed, "fsdp", scatter_dimension=0, tiled=True)
    count = lax.axis_size("fsdp") * lax.axis_size("ctx") * rows * GROUP_CH
    grad_filters = tap_sums * (1.0 / math.sqrt(count))
    return (grad_query[None], grad_gated[None], grad_filters)


def solution(mesh):
    return jax.shard_map(
        per_device,
        mesh=mesh,
        in_specs=(
            P("fsdp", None, "ctx"),
            P("fsdp", None, "ctx"),
            P("fsdp", None, "ctx"),
            P("fsdp", None),
        ),
        out_specs=(P("fsdp", None, "ctx"), P("fsdp", None, "ctx"), P("fsdp", None)),
        check_vma=False,
    )
```

profile of v0, /device:TPU:0, one launch (start us, length us, event | category | flops | bytes accessed | tf_op | source)
XLA Modules:
  0.0 812.6 jit_solution(10981790452433031120)
XLA Ops:
  7.2 5.2 collective-permute-start
  12.4 0.8 convert_element_type.51
  13.3 5.4 all_gather.3
  18.7 0.4 rev.6
  19.1 0.1 copy.16
  19.2 11.6 %tile.4 = bf16[512,128,257]{0,2,1:T(8,128)(2,1)} broadcast(bf16[512,257]{0,1:T(8,128)(2,1)S(1)} %concatenate.20.clone), dimensions={0,2} | broadcast | bytes 33948672 | tf_op jit(solution)/shard_map/tile | solution.py:21
  30.9 30.6 %tile.10 = bf16[512,32896]{0,1:T(8,128)(2,1)} reshape(bf16[512,128,257]{0,2,1:T(8,128)(2,1)} %tile.4) | data formatting | bytes 67371008 | tf_op jit(solution)/shard_map/tile | solution.py:21
  61.4 23.3 %pad_slice_fusion.1 = bf16[512,32768]{0,1:T(8,128)(2,1)} fusion(bf16[512,32896]{0,1:T(8,128)(2,1)} %tile.10), kind=kLoop, calls=%fused_computation.1 | loop fusion | bytes 67239936 | tf_op jit(solution)/shard_map/slice | solution.py:22
  84.7 45.7 %copy.14 = bf16[512,128,256]{2,1,0:T(8,128)(2,1)} copy(bf16[512,128,256]{0,2,1:T(8,128)(2,1)} %bitcast.28) | data formatting | bytes 67108864 | tf_op jit(solution)/shard_map/reshape | solution.py:25
  130.4 17.1 %fusion.6 = f32[512,16,128]{2,1,0:T(8,128)} fusion(bf16[512,128,256]{2,1,0:T(8,128)(2,1)} %copy.14, bf16[512,16,1,128]{3,1,0,2:T(8,128)(2,1)S(1)} %bitcast.35, bf16[512,16,1,128]{3,1,0,2:T(8,128)(2,1)} %bitcast.1), kind=kOutput, calls=%fused_computation.14 | convolution fusion | flops 545259520 | bytes 41943040 | tf_op jit(solution)/shard_map/gim,gcnm->gcni/dot_general | solution.py:54
  147.5 5.6 fusion.3
  153.1 25.8 %fusion.5 = f32[512,128,256]{2,1,0:T(8,128)} fusion(bf16[512,16,128]{2,1,0:T(8,128)(2,1)S(1)} %bitcast.29, bf16[512,16,1,128]{3,1,0,2:T(8,128)(2,1)} %bitcast.34, bf16[512,16,1,128]{3,1,0,2:T(8,128)(2,1)} %bitcast.1), kind=kOutput, calls=%fused_computation.13 | convolution fusion | flops 545259520 | bytes 73400320 | tf_op jit(solution)/shard_map/gcni,gcnm->gim/dot_general | solution.py:68
  178.9 69.3 %copy.15 = f32[512,128,256]{0,2,1:T(8,128)} copy(f32[512,128,256]{2,1,0:T(8,128)} %fusion.5) | data formatting | bytes 134217728 | tf_op jit(solution)/shard_map/reshape | solution.py:30
  248.2 43.3 %pad_slice_fusion = f32[512,32896]{0,1:T(8,128)} fusion(f32[512,32768]{0,1:T(8,128)} %bitcast.12), kind=kLoop, calls=%fused_computation | loop fusion | bytes 134479872 | tf_op jit(solution)/shard_map/slice | solution.py:32
  291.5 76.0 %reshape.72 = f32[512,128,257]{0,2,1:T(8,128)} reshape(f32[512,32896]{0,1:T(8,128)} %pad_slice_fusion) | data formatting | bytes 134742016 | tf_op jit(solution)/shard_map/reshape | solution.py:32
  367.5 12.0 %slice_reduce_fusion = f32[512,128]{0,1:T(8,128)S(1)} fusion(f32[512,128,257]{0,2,1:T(8,128)} %reshape.72), kind=kLoop, calls=%fused_computation.2 | loop fusion | flops 8323072 | bytes 33816576 | tf_op jit(solution)/shard_map/reduce_sum | solution.py:35
  379.5 1.3 rev.7
  380.9 1.5 collective-permute-start.1
  382.4 58.9 %reduce-scatter.2.cloned.1.call-done = f32[128,128]{0,1:T(8,128)} async-done(((f32[512,128]{0,1:T(8,128)}), f32[128,128]{0,1:T(8,128)}) %reduce-scatter.2.cloned.1.call-update) | async-done | bytes 65552 | tf_op jit(solution)/shard_map/reduce_scatter | solution.py:71
  441.3 16.4 %convolution_bitcast_fusion = f32[512,16,1,256]{3,1,0,2:T(8,128)} fusion(bf16[512,16,128]{2,1,0:T(8,128)(2,1)S(1)} %bitcast.31, bf16[512,128,256]{2,1,0:T(8,128)(2,1)} %copy.14), kind=kOutput, calls=%fused_computation.12 | convolution fusion | flops 536870912 | bytes 44040192 | tf_op jit(solution)/shard_map/gim,gcni->gcnm/dot_general | solution.py:59
  457.7 335.6 %all-reduce.5.cloned.1.call-done = f32[128,128]{0,1:T(8,128)} async-done(((f32[128,128]{0,1:T(8,128)}), f32[128,128]{0,1:T(8,128)}) %all-reduce.5.cloned.1.call-update) | async-done | bytes 65552 | tf_op jit(solution)/shard_map/psum | solution.py:70
  793.4 0.8 broadcast_multiply_fusion
  794.2 0.7 copy.13
  794.9 10.8 %fusion.4 = bf16[512,16,1,128]{3,1,0,2:T(8,128)(2,1)} fusion(f32[512,16,1,256]{3,1,0,2:T(8,128)} %convolution_bitcast_fusion, bf16[512,16,128]{2,1,0:T(8,128)(2,1)} %bitcast.9, bf16[512,128,256]{2,1,0:T(8,128)(2,1)} %copy.14), kind=kOutput, calls=%fused_computation.10 | convolution fusion | flops 270532608 | bytes 25165824 | tf_op jit(solution)/shard_map/gim,gci->gcm/dot_general | solution.py:60
  (9 shorter events, 0.1 us)
Async XLA Ops:
  7.2 434.1 %reduce-scatter.2.cloned.1.call-start = ((), (), s32[]{:S(2)}) async-start(), calls=%async_computation.1 | async-start | bytes 327680 | tf_op jit(solution)/shard_map/reduce_scatter | solution.py:71
  7.2 123.2 %collective-permute-start = (bf16[8192,128]{1,0:T(8,128)(2,1)}, bf16[8192,128]{1,0:T(8,128)(2,1)}, u32[]{:S(2)}, u32[]{:S(2)}) collective-permute-start(bf16[8192,128]{1,0:T(8,128)(2,1)} %bitcast.33), channel_id=1, source_target_pairs={{0,4},{4,8},{8,12},{12,16},{16,20},{20,24},{24,28},{28,32},{32,36}... | collective-permute-start | bytes 6291464 | tf_op jit(solution)/shard_map/ppermute | solution.py:15
  84.7 45.7 %copy-start = (bf16[1,8192,128]{2,1,0:T(8,128)(2,1)S(1)}, bf16[1,8192,128]{2,1,0:T(8,128)(2,1)}, u32[]{:S(2)}) copy-start(bf16[1,8192,128]{2,1,0:T(8,128)(2,1)} %param.5) | copy-start | bytes 6291460
  380.9 412.5 %all-reduce.5.cloned.1.call-start = ((), (), s32[]{:S(2)}) async-start(), calls=%async_computation.2 | async-start | bytes 131072 | tf_op jit(solution)/shard_map/psum | solution.py:70
  380.9 414.0 %collective-permute-start.1 = (bf16[8192,128]{1,0:T(8,128)(2,1)S(1)}, bf16[8192,128]{1,0:T(8,128)(2,1)}, u32[]{:S(2)}, u32[]{:S(2)}) collective-permute-start(bf16[8192,128]{1,0:T(8,128)(2,1)S(1)} %bitcast.30), channel_id=1, source_target_pairs={{4,0},{8,4},{12,8},{16,12},{20,16},{24,20},{28,24},{32,28},{36,32}... | collective-permute-start | bytes 6291464 | tf_op jit(solution)/shard_map/ppermute | solution.py:15
Sparse Core Ops, SparseCore 0:
  381.0 60.2 reduce-scatter.1
  443.9 349.3 all-reduce.4
where the time goes:
time: 816 us; the launch traced here: 813 us
  waiting for transfers between devices  395 us (48%)
  local copies, waits for them, and re-layouts  302 us (37%)
  matrix products  70.1 us (9%)
  other arithmetic  19.3 us (2%)
  between operations  14.1 us (2%)
    psum x1, waiting for transfers between devices, per_device(): summed = lax.psum(partial_taps, 'ctx')  336 us
    reshape x1, local copies, waits for them, and re-layouts, fold_taps(): flat[:, 1:1 + length * (2 * length + 1)]  76 us
    reshape x1, local copies, waits for them, and re-layouts, fold_taps(): flat = outer.reshape(groups, length * 2 * length)  69.3 us
    reduce_scatter x1, waiting for transfers between devices, per_device(): tap_sums = lax.psum_scatter(summed, 'fsdp', scatter_dimension=0, tiled=True)  58.9 us
    reshape x1, local copies, waits for them, and re-layouts, build_band(): return flat.reshape(groups, length, 2 * length)  45.7 us
    slice x1, local copies, waits for them, and re-layouts, fold_taps(): flat[:, 1:1 + length * (2 * length + 1)]  43.3 us
    another operation x2, local copies, waits for them, and re-layouts, build_band(): flat = jnp.tile(row, (1, length))  42.2 us
    dot_general x1, matrix products, per_device(): jnp.einsum('gcni,gcnm->gim', core_blocks, windows, preferred_element_type...  25.8 us
  transfers between devices with their start and end apart: 4, of which 2 were waited for; matrix products, arithmetic and copies ran while one was open for 16% of the time, Pallas kernels for 0%

commit v1 on v0

v1 whole, which is shorter than its diff:
```python
import math

import jax
import jax.numpy as jnp
import ml_dtypes
import numpy as np
from jax import lax
from jax.experimental import pallas as pl
from jax.experimental.pallas import tpu as pltpu
from jax.sharding import PartitionSpec as P

FLEN = 128
GROUP_CH = 16
WIN = 2 * FLEN
BLOCK = 512
F32, BF16 = jnp.float32, jnp.bfloat16


def split(a):
    hi = a.astype(ml_dtypes.bfloat16)
    lo = (a - hi.astype(np.float64)).astype(ml_dtypes.bfloat16)
    return hi, lo


def tables():
    n = np.arange(WIN)[:, None]
    k = np.arange(FLEN)[None, :]
    angle = np.pi * (((2 * k + 1) * n) % (2 * WIN)) / WIN
    fwd = np.concatenate([np.cos(angle), -np.sin(angle)], axis=1)
    inv = fwd.T / FLEN
    fwd_hi, fwd_lo = split(fwd)
    inv_hi, inv_lo = split(inv)
    fwd2 = np.concatenate([fwd_hi, fwd_lo], axis=0)
    left = np.concatenate([fwd_hi[:FLEN], fwd_lo[:FLEN]], axis=0)
    right = np.concatenate([fwd_hi[FLEN:], fwd_lo[FLEN:]], axis=0)
    inv3 = np.concatenate([inv_hi, inv_hi, inv_lo], axis=0)
    return fwd2, left, right, inv3[:, :FLEN], inv3[:, FLEN:]


def dot(a, b):
    return jnp.dot(a, b, preferred_element_type=F32)


def spectrum(first, second, table):
    return dot(jnp.concatenate([first, second, first, second], axis=1), table)


def half_spectrum(block, table):
    return dot(jnp.concatenate([block, block], axis=1), table)


def invert(re, im, table):
    y = jnp.concatenate([re, im], axis=1)
    hi = y.astype(BF16)
    lo = (y - hi.astype(F32)).astype(BF16)
    return dot(jnp.concatenate([hi, lo, hi], axis=1), table)


def per_channel(h):
    groups = h.shape[0]
    return jnp.broadcast_to(h[:, None, :], (groups, GROUP_CH, FLEN)).reshape(groups * GROUP_CH, FLEN)


def group_sum(x):
    return jnp.sum(x.reshape(x.shape[0] // GROUP_CH, GROUP_CH, FLEN), axis=1)


def convolve(x, h, table):
    hr, hi = per_channel(h[:, :FLEN]), per_channel(h[:, FLEN:])
    xr, xi = x[:, :FLEN], x[:, FLEN:]
    return invert(xr * hr - xi * hi, xr * hi + xi * hr, table)


def correlate(v, h, table):
    hr, hi = per_channel(h[:, :FLEN]), per_channel(h[:, FLEN:])
    vr, vi = v[:, :FLEN], v[:, FLEN:]
    return invert(vr * hr + vi * hi, vi * hr - vr * hi, table)


def cross(a, b):
    ar, ai, br, bi = a[:, :FLEN], a[:, FLEN:], b[:, :FLEN], b[:, FLEN:]
    return jnp.concatenate([group_sum(ar * br + ai * bi), group_sum(ai * br - ar * bi)], axis=1)


def keep(flag, block):
    return jnp.where(flag > 0, block, jnp.zeros_like(block))


def forward(flags, prev, cur, gate, h, fwd2, inv_b, gq):
    x = spectrum(keep(flags[0], prev[...]), cur[...], fwd2[...])
    conv = convolve(x, h[...], inv_b[...])
    gq[...] = (gate[...].astype(F32) * conv).astype(BF16)
    return x


def backward(flags, nxt, core, h, fwd2, inv_a, gg):
    v = spectrum(core[...], keep(flags[1], nxt[...]), fwd2[...])
    gg[...] = correlate(v, h[...], inv_a[...]).astype(BF16)
    return v


def first_kernel(flags, prev, cur_a, gate, core_a, h_a, nxt, core_b, cur_b, h_b, fwd2, left, right, inv_a, inv_b,
                 *rest):
    gq, gg, sums_a, sums_b = rest[-4:]
    x = forward(flags, prev, cur_a, gate, h_a, fwd2, inv_b, gq)
    sums_a[...] = cross(half_spectrum(core_a[...], right[...]), x)
    v = backward(flags, nxt, core_b, h_b, fwd2, inv_a, gg)
    sums_b[...] = cross(v, half_spectrum(cur_b[...], left[...]))


def second_kernel(flags, prev, cur_b, gate, h_b, nxt, core_a, h_a, fwd2, inv_a, inv_b, *rest):
    gq, gg = rest[-2:]
    forward(flags, prev, cur_b, gate, h_b, fwd2, inv_b, gq)
    backward(flags, nxt, core_a, h_a, fwd2, inv_a, gg)


def rows_at(start, width, block):
    return pl.BlockSpec((block, width), lambda i, *_: (start // block + i, 0))


def whole(a):
    return pl.BlockSpec(a.shape, lambda i, *_: (0, 0))


ANY = pl.BlockSpec(memory_space=pl.ANY)


def run(kernel, flags, blocks, consts, carried, outs, count, extra, name):
    width = blocks[0][0].shape[1]
    args = [a for a, _ in blocks] + list(consts)
    specs = [s for _, s in blocks] + [whole(c) for c in consts]
    aliases = {}
    if carried is not None:
        aliases = {1 + len(args): 0, 2 + len(args): 1}
        args += list(carried)
        specs += [ANY, ANY]
    full = jax.ShapeDtypeStruct(outs[0], BF16)
    return pl.pallas_call(
        kernel,
        out_shape=[full, full] + [s for s, _ in extra],
        grid_spec=pltpu.PrefetchScalarGridSpec(
            num_scalar_prefetch=1,
            grid=(count,),
            in_specs=specs,
            out_specs=list(outs[1:]) + [s for _, s in extra],
        ),
        input_output_aliases=aliases,
        compiler_params=pltpu.CompilerParams(vmem_limit_bytes=40 * 1024 * 1024),
        name=name,
    )(flags, *args)


def exchange(x, partner):
    n_ctx, n_fsdp = lax.axis_size("ctx"), lax.axis_size("fsdp")
    pairs = []
    for c in range(n_ctx):
        for f in range(n_fsdp):
            pc, pf = partner(c, f)
            pairs.append((c * n_fsdp + f, pc * n_fsdp + pf))
    return lax.ppermute(x, ("ctx", "fsdp"), pairs)


def reduce_taps(partial):
    f = lax.axis_index("fsdp")
    core, low = f % 2, f // 2
    x = partial.reshape(2, 2, -1, FLEN)
    pick = lambda a, i, axis: lax.dynamic_index_in_dim(a, i, axis, keepdims=False)
    x = pick(x, core, 1) + exchange(pick(x, 1 - core, 1), lambda c, f: (c, f ^ 1))
    x = pick(x, low, 0) + exchange(pick(x, 1 - low, 0), lambda c, f: (c, f ^ 2))
    for partner in (
        lambda c, f: (c ^ 1, f),
        lambda c, f: (c - c % 4 + 3 - c % 4, f),
        lambda c, f: (c ^ 4, f),
        lambda c, f: (c ^ 8, f),
        lambda c, f: ((3 - c // 8) * 8 + c % 8, f),
    ):
        x = x + exchange(x, partner)
    return x


def per_device(query, gated, grad_out, filters):
    query, gated, grad_out = query[0], gated[0], grad_out[0]
    width = gated.shape[0]
    half, quarter = width // 2, width // 4
    n_ctx = lax.axis_size("ctx")
    me = lax.axis_index("ctx")
    flags = jnp.stack([(me > 0), (me < n_ctx - 1)]).astype(jnp.int32)
    fwd2, left, right, inv_a, inv_b = (jnp.asarray(t) for t in tables())
    up = [(i, (i + 1) % n_ctx) for i in range(n_ctx)]
    down = [(b, a) for a, b in up]

    starts = [0, quarter, half, half + quarter]
    part = lambda a, i: lax.slice_in_dim(a, starts[i], starts[i] + quarter, axis=0)
    core = [(part(grad_out, i).astype(F32) * part(query, i).astype(F32)).astype(BF16) for i in range(4)]
    prev = [lax.ppermute(part(gated, i), "ctx", up) for i in (0, 1, 2, 3)]
    nxt = [None] * 4
    for i in (2, 3, 0, 1):
        nxt[i] = lax.ppermute(core[i], "ctx", down)

    taps = lax.all_gather(filters.astype(BF16), "fsdp", axis=0, tiled=True)
    h = dot(jnp.concatenate([taps, taps], axis=1), left)

    steps = quarter // BLOCK
    gb = BLOCK // GROUP_CH
    at = lambda i: rows_at(starts[i], FLEN, BLOCK)
    zero = rows_at(0, FLEN, BLOCK)
    h_at = lambda i: rows_at(starts[i] // GROUP_CH, WIN, gb)
    sums = (jax.ShapeDtypeStruct((quarter // GROUP_CH, WIN), F32), rows_at(0, WIN, gb))

    carried = None
    tap_spec = [None] * 4
    for i, j in ((0, 2), (1, 3)):
        gq, gg, tap_spec[i], tap_spec[j] = run(
            first_kernel,
            flags,
            [(prev[i], zero), (gated, at(i)), (grad_out, at(i)), (core[i], zero), (h, h_at(i)),
             (nxt[j], zero), (core[j], zero), (gated, at(j)), (h, h_at(j))],
            (fwd2, left, right, inv_a, inv_b),
            carried,
            (gated.shape, at(i), at(j)),
            steps,
            [sums, sums],
            "conv_and_taps",
        )
        carried = (gq, gg)
    spec = jnp.concatenate(tap_spec, axis=0)
    partial = invert(spec[:, :FLEN], spec[:, FLEN:], inv_a)
    summed = reduce_taps(partial)
    count = lax.axis_size("fsdp") * n_ctx * FLEN * GROUP_CH
    grad_filters = summed * (1.0 / math.sqrt(count))
    for i, j in ((2, 0), (3, 1)):
        carried = run(
            second_kernel,
            flags,
            [(prev[i], zero), (gated, at(i)), (grad_out, at(i)), (h, h_at(i)),
             (nxt[j], zero), (core[j], zero), (h, h_at(j))],
            (fwd2, inv_a, inv_b),
            carried,
            (gated.shape, at(i), at(j)),
            steps,
            [],
            "conv_only",
        )
    gq, gg = carried
    return (gq[None], gg[None], grad_filters)


def solution(mesh):
    return jax.shard_map(
        per_device,
        mesh=mesh,
        in_specs=(
            P("fsdp", None, "ctx"),
            P("fsdp", None, "ctx"),
            P("fsdp", None, "ctx"),
            P("fsdp", None),
        ),
        out_specs=(P("fsdp", None, "ctx"), P("fsdp", None, "ctx"), P("fsdp", None)),
        check_vma=False,
    )
```

time: 816 us -> 139 us (0.17)
  waiting for transfers between devices: 395 us -> 38.8 us
  local copies, waits for them, and re-layouts: 302 us -> 13.6 us
  matrix products: 70.1 us -> 3.02 us
  Pallas kernels: 0 us -> 28.9 us
  starting transfers between devices: 6.78 us -> 31.6 us
  between operations: 14.1 us -> 0.91 us
  other arithmetic: 19.3 us -> 6.45 us
  blocking collectives: 5.41 us -> 14.9 us
    psum x1 -> x0, waiting for transfers between devices: 336 us -> none  [per_device(): summed = lax.psum(partial_taps, 'ctx')]
    reshape x3 -> x0, local copies, waits for them, and re-layouts: 191 us -> none  [the longest x1 76 us: fold_taps(): flat[:, 1:1 + length * (2 * length + 1)]]
    dot_general x4 -> x5, matrix products: 70.1 us -> 3.02 us  [dot(): return jnp.dot(a, b, preferred_element_type=F32)]
    slice x2 -> x1, local copies, waits for them, and re-layouts: 66.6 us -> 1.36 us  [per_device(): lax.slice_in_dim(a, starts[i], starts[i] + quarter, axis=0)]
    reduce_scatter x1 -> x0, waiting for transfers between devices: 58.9 us -> none  [per_device(): tap_sums = lax.psum_scatter(summed, 'fsdp', scatter_dimension=0, tiled=True)]
    another operation x2 -> x0, local copies, waits for them, and re-layouts: 42.2 us -> none  [build_band(): flat = jnp.tile(row, (1, length))]
    ppermute x2 -> x15, waiting for transfers between devices: 0.01 us -> 38.8 us  [the longest x7 38.8 us: exchange(): return lax.ppermute(x, ('ctx', 'fsdp'), pairs)]
    pallas_call x0 -> x4, Pallas kernels: none -> 28.9 us  [run(): pl.pallas_call(kernel, out_shape=[full, full] + [s for s, _ in extra], gr...]
  transfers between devices with their start and end apart: 4 -> 15, of which waited for: 2 -> 5; matrix products, arithmetic and copies ran while one was open for 16% -> 3% of each run, Pallas kernels for 0% -> 16%
where the time goes in v1:
time: 139 us; the launch traced here: 138 us
  waiting for transfers between devices  38.8 us (28%)
  starting transfers between devices  31.6 us (23%)
  Pallas kernels  28.9 us (21%)
  blocking collectives  14.9 us (11%)
  local copies, waits for them, and re-layouts  13.6 us (10%)
  other arithmetic  6.45 us (5%)
  matrix products  3.02 us (2%)
    ppermute x7, waiting for transfers between devices, exchange(): return lax.ppermute(x, ('ctx', 'fsdp'), pairs)  38.8 us
    pallas_call x4, Pallas kernels, run(): pl.pallas_call(kernel, out_shape=[full, full] + [s for s, _ in extra], gr...  28.9 us
    ppermute x4, starting transfers between devices, per_device(): nxt[i] = lax.ppermute(core[i], 'ctx', down)  25.9 us
    all_gather x1, blocking collectives, per_device(): taps = lax.all_gather(filters.astype(BF16), 'fsdp', axis=0, tiled=True)  14.9 us
    unnamed x47, local copies, waits for them, and re-layouts  11.6 us
    convert_element_type x1, other arithmetic, per_device(): (part(grad_out, i).astype(F32) * part(query, i).astype(F32)).astype(BF16)  3.86 us
    ppermute x7, starting transfers between devices, exchange(): return lax.ppermute(x, ('ctx', 'fsdp'), pairs)  3.67 us
    dot_general x5, matrix products, dot(): return jnp.dot(a, b, preferred_element_type=F32)  3.02 us
  transfers between devices with their start and end apart: 15, of which 5 were waited for; matrix products, arithmetic and copies ran while one was open for 3% of the time, Pallas kernels for 16%

profile of v1, /device:TPU:0, one launch (start us, length us, event | category | flops | bytes accessed | tf_op | source)
XLA Modules:
  0.0 138.3 jit_solution(14587400880296902249)
XLA Ops:
  0.6 3.9 %fusion.4 = (bf16[2048,128]{1,0:T(8,128)(2,1)}, bf16[2048,128]{1,0:T(8,128)(2,1)}, bf16[2048,128]{1,0:T(8,128)(2,1)S(1)}, bf16[2048,128]{1,0:T(8,128)(2,1)}) fusion(bf16[1,8192,128]{2,1,0:T(8,128)(2,1)} %param.9, bf16[1,8192,128]{2,1,0:T(8,128)(2,1)} %param.11), kind=kLoop, calls=%fused_computation.11 | loop fusion | flops 4194304 | bytes 6291456 | tf_op jit(solution)/shard_map/convert_element_type | solution.py:194
  4.5 9.0 %collective-permute-start.7 = (bf16[2048,128]{1,0:T(8,128)(2,1)}, bf16[2048,128]{1,0:T(8,128)(2,1)}, u32[]{:S(2)}, u32[]{:S(2)}) collective-permute-start(bf16[2048,128]{1,0:T(8,128)(2,1)} %get-tuple-element.27.core_b), channel_id=1, source_target_pairs={{4,0},{8,4},{12,8},{16,12},{20,16},{24,20},{28,24},{32,28},{36,32}... | collective-permute-start | bytes 1572872 | tf_op jit(solution)/shard_map/ppermute | solution.py:198
  13.5 1.4 slice_bitcast_fusion
  14.8 7.7 %collective-permute-start.5 = (bf16[2048,128]{1,0:T(8,128)(2,1)}, bf16[2048,128]{1,0:T(8,128)(2,1)}, u32[]{:S(2)}, u32[]{:S(2)}) collective-permute-start(bf16[2048,128]{1,0:T(8,128)(2,1)} %get-tuple-element.30.core_b), channel_id=1, source_target_pairs={{4,0},{8,4},{12,8},{16,12},{20,16},{24,20},{28,24},{32,28},{36,32}... | collective-permute-start | bytes 1572872 | tf_op jit(solution)/shard_map/ppermute | solution.py:198
  22.6 14.9 %all_gather.3 = bf16[512,128]{1,0:T(8,128)(2,1)S(1)} all-gather(bf16[128,128]{1,0:T(8,128)(2,1)S(1)} %convert_element_type.68), channel_id=1, replica_groups=mesh['ctx'=32,'fsdp'=4] {'fsdp'}, dimensions={0}, use_global_device_ids=true | all-gather | bytes 163840 | tf_op jit(solution)/shard_map/all_gather | solution.py:200
  38.1 1.0 fusion.9
  39.2 1.3 fusion.h_a.h_b
  40.6 1.6 %copy-done.1 = bf16[1,8192,128]{2,1,0:T(8,128)(2,1)S(1)} copy-done((bf16[1,8192,128]{2,1,0:T(8,128)(2,1)S(1)}, bf16[1,8192,128]{2,1,0:T(8,128)(2,1)}, u32[]{:S(2)}) %copy-start.1) | copy-done | bytes 2097176
  42.2 1.0 copy-done.3
  46.0 7.3 %conv_and_taps.2 = (bf16[8192,128]{1,0:T(8,128)(2,1)}, bf16[8192,128]{1,0:T(8,128)(2,1)}, f32[128,256]{1,0:T(8,128)S(1)}, f32[128,256]{1,0:T(8,128)S(1)}) custom-call(s32[2]{0:T(128)S(1)} %add_convert_fusion.flags, bf16[2048,128]{1,0:T(8,128)(2,1)} %collective-permute-done.6.prev, bf16[8192,128]{1,0:T(8,128)(2,1)S(1)} %bitcast.40, ...), custom_call_target="tpu_custom_call" | custom-call | tf_op jit(solution)/shard_map/conv_and_taps/pallas_call | solution.py:138
  53.4 7.3 %conv_and_taps.3 = (bf16[8192,128]{1,0:T(8,128)(2,1)}, bf16[8192,128]{1,0:T(8,128)(2,1)}, f32[128,256]{1,0:T(8,128)S(1)}, f32[128,256]{1,0:T(8,128)S(1)}) custom-call(s32[2]{0:T(128)S(1)} %add_convert_fusion.flags, bf16[2048,128]{1,0:T(8,128)(2,1)} %collective-permute-done.4.prev, ...), custom_call_target="tpu_custom_call", output_to_operand_aliasing={{0}: (15, {}), {1}: (16, {})} | custom-call | tf_op jit(solution)/shard_map/conv_and_taps/pallas_call | solution.py:138
  62.9 1.1 collective-permute-done.8
  65.6 1.4 collective-permute-start.9
  67.0 9.2 %collective-permute-start.3 = (bf16[2048,128]{1,0:T(8,128)(2,1)}, bf16[2048,128]{1,0:T(8,128)(2,1)}, u32[]{:S(2)}, u32[]{:S(2)}) collective-permute-start(bf16[2048,128]{1,0:T(8,128)(2,1)} %get-tuple-element.28.core_a), channel_id=1, source_target_pairs={{4,0},{8,4},{12,8},{16,12},{20,16},{24,20},{28,24},{32,28},{36,32}... | collective-permute-start | bytes 1572872 | tf_op jit(solution)/shard_map/ppermute | solution.py:198
  76.2 2.0 %collective-permute-start.2 = (bf16[2048,128]{1,0:T(8,128)(2,1)}, bf16[2048,128]{1,0:T(8,128)(2,1)}, u32[]{:S(2)}, u32[]{:S(2)}) collective-permute-start(bf16[2048,128]{1,0:T(8,128)(2,1)} %get-tuple-element.32), channel_id=1, source_target_pairs={{0,4},{4,8},{8,12},{12,16},{16,20},{20,24},{24,28},{28,32},{32,36}... | collective-permute-start | bytes 1572872 | tf_op jit(solution)/shard_map/ppermute | solution.py:195
  79.2 22.7 %collective-permute-done.10 = f32[128,128]{1,0:T(8,128)S(1)} collective-permute-done((f32[128,128]{1,0:T(8,128)S(1)}, f32[128,128]{1,0:T(8,128)S(1)}, u32[]{:S(2)}, u32[]{:S(2)}) %collective-permute-start.10) | collective-permute-done | bytes 65568 | tf_op jit(solution)/shard_map/ppermute | solution.py:160
  102.0 6.4 %collective-permute-done.11 = f32[128,128]{1,0:T(8,128)S(1)} collective-permute-done((f32[128,128]{1,0:T(8,128)S(1)}, f32[128,128]{1,0:T(8,128)S(1)}, u32[]{:S(2)}, u32[]{:S(2)}) %collective-permute-start.11) | collective-permute-done | bytes 65568 | tf_op jit(solution)/shard_map/ppermute | solution.py:160
  108.5 5.8 %collective-permute-done.12 = f32[128,128]{1,0:T(8,128)S(1)} collective-permute-done((f32[128,128]{1,0:T(8,128)S(1)}, f32[128,128]{1,0:T(8,128)S(1)}, u32[]{:S(2)}, u32[]{:S(2)}) %collective-permute-start.12) | collective-permute-done | bytes 65568 | tf_op jit(solution)/shard_map/ppermute | solution.py:160
  114.3 1.6 %collective-permute-start.13 = (f32[128,128]{1,0:T(8,128)S(1)}, f32[128,128]{1,0:T(8,128)S(1)}, u32[]{:S(2)}, u32[]{:S(2)}) collective-permute-start(f32[128,128]{1,0:T(8,128)S(1)} %add.51), channel_id=1, source_target_pairs={{0,32},{1,33},{2,34},{3,35},{4,36},{5,37},{6,38},{7,39},{8,40},{9,... | collective-permute-start | bytes 196616 | tf_op jit(solution)/shard_map/ppermute | solution.py:160
  115.8 2.8 %collective-permute-done.13 = f32[128,128]{1,0:T(8,128)S(1)} collective-permute-done((f32[128,128]{1,0:T(8,128)S(1)}, f32[128,128]{1,0:T(8,128)S(1)}, u32[]{:S(2)}, u32[]{:S(2)}) %collective-permute-start.13) | collective-permute-done | bytes 65568 | tf_op jit(solution)/shard_map/ppermute | solution.py:160
  118.8 1.6 %copy-done.2 = bf16[1,8192,128]{2,1,0:T(8,128)(2,1)S(1)} copy-done((bf16[1,8192,128]{2,1,0:T(8,128)(2,1)S(1)}, bf16[1,8192,128]{2,1,0:T(8,128)(2,1)}, u32[]{:S(2)}) %copy-start.2) | copy-done | bytes 2097176
  120.3 1.0 copy-done.4
  123.2 7.2 %conv_only.2 = (bf16[8192,128]{1,0:T(8,128)(2,1)}, bf16[8192,128]{1,0:T(8,128)(2,1)}) custom-call(s32[2]{0:T(128)S(1)} %add_convert_fusion.flags, bf16[2048,128]{1,0:T(8,128)(2,1)} %collective-permute-done.2.prev, bf16[8192,128]{1,0:T(8,128)(2,1)S(1)} %bitcast.44, bf16[8192,128]{1,0:T(8,128)(2,1)S(1)} %bitcast.48, ...), custom_call_target="tpu_custom_call", output_to_operand_aliasing={{0}: (11, {}), {1}: (12, {})} | custom-call | tf_op jit(solution)/shard_map/conv_only/pallas_call | solution.py:138
  130.4 7.2 %conv_only.3 = (bf16[8192,128]{1,0:T(8,128)(2,1)}, bf16[8192,128]{1,0:T(8,128)(2,1)}) custom-call(s32[2]{0:T(128)S(1)} %add_convert_fusion.flags, bf16[2048,128]{1,0:T(8,128)(2,1)} %collective-permute-done.prev, bf16[8192,128]{1,0:T(8,128)(2,1)S(1)} %bitcast.45, bf16[8192,128]{1,0:T(8,128)(2,1)S(1)} %bitcast.49, ...), custom_call_target="tpu_custom_call", output_to_operand_aliasing={{0}: (11, {}), {1}: (12, {})} | custom-call | tf_op jit(solution)/shard_map/conv_only/pallas_call | solution.py:138
  (77 shorter events, 11.1 us)
Async XLA Ops:
  0.6 12.8 %copy-start = (bf16[1,8192,128]{2,1,0:T(8,128)(2,1)S(1)}, bf16[1,8192,128]{2,1,0:T(8,128)(2,1)}, u32[]{:S(2)}) copy-start(bf16[1,8192,128]{2,1,0:T(8,128)(2,1)} %param.10) | copy-start | bytes 6291460
  4.5 18.1 %copy-start.20 = (f32[128,128]{1,0:T(8,128)S(1)}, f32[128,128]{1,0:T(8,128)}, u32[]{:S(2)}) copy-start(f32[128,128]{1,0:T(8,128)} %param.12) | copy-start | bytes 196612
  4.5 33.6 %copy-start.21 = (bf16[128,256]{1,0:T(8,128)(2,1)S(1)}, bf16[128,256]{1,0:T(8,128)(2,1)}, u32[]{:S(2)}) copy-start(bf16[128,256]{1,0:T(8,128)(2,1)} %constant.72) | copy-start | bytes 196612
  4.5 36.1 %collective-permute-start.7 = (bf16[2048,128]{1,0:T(8,128)(2,1)}, bf16[2048,128]{1,0:T(8,128)(2,1)}, u32[]{:S(2)}, u32[]{:S(2)}) collective-permute-start(bf16[2048,128]{1,0:T(8,128)(2,1)} %get-tuple-element.27.core_b), channel_id=1, source_target_pairs={{4,0},{8,4},{12,8},{16,12},{20,16},{24,20},{28,24},{32,28},{36,32}... | collective-permute-start | bytes 1572872 | tf_op jit(solution)/shard_map/ppermute | solution.py:198
  14.8 25.8 %copy-start.5 = (bf16[512,256]{1,0:T(8,128)(2,1)S(1)}, bf16[512,256]{1,0:T(8,128)(2,1)}, u32[]{:S(2)}) copy-start(bf16[512,256]{1,0:T(8,128)(2,1)} %constant.64.clone.fwd2) | copy-start | bytes 786436
  14.8 25.8 %copy-start.13 = (bf16[256,256]{1,0:T(8,128)(2,1)S(1)}, bf16[256,256]{1,0:T(8,128)(2,1)}, u32[]{:S(2)}) copy-start(bf16[256,256]{1,0:T(8,128)(2,1)} %constant.65.clone.left) | copy-start | bytes 393220
  14.8 25.8 %collective-permute-start.6 = (bf16[2048,128]{1,0:T(8,128)(2,1)}, bf16[2048,128]{1,0:T(8,128)(2,1)}, u32[]{:S(2)}, u32[]{:S(2)}) collective-permute-start(bf16[2048,128]{1,0:T(8,128)(2,1)} %get-tuple-element.31), channel_id=1, source_target_pairs={{0,4},{4,8},{8,12},{12,16},{16,20},{20,24},{24,28},{28,32},{32,36}... | collective-permute-start | bytes 1572872 | tf_op jit(solution)/shard_map/ppermute | solution.py:195
  14.8 38.5 %collective-permute-start.5 = (bf16[2048,128]{1,0:T(8,128)(2,1)}, bf16[2048,128]{1,0:T(8,128)(2,1)}, u32[]{:S(2)}, u32[]{:S(2)}) collective-permute-start(bf16[2048,128]{1,0:T(8,128)(2,1)} %get-tuple-element.30.core_b), channel_id=1, source_target_pairs={{4,0},{8,4},{12,8},{16,12},{20,16},{24,20},{28,24},{32,28},{36,32}... | collective-permute-start | bytes 1572872 | tf_op jit(solution)/shard_map/ppermute | solution.py:198
  22.6 30.7 %collective-permute-start.4 = (bf16[2048,128]{1,0:T(8,128)(2,1)}, bf16[2048,128]{1,0:T(8,128)(2,1)}, u32[]{:S(2)}, u32[]{:S(2)}) collective-permute-start(bf16[2048,128]{1,0:T(8,128)(2,1)} %get-tuple-element.34), channel_id=1, source_target_pairs={{0,4},{4,8},{8,12},{12,16},{16,20},{20,24},{24,28},{28,32},{32,36}... | collective-permute-start | bytes 1572872 | tf_op jit(solution)/shard_map/ppermute | solution.py:195
  46.0 7.3 %copy-start.7 = (bf16[768,128]{1,0:T(8,128)(2,1)S(1)}, bf16[768,128]{1,0:T(8,128)(2,1)}, u32[]{:S(2)}) copy-start(bf16[768,128]{1,0:T(8,128)(2,1)} %constant.67.clone.inv_a) | copy-start | bytes 589828
  46.0 7.3 %copy-start.11 = (bf16[768,128]{1,0:T(8,128)(2,1)S(1)}, bf16[768,128]{1,0:T(8,128)(2,1)}, u32[]{:S(2)}) copy-start(bf16[768,128]{1,0:T(8,128)(2,1)} %constant.68.clone.inv_b) | copy-start | bytes 589828
  46.0 7.3 %copy-start.15 = (bf16[256,256]{1,0:T(8,128)(2,1)S(1)}, bf16[256,256]{1,0:T(8,128)(2,1)}, u32[]{:S(2)}) copy-start(bf16[256,256]{1,0:T(8,128)(2,1)} %constant.66.clone.right) | copy-start | bytes 393220
  53.4 7.4 %copy-start.18 = (bf16[256,128]{1,0:T(8,128)(2,1)S(1)}, bf16[256,128]{1,0:T(8,128)(2,1)}, u32[]{:S(2)}) copy-start(bf16[256,128]{1,0:T(8,128)(2,1)} %constant.74) | copy-start | bytes 196612
  62.4 1.6 %collective-permute-start.8 = (f32[2,128,128]{2,1,0:T(8,128)S(1)}, f32[2,128,128]{2,1,0:T(8,128)}, u32[]{:S(2)}, u32[]{:S(2)}) collective-permute-start(f32[2,128,128]{2,1,0:T(8,128)S(1)} %dynamic-slice_bitcast_fusion), channel_id=1, source_target_pairs={{0,1},{1,0},{2,3},{3,2},{4,5},{5,4},{6,7},{7,6},{8,9},{9,8},{10,11... | collective-permute-start | bytes 393224 | tf_op jit(solution)/shard_map/ppermute | solution.py:160
  65.6 12.6 %collective-permute-start.9 = (f32[128,128]{1,0:T(8,128)}, f32[128,128]{1,0:T(8,128)}, u32[]{:S(2)}, u32[]{:S(2)}) collective-permute-start(f32[128,128]{1,0:T(8,128)} %dynamic-slice_bitcast_fusion.1), channel_id=1, source_target_pairs={{0,2},{1,3},{2,0},{3,1},{4,6},{5,7},{6,4},{7,5},{8,10},{9,11},{10,... | collective-permute-start | bytes 196616 | tf_op jit(solution)/shard_map/ppermute | solution.py:160
  67.0 51.7 %collective-permute-start.3 = (bf16[2048,128]{1,0:T(8,128)(2,1)}, bf16[2048,128]{1,0:T(8,128)(2,1)}, u32[]{:S(2)}, u32[]{:S(2)}) collective-permute-start(bf16[2048,128]{1,0:T(8,128)(2,1)} %get-tuple-element.28.core_a), channel_id=1, source_target_pairs={{4,0},{8,4},{12,8},{16,12},{20,16},{24,20},{28,24},{32,28},{36,32}... | collective-permute-start | bytes 1572872 | tf_op jit(solution)/shard_map/ppermute | solution.py:198
  76.2 54.2 %collective-permute-start.1 = (bf16[2048,128]{1,0:T(8,128)(2,1)S(1)}, bf16[2048,128]{1,0:T(8,128)(2,1)}, u32[]{:S(2)}, u32[]{:S(2)}) collective-permute-start(bf16[2048,128]{1,0:T(8,128)(2,1)S(1)} %get-tuple-element.29.core_a), channel_id=1, source_target_pairs={{4,0},{8,4},{12,8},{16,12},{20,16},{24,20},{28,24},{32,28},{36,32}... | collective-permute-start | bytes 1572872 | tf_op jit(solution)/shard_map/ppermute | solution.py:198
  76.2 42.5 %collective-permute-start.2 = (bf16[2048,128]{1,0:T(8,128)(2,1)}, bf16[2048,128]{1,0:T(8,128)(2,1)}, u32[]{:S(2)}, u32[]{:S(2)}) collective-permute-start(bf16[2048,128]{1,0:T(8,128)(2,1)} %get-tuple-element.32), channel_id=1, source_target_pairs={{0,4},{4,8},{8,12},{12,16},{16,20},{20,24},{24,28},{28,32},{32,36}... | collective-permute-start | bytes 1572872 | tf_op jit(solution)/shard_map/ppermute | solution.py:195
  78.2 52.2 %collective-permute-start = (bf16[2048,128]{1,0:T(8,128)(2,1)}, bf16[2048,128]{1,0:T(8,128)(2,1)}, u32[]{:S(2)}, u32[]{:S(2)}) collective-permute-start(bf16[2048,128]{1,0:T(8,128)(2,1)} %get-tuple-element.33), channel_id=1, source_target_pairs={{0,4},{4,8},{8,12},{12,16},{16,20},{20,24},{24,28},{28,32},{32,36}... | collective-permute-start | bytes 1572872 | tf_op jit(solution)/shard_map/ppermute | solution.py:195
  79.1 22.8 %collective-permute-start.10 = (f32[128,128]{1,0:T(8,128)S(1)}, f32[128,128]{1,0:T(8,128)S(1)}, u32[]{:S(2)}, u32[]{:S(2)}) collective-permute-start(f32[128,128]{1,0:T(8,128)S(1)} %bitcast_add_fusion.1), channel_id=1, source_target_pairs={{0,4},{1,5},{2,6},{3,7},{4,0},{5,1},{6,2},{7,3},{8,12},{9,13},{10,... | collective-permute-start | bytes 196616 | tf_op jit(solution)/shard_map/ppermute | solution.py:160
  101.9 6.5 %collective-permute-start.11 = (f32[128,128]{1,0:T(8,128)S(1)}, f32[128,128]{1,0:T(8,128)S(1)}, u32[]{:S(2)}, u32[]{:S(2)}) collective-permute-start(f32[128,128]{1,0:T(8,128)S(1)} %add.49), channel_id=1, source_target_pairs={{0,12},{1,13},{2,14},{3,15},{4,8},{5,9},{6,10},{7,11},{8,4},{9,5},... | collective-permute-start | bytes 196616 | tf_op jit(solution)/shard_map/ppermute | solution.py:160
  108.4 5.8 %collective-permute-start.12 = (f32[128,128]{1,0:T(8,128)S(1)}, f32[128,128]{1,0:T(8,128)S(1)}, u32[]{:S(2)}, u32[]{:S(2)}) collective-permute-start(f32[128,128]{1,0:T(8,128)S(1)} %add.50), channel_id=1, source_target_pairs={{0,16},{1,17},{2,18},{3,19},{4,20},{5,21},{6,22},{7,23},{8,24},{9,... | collective-permute-start | bytes 196616 | tf_op jit(solution)/shard_map/ppermute | solution.py:160
  114.3 4.3 %collective-permute-start.13 = (f32[128,128]{1,0:T(8,128)S(1)}, f32[128,128]{1,0:T(8,128)S(1)}, u32[]{:S(2)}, u32[]{:S(2)}) collective-permute-start(f32[128,128]{1,0:T(8,128)S(1)} %add.51), channel_id=1, source_target_pairs={{0,32},{1,33},{2,34},{3,35},{4,36},{5,37},{6,38},{7,39},{8,40},{9,... | collective-permute-start | bytes 196616 | tf_op jit(solution)/shard_map/ppermute | solution.py:160
  118.6 19.0 %collective-permute-start.14 = (f32[128,128]{1,0:T(8,128)S(1)}, f32[128,128]{1,0:T(8,128)S(1)}, u32[]{:S(2)}, u32[]{:S(2)}) collective-permute-start(f32[128,128]{1,0:T(8,128)S(1)} %add.52), channel_id=1, source_target_pairs={{0,96},{1,97},{2,98},{3,99},{4,100},{5,101},{6,102},{7,103},{8,104... | collective-permute-start | bytes 196616 | tf_op jit(solution)/shard_map/ppermute | solution.py:160
  (13 other events, 19.3 us)

commit v2 on v1

v2 whole, which is shorter than its diff:
```python
import math

import jax
import jax.numpy as jnp
import ml_dtypes
import numpy as np
from jax import lax
from jax.experimental import pallas as pl
from jax.experimental.pallas import tpu as pltpu
from jax.sharding import PartitionSpec as P

FLEN = 128
GROUP_CH = 16
WIN = 2 * FLEN
BLOCK = 1024
VMEM_MB = 60
F32, BF16 = jnp.float32, jnp.bfloat16


def split(a):
    hi = a.astype(ml_dtypes.bfloat16)
    lo = (a - hi.astype(np.float64)).astype(ml_dtypes.bfloat16)
    return hi, lo


def tables():
    n = np.arange(WIN)[:, None]
    k = np.arange(FLEN)[None, :]
    angle = np.pi * (((2 * k + 1) * n) % (2 * WIN)) / WIN
    fwd = np.concatenate([np.cos(angle), -np.sin(angle)], axis=1)
    inv = fwd.T / FLEN
    fwd_hi, fwd_lo = split(fwd)
    inv_hi, inv_lo = split(inv)
    fwd2 = np.concatenate([fwd_hi, fwd_lo], axis=0)
    left = np.concatenate([fwd_hi[:FLEN], fwd_lo[:FLEN]], axis=0)
    right = np.concatenate([fwd_hi[FLEN:], fwd_lo[FLEN:]], axis=0)
    pair = lambda cols: np.concatenate([inv_hi[:, cols], inv_lo[:, cols]], axis=1)
    return fwd2, left, right, pair(slice(0, FLEN)), pair(slice(FLEN, WIN))


def dot(a, b):
    return jnp.dot(a, b, preferred_element_type=F32)


def spectrum(first, second, table):
    return dot(jnp.concatenate([first, second, first, second], axis=1), table)


def half_spectrum(block, table):
    return dot(jnp.concatenate([block, block], axis=1), table)


def invert(re, im, table):
    y = dot(jnp.concatenate([re.astype(BF16), im.astype(BF16)], axis=1), table)
    return y[:, :FLEN] + y[:, FLEN:]


def invert_wide(y, table):
    hi = y.astype(BF16)
    lo = (y - hi.astype(F32)).astype(BF16)
    a, b = dot(hi, table), dot(lo, table)
    return a[:, :FLEN] + (a[:, FLEN:] + b[:, :FLEN])


def per_channel(h):
    groups = h.shape[0]
    return jnp.broadcast_to(h[:, None, :], (groups, GROUP_CH, FLEN)).reshape(groups * GROUP_CH, FLEN)


def group_sum(x):
    return jnp.sum(x.reshape(x.shape[0] // GROUP_CH, GROUP_CH, FLEN), axis=1)


def convolve(x, h, table):
    hr, hi = per_channel(h[:, :FLEN]), per_channel(h[:, FLEN:])
    xr, xi = x[:, :FLEN], x[:, FLEN:]
    return invert(xr * hr - xi * hi, xr * hi + xi * hr, table)


def correlate(v, h, table):
    hr, hi = per_channel(h[:, :FLEN]), per_channel(h[:, FLEN:])
    vr, vi = v[:, :FLEN], v[:, FLEN:]
    return invert(vr * hr + vi * hi, vi * hr - vr * hi, table)


def cross(a, b):
    ar, ai, br, bi = a[:, :FLEN], a[:, FLEN:], b[:, :FLEN], b[:, FLEN:]
    return jnp.concatenate([group_sum(ar * br + ai * bi), group_sum(ai * br - ar * bi)], axis=1)


def masked(flag, block):
    return jnp.where(flag[...] > 0, block, jnp.zeros_like(block))


def conv_kernel(flag, prev, cur, gate, h, fwd2, inv_b, gq):
    x = spectrum(masked(flag, prev[...]), cur[...], fwd2[...])
    gq[...] = (gate[...].astype(F32) * convolve(x, h[...], inv_b[...])).astype(BF16)
    return x


def corr_kernel(flag, nxt, core, h, fwd2, inv_a, gg):
    v = spectrum(core[...], masked(flag, nxt[...]), fwd2[...])
    gg[...] = correlate(v, h[...], inv_a[...]).astype(BF16)
    return v


def conv_taps_kernel(flag, prev, cur, gate, h, core, fwd2, inv_b, right, inv_a, gq, taps):
    x = conv_kernel(flag, prev, cur, gate, h, fwd2, inv_b, gq)
    taps[...] = invert_wide(cross(half_spectrum(core[...], right[...]), x), inv_a[...])


def corr_taps_kernel(flag, nxt, core, h, cur, fwd2, inv_a, left, gg, taps):
    v = corr_kernel(flag, nxt, core, h, fwd2, inv_a, gg)
    taps[...] = invert_wide(cross(v, half_spectrum(cur[...], left[...])), inv_a[...])


def rows_at(start, width, block):
    return pl.BlockSpec((block, width), lambda i, *_: (start // block + i, 0))


def whole(a):
    return pl.BlockSpec(a.shape, lambda i, *_: (0, 0))


ANY = pl.BlockSpec(memory_space=pl.ANY)


def run(kernel, flag, blocks, consts, out, start, size, carried=None, taps=False, cost=0):
    args = [flag] + [a for a, _ in blocks] + list(consts)
    specs = [whole(flag)] + [s for _, s in blocks] + [whole(c) for c in consts]
    drop, aliases = None, {}
    if carried is not None:
        at = len(args)
        aliases = {at: 0}
        args.append(carried)
        specs.append(ANY)
        drop = at
    shapes = [jax.ShapeDtypeStruct(out.shape, BF16)]
    outs = [rows_at(start, FLEN, BLOCK)]
    if taps:
        shapes.append(jax.ShapeDtypeStruct((size // GROUP_CH, FLEN), F32))
        outs.append(rows_at(0, FLEN, BLOCK // GROUP_CH))

    def body(*refs):
        kernel(*(r for i, r in enumerate(refs) if i != drop))

    return pl.pallas_call(
        body,
        out_shape=shapes,
        grid=(size // BLOCK,),
        in_specs=specs,
        out_specs=outs,
        input_output_aliases=aliases,
        compiler_params=pltpu.CompilerParams(vmem_limit_bytes=VMEM_MB * 1024 * 1024),
        cost_estimate=pl.CostEstimate(flops=cost * 10**9, bytes_accessed=cost * 10**7, transcendentals=0),
        name=kernel.__name__,
    )(*args)


def exchange(x, partner):
    n_ctx, n_fsdp = lax.axis_size("ctx"), lax.axis_size("fsdp")
    pairs = []
    for c in range(n_ctx):
        for f in range(n_fsdp):
            to = partner(c, f)
            if to is not None:
                pairs.append((c * n_fsdp + f, to[0] * n_fsdp + to[1]))
    return lax.ppermute(x, ("ctx", "fsdp"), pairs)


def after(array, done):
    return lax.optimization_barrier((array, done))[0]


def pick(a, i, axis):
    return lax.dynamic_index_in_dim(a, i, axis, keepdims=False)


def reduce_taps(x):
    core, low = lax.axis_index("fsdp") % 2, lax.axis_index("fsdp") // 2
    x = pick(x, core, 1) + exchange(pick(x, 1 - core, 1), lambda c, f: (c, f ^ 1))
    x = pick(x, low, 0) + exchange(pick(x, 1 - low, 0), lambda c, f: (c, f ^ 2))
    for partner in (
        lambda c, f: (c ^ 8, f),
        lambda c, f: ((3 - c // 8) * 8 + c % 8, f),
        lambda c, f: (c ^ 4, f),
        lambda c, f: (c ^ 1, f),
        lambda c, f: (c // 4 * 4 + 3 - c % 4, f),
    ):
        x = x + exchange(x, partner)
    return x


def per_device(query, gated, grad_out, filters):
    query, gated, grad_out = query[0], gated[0], grad_out[0]
    width = gated.shape[0]
    half = width // 2
    n_ctx = lax.axis_size("ctx")
    me = lax.axis_index("ctx")
    has_prev = jnp.full((1, FLEN), me > 0, BF16)
    has_next = jnp.full((1, FLEN), me < n_ctx - 1, BF16)
    fwd2, left, right, inv_a, inv_b = (jnp.asarray(t) for t in tables())
    up = [(i, (i + 1) % n_ctx) for i in range(n_ctx)]
    down = [(b, a) for a, b in up]

    rows = lambda a, start, size: lax.slice_in_dim(a, start, start + size, axis=0)
    product = lambda o, q, start, size: (rows(o, start, size).astype(F32) * rows(q, start, size).astype(F32)).astype(BF16)
    h_at = lambda start: rows_at(start // GROUP_CH, WIN, BLOCK // GROUP_CH)
    at = lambda start: rows_at(start, FLEN, BLOCK)

    fsdp = lax.axis_index("fsdp")
    far = exchange(filters, lambda c, f: (c, f ^ 2))
    column = jnp.where(fsdp // 2 == 0, jnp.stack([filters, far]), jnp.stack([far, filters])).astype(BF16)
    near = exchange(column, lambda c, f: (c, f ^ 1))
    taps = jnp.where(fsdp % 2 == 0, jnp.stack([column, near], axis=1), jnp.stack([near, column], axis=1)).reshape(-1, FLEN)
    h = dot(jnp.concatenate([taps, taps], axis=1), left)

    core_b = product(grad_out, query, half, half)
    sent_a, core_b, _ = lax.optimization_barrier((rows(gated, 0, half), core_b, far))
    prev_a = lax.ppermute(sent_a, "ctx", up)
    nxt_b = lax.ppermute(core_b, "ctx", down)
    late = lax.optimization_barrier((gated, grad_out, query, core_b))[:3]
    core_a = product(late[1], late[2], 0, half)
    prev_b = lax.ppermute(rows(late[0], half, half), "ctx", up)
    nxt_a = lax.ppermute(core_a, "ctx", down)

    gq, taps_a = run(
        conv_taps_kernel,
        has_prev,
        [(prev_a, at(0)), (gated, at(0)), (grad_out, at(0)), (h, h_at(0)), (core_a, at(0))],
        (fwd2, inv_b, right, inv_a),
        gated, 0, half, taps=True,
    )
    has_next, _ = lax.optimization_barrier((has_next, taps_a))
    gg, taps_b = run(
        corr_taps_kernel,
        has_next,
        [(nxt_b, at(0)), (core_b, at(0)), (h, h_at(half)), (gated, at(half))],
        (fwd2, inv_a, left),
        gated, half, half, taps=True,
    )
    partial = jnp.stack([taps_a, taps_b]).reshape(2, 2, -1, FLEN)
    prev_b, nxt_a, partial = lax.optimization_barrier((prev_b, nxt_a, partial))
    summed = reduce_taps(partial)
    gq, = run(
        conv_kernel,
        has_prev,
        [(prev_b, at(0)), (gated, at(half)), (grad_out, at(half)), (h, h_at(half))],
        (fwd2, inv_b),
        gated, half, half, carried=gq, cost=1,
    )
    gg, = run(
        corr_kernel,
        has_next,
        [(nxt_a, at(0)), (core_a, at(0)), (h, h_at(0))],
        (fwd2, inv_a),
        gated, 0, half, carried=gg, cost=1,
    )
    count = lax.axis_size("fsdp") * n_ctx * FLEN * GROUP_CH
    grad_filters = summed * (1.0 / math.sqrt(count))
    return (gq[None], gg[None], grad_filters)


def solution(mesh):
    return jax.shard_map(
        per_device,
        mesh=mesh,
        in_specs=(
            P("fsdp", None, "ctx"),
            P("fsdp", None, "ctx"),
            P("fsdp", None, "ctx"),
            P("fsdp", None),
        ),
        out_specs=(P("fsdp", None, "ctx"), P("fsdp", None, "ctx"), P("fsdp", None)),
        check_vma=False,
    )
```

time: 139 us -> 102 us (0.73)
  blocking collectives: 14.9 us -> 0 us
  starting transfers between devices: 31.6 us -> 19 us
  local copies, waits for them, and re-layouts: 13.6 us -> 3.21 us
  waiting for transfers between devices: 38.8 us -> 45.7 us
  Pallas kernels: 28.9 us -> 24.7 us
  matrix products: 3.02 us -> 1.21 us
    ppermute x8 -> x4, waiting for transfers between devices: 0.02 us -> 23.7 us  [the longest x1 19.1 us: per_device(): prev_a = lax.ppermute(sent_a, 'ctx', up)]
    ppermute x7 -> x9, waiting for transfers between devices: 38.8 us -> 22 us  [exchange(): return lax.ppermute(x, ('ctx', 'fsdp'), pairs)]
    all_gather x1 -> x0, blocking collectives: 14.9 us -> none  [per_device(): taps = lax.all_gather(filters.astype(BF16), 'fsdp', axis=0, tiled=True)]
    ppermute x8 -> x4, starting transfers between devices: 27.9 us -> 16.4 us  [the longest x1 8.57 us: per_device(): nxt_b = lax.ppermute(core_b, 'ctx', down)]
    unnamed x47 -> x16, local copies, waits for them, and re-layouts: 11.6 us -> 0.04 us
    pallas_call x4, Pallas kernels: 28.9 us -> 24.7 us  [run(): pl.pallas_call(body, out_shape=shapes, grid=(size // BLOCK,), in_specs=sp...]
    dot_general x5 -> x2, matrix products: 3.02 us -> 1.21 us  [dot(): return jnp.dot(a, b, preferred_element_type=F32)]
    ppermute x7 -> x9, starting transfers between devices: 3.67 us -> 2.64 us  [exchange(): return lax.ppermute(x, ('ctx', 'fsdp'), pairs)]
  transfers between devices with their start and end apart: 15 -> 13, of which waited for: 5 -> 8; matrix products, arithmetic and copies ran while one was open for 3% -> 9% of each run, Pallas kernels for 16% -> 24%
where the time goes in v2:
time: 102 us
  waiting for transfers between devices  45.7 us (45%)
  Pallas kernels  24.7 us (24%)
  starting transfers between devices  19 us (19%)
  other arithmetic  6.98 us (7%)
  local copies, waits for them, and re-layouts  3.21 us (3%)
  matrix products  1.21 us (1%)
    pallas_call x4, Pallas kernels, run(): pl.pallas_call(body, out_shape=shapes, grid=(size // BLOCK,), in_specs=sp...  24.7 us
    ppermute x9, waiting for transfers between devices, exchange(): return lax.ppermute(x, ('ctx', 'fsdp'), pairs)  22 us
    ppermute x1, waiting for transfers between devices, per_device(): prev_a = lax.ppermute(sent_a, 'ctx', up)  19.1 us
    ppermute x1, starting transfers between devices, per_device(): nxt_b = lax.ppermute(core_b, 'ctx', down)  8.57 us
    ppermute x1, starting transfers between devices, per_device(): nxt_a = lax.ppermute(core_a, 'ctx', down)  7.78 us
    ppermute x1, waiting for transfers between devices, per_device(): prev_b = lax.ppermute(rows(late[0], half, half), 'ctx', up)  4.6 us
    convert_element_type x2, other arithmetic, per_device(): (rows(o, start, size).astype(F32) * rows(q, start, size).astype(F32)).ast...  4.33 us
    ppermute x9, starting transfers between devices, exchange(): return lax.ppermute(x, ('ctx', 'fsdp'), pairs)  2.64 us
  transfers between devices with their start and end apart: 13, of which 8 were waited for; matrix products, arithmetic and copies ran while one was open for 9% of the time, Pallas kernels for 24%

profile of v2, /device:TPU:0, one launch (start us, length us, event | category | flops | bytes accessed | tf_op | source)
XLA Modules:
  0.0 101.6 jit_solution(12193503795383282476)
XLA Ops:
  0.6 1.0 convert
  1.6 1.7 %collective-permute-start = (bf16[128,128]{1,0:T(8,128)(2,1)S(1)}, bf16[128,128]{1,0:T(8,128)(2,1)S(1)}, u32[]{:S(2)}, u32[]{:S(2)}) collective-permute-start(bf16[128,128]{1,0:T(8,128)(2,1)S(1)} %convert), channel_id=1, source_target_pairs={{0,2},{1,3},{2,0},{3,1},{4,6},{5,7},{6,4},{7,5},{8,10},{9,11},{10,... | collective-permute-start | bytes 98312 | tf_op jit(solution)/shard_map/ppermute | solution.py:168
  3.3 2.8 %fusion.refs_2_ = bf16[4096,128]{1,0:T(8,128)(2,1)} fusion(bf16[1,8192,128]{2,1,0:T(8,128)(2,1)} %param.9, bf16[1,8192,128]{2,1,0:T(8,128)(2,1)} %param.11), kind=kLoop, calls=%fused_computation.3 | loop fusion | flops 2097152 | bytes 3145728 | tf_op jit(solution)/shard_map/convert_element_type | solution.py:207
  6.1 1.0 %slice_bitcast_fusion = bf16[4096,128]{1,0:T(8,128)(2,1)} fusion(bf16[1,8192,128]{2,1,0:T(8,128)(2,1)S(1)} %copy-done), kind=kLoop, calls=%fused_computation.4 | loop fusion | bytes 2097152 | tf_op jit(solution)/shard_map/slice | solution.py:206
  7.1 8.6 %collective-permute-start.5 = (bf16[4096,128]{1,0:T(8,128)(2,1)}, bf16[4096,128]{1,0:T(8,128)(2,1)}, u32[]{:S(2)}, u32[]{:S(2)}) collective-permute-start(bf16[4096,128]{1,0:T(8,128)(2,1)} %fusion.refs_2_), channel_id=1, source_target_pairs={{4,0},{8,4},{12,8},{16,12},{20,16},{24,20},{28,24},{32,28},{36,32}... | collective-permute-start | bytes 3145736 | tf_op jit(solution)/shard_map/ppermute | solution.py:221
  15.7 1.5 %multiply_convert_fusion.refs_5_.refs_2_ = bf16[4096,128]{1,0:T(8,128)(2,1)S(1)} fusion(bf16[8192,128]{1,0:T(8,128)(2,1)} %bitcast.36, bf16[8192,128]{1,0:T(8,128)(2,1)S(1)} %bitcast.35), kind=kLoop, calls=%fused_computation | loop fusion | flops 2097152 | bytes 3145728 | tf_op jit(solution)/shard_map/convert_element_type | solution.py:207
  17.3 7.8 %collective-permute-start.2 = (bf16[4096,128]{1,0:T(8,128)(2,1)S(1)}, bf16[4096,128]{1,0:T(8,128)(2,1)}, u32[]{:S(2)}, u32[]{:S(2)}) collective-permute-start(bf16[4096,128]{1,0:T(8,128)(2,1)S(1)} %multiply_convert_fusion.refs_5_.refs_2_), channel_id=1, source_target_pairs={{4,0},{8,4},{12,8},{16,12},{20,16},{24,20},{28,24},{32,28},{36,32}... | collective-permute-start | bytes 3145736 | tf_op jit(solution)/shard_map/ppermute | solution.py:225
  25.1 1.1 %slice.27 = bf16[4096,128]{1,0:T(8,128)(2,1)} slice(bf16[8192,128]{1,0:T(8,128)(2,1)S(1)} %bitcast.32), slice={[4096:8192], [0:128]} | slice | bytes 2097152 | tf_op jit(solution)/shard_map/slice | solution.py:206
  26.3 1.2 %collective-permute-done.4 = bf16[2,128,128]{2,1,0:T(8,128)(2,1)S(1)} collective-permute-done((bf16[2,128,128]{2,1,0:T(8,128)(2,1)S(1)}, bf16[2,128,128]{2,1,0:T(8,128)(2,1)S(1)}, u32[]{:S(2)}, u32[]{:S(2)}) %collective-permute-start.4) | collective-permute-done | bytes 65568 | tf_op jit(solution)/shard_map/ppermute | solution.py:168
  27.7 1.0 convolution_add_fusion.refs_4_.refs_3_
  28.7 19.1 %collective-permute-done.3.refs_1_ = bf16[4096,128]{1,0:T(8,128)(2,1)} collective-permute-done((bf16[4096,128]{1,0:T(8,128)(2,1)}, bf16[4096,128]{1,0:T(8,128)(2,1)}, u32[]{:S(2)}, u32[]{:S(2)}) %collective-permute-start.3) | collective-permute-done | bytes 1048608 | tf_op jit(solution)/shard_map/ppermute | solution.py:220
  48.4 7.0 %conv_taps_kernel.1 = (bf16[8192,128]{1,0:T(8,128)(2,1)}, f32[256,128]{1,0:T(8,128)}) custom-call(bf16[1,128]{1,0:T(2,128)(2,1)} %broadcast_in_dim.12.refs_0_, bf16[4096,128]{1,0:T(8,128)(2,1)} %collective-permute-done.3.refs_1_, bf16[8192,128]{1,0:T(8,128)(2,1)} %bitcast.29, bf16[8192,128]{1,0:T(8,128)(2,1)} %bitcast.33, ...), custom_call_target="tpu_custom_call" | custom-call | tf_op jit(solution)/shard_map/conv_taps_kernel/pallas_call | solution.py:147
  55.4 0.5 broadcast_in_dim.13.refs_0_
  56.0 6.9 %corr_taps_kernel.1 = (bf16[8192,128]{1,0:T(8,128)(2,1)}, f32[256,128]{1,0:T(8,128)}) custom-call(bf16[1,128]{1,0:T(2,128)(2,1)} %broadcast_in_dim.13.refs_0_, bf16[4096,128]{1,0:T(8,128)(2,1)} %collective-permute-done.5.refs_1_, bf16[4096,128]{1,0:T(8,128)(2,1)} %fusion.refs_2_, f32[512,256]{1,0:T(8,128)} %convolution_add_fusion.refs_4_.refs_3_, ...), custom_call_target="tpu_custom_call" | custom-call | tf_op jit(solution)/shard_map/corr_taps_kernel/pallas_call | solution.py:147
  62.9 0.9 pad_maximum_fusion
  63.8 4.6 %collective-permute-done.1.refs_1_ = bf16[4096,128]{1,0:T(8,128)(2,1)S(1)} collective-permute-done((bf16[4096,128]{1,0:T(8,128)(2,1)}, bf16[4096,128]{1,0:T(8,128)(2,1)S(1)}, u32[]{:S(2)}, u32[]{:S(2)}) %collective-permute-start.1) | collective-permute-done | bytes 1048608 | tf_op jit(solution)/shard_map/ppermute | solution.py:224
  68.6 1.3 %collective-permute-done.6 = f32[2,128,128]{2,1,0:T(8,128)S(1)} collective-permute-done((f32[2,128,128]{2,1,0:T(8,128)S(1)}, f32[2,128,128]{2,1,0:T(8,128)S(1)}, u32[]{:S(2)}, u32[]{:S(2)}) %collective-permute-start.6) | collective-permute-done | bytes 131104 | tf_op jit(solution)/shard_map/ppermute | solution.py:168
  70.3 4.0 %collective-permute-done.7 = f32[128,128]{1,0:T(8,128)S(1)} collective-permute-done((f32[128,128]{1,0:T(8,128)S(1)}, f32[128,128]{1,0:T(8,128)S(1)}, u32[]{:S(2)}, u32[]{:S(2)}) %collective-permute-start.7) | collective-permute-done | bytes 65568 | tf_op jit(solution)/shard_map/ppermute | solution.py:168
  74.4 4.3 %collective-permute-done.8 = f32[128,128]{1,0:T(8,128)S(1)} collective-permute-done((f32[128,128]{1,0:T(8,128)S(1)}, f32[128,128]{1,0:T(8,128)S(1)}, u32[]{:S(2)}, u32[]{:S(2)}) %collective-permute-start.8) | collective-permute-done | bytes 65568 | tf_op jit(solution)/shard_map/ppermute | solution.py:168
  78.7 5.5 %collective-permute-done.9 = f32[128,128]{1,0:T(8,128)S(1)} collective-permute-done((f32[128,128]{1,0:T(8,128)S(1)}, f32[128,128]{1,0:T(8,128)S(1)}, u32[]{:S(2)}, u32[]{:S(2)}) %collective-permute-start.9) | collective-permute-done | bytes 65568 | tf_op jit(solution)/shard_map/ppermute | solution.py:168
  84.3 5.8 %collective-permute-done.10 = f32[128,128]{1,0:T(8,128)S(1)} collective-permute-done((f32[128,128]{1,0:T(8,128)S(1)}, f32[128,128]{1,0:T(8,128)S(1)}, u32[]{:S(2)}, u32[]{:S(2)}) %collective-permute-start.10) | collective-permute-done | bytes 65568 | tf_op jit(solution)/shard_map/ppermute | solution.py:168
  90.2 5.2 %corr_kernel.1 = bf16[8192,128]{1,0:T(8,128)(2,1)} custom-call(bf16[1,128]{1,0:T(2,128)(2,1)} %broadcast_in_dim.13.refs_0_, bf16[4096,128]{1,0:T(8,128)(2,1)} %collective-permute-done.2.refs_1_, bf16[4096,128]{1,0:T(8,128)(2,1)} %copy-done.2, f32[512,256]{1,0:T(8,128)} %convolution_add_fusion.refs_4_.refs_3_, ...), custom_call_target="tpu_custom_call", output_to_operand_aliasing={{}: (6, {})} | custom-call | flops 1000000000 | bytes 10000000 | tf_op jit(solution)/shard_map/corr_kernel/pallas_call | solution.py:147
  95.5 5.5 %conv_kernel.1 = bf16[8192,128]{1,0:T(8,128)(2,1)} custom-call(bf16[1,128]{1,0:T(2,128)(2,1)} %broadcast_in_dim.12.refs_0_, bf16[4096,128]{1,0:T(8,128)(2,1)} %copy-done.3, bf16[8192,128]{1,0:T(8,128)(2,1)} %bitcast.31, bf16[8192,128]{1,0:T(8,128)(2,1)} %bitcast.34, f32[512,256]{1,0:T(8,128)} %convolution_add_fusion.refs_4_.refs_3_, ...), custom_call_target="tpu_custom_call", output_to_operand_aliasing={{}: (7, {})} | custom-call | flops 1000000000 | bytes 10000000 | tf_op jit(solution)/shard_map/conv_kernel/pallas_call | solution.py:147
  101.0 0.6 add_multiply_fusion
  (44 shorter events, 1.9 us)
Async XLA Ops:
  0.6 5.5 %copy-start = (bf16[1,8192,128]{2,1,0:T(8,128)(2,1)S(1)}, bf16[1,8192,128]{2,1,0:T(8,128)(2,1)}, u32[]{:S(2)}) copy-start(bf16[1,8192,128]{2,1,0:T(8,128)(2,1)} %param.10) | copy-start | bytes 6291460
  1.6 14.1 %copy-start.1 = (bf16[1,8192,128]{2,1,0:T(8,128)(2,1)S(1)}, bf16[1,8192,128]{2,1,0:T(8,128)(2,1)}, u32[]{:S(2)}) copy-start(bf16[1,8192,128]{2,1,0:T(8,128)(2,1)} %param.11) | copy-start | bytes 6291460
  1.6 5.5 %collective-permute-start = (bf16[128,128]{1,0:T(8,128)(2,1)S(1)}, bf16[128,128]{1,0:T(8,128)(2,1)S(1)}, u32[]{:S(2)}, u32[]{:S(2)}) collective-permute-start(bf16[128,128]{1,0:T(8,128)(2,1)S(1)} %convert), channel_id=1, source_target_pairs={{0,2},{1,3},{2,0},{3,1},{4,6},{5,7},{6,4},{7,5},{8,10},{9,11},{10,... | collective-permute-start | bytes 98312 | tf_op jit(solution)/shard_map/ppermute | solution.py:168
  7.1 48.8 %collective-permute-start.5 = (bf16[4096,128]{1,0:T(8,128)(2,1)}, bf16[4096,128]{1,0:T(8,128)(2,1)}, u32[]{:S(2)}, u32[]{:S(2)}) collective-permute-start(bf16[4096,128]{1,0:T(8,128)(2,1)} %fusion.refs_2_), channel_id=1, source_target_pairs={{4,0},{8,4},{12,8},{16,12},{20,16},{24,20},{28,24},{32,28},{36,32}... | collective-permute-start | bytes 3145736 | tf_op jit(solution)/shard_map/ppermute | solution.py:221
  15.7 10.4 %copy-start.4 = (f32[128,128]{1,0:T(8,128)S(1)}, f32[128,128]{1,0:T(8,128)}, u32[]{:S(2)}) copy-start(f32[128,128]{1,0:T(8,128)} %param.12) | copy-start | bytes 196612
  15.7 32.1 %collective-permute-start.3 = (bf16[4096,128]{1,0:T(8,128)(2,1)}, bf16[4096,128]{1,0:T(8,128)(2,1)}, u32[]{:S(2)}, u32[]{:S(2)}) collective-permute-start(bf16[4096,128]{1,0:T(8,128)(2,1)} %slice_bitcast_fusion), channel_id=1, source_target_pairs={{0,4},{4,8},{8,12},{12,16},{16,20},{20,24},{24,28},{28,32},{32,36}... | collective-permute-start | bytes 3145736 | tf_op jit(solution)/shard_map/ppermute | solution.py:220
  17.3 11.5 %copy-start.2 = (bf16[4096,128]{1,0:T(8,128)(2,1)}, bf16[4096,128]{1,0:T(8,128)(2,1)S(1)}, u32[]{:S(2)}) copy-start(bf16[4096,128]{1,0:T(8,128)(2,1)S(1)} %multiply_convert_fusion.refs_5_.refs_2_) | copy-start | bytes 3145732
  17.3 10.2 %copy-start.7 = (bf16[128,256]{1,0:T(8,128)(2,1)S(1)}, bf16[128,256]{1,0:T(8,128)(2,1)}, u32[]{:S(2)}) copy-start(bf16[128,256]{1,0:T(8,128)(2,1)} %constant.76) | copy-start | bytes 196612
  17.3 10.4 %copy-start.6 = (bf16[128,256]{1,0:T(8,128)(2,1)S(1)}, bf16[128,256]{1,0:T(8,128)(2,1)}, u32[]{:S(2)}) copy-start(bf16[128,256]{1,0:T(8,128)(2,1)} %constant.77) | copy-start | bytes 196612
  17.3 46.6 %collective-permute-start.2 = (bf16[4096,128]{1,0:T(8,128)(2,1)S(1)}, bf16[4096,128]{1,0:T(8,128)(2,1)}, u32[]{:S(2)}, u32[]{:S(2)}) collective-permute-start(bf16[4096,128]{1,0:T(8,128)(2,1)S(1)} %multiply_convert_fusion.refs_5_.refs_2_), channel_id=1, source_target_pairs={{4,0},{8,4},{12,8},{16,12},{20,16},{24,20},{28,24},{32,28},{36,32}... | collective-permute-start | bytes 3145736 | tf_op jit(solution)/shard_map/ppermute | solution.py:225
  26.1 42.3 %collective-permute-start.1 = (bf16[4096,128]{1,0:T(8,128)(2,1)}, bf16[4096,128]{1,0:T(8,128)(2,1)S(1)}, u32[]{:S(2)}, u32[]{:S(2)}) collective-permute-start(bf16[4096,128]{1,0:T(8,128)(2,1)} %slice.27), channel_id=1, source_target_pairs={{0,4},{4,8},{8,12},{12,16},{16,20},{20,24},{24,28},{28,32},{32,36}... | collective-permute-start | bytes 3145736 | tf_op jit(solution)/shard_map/ppermute | solution.py:224
  26.1 1.3 %collective-permute-start.4 = (bf16[2,128,128]{2,1,0:T(8,128)(2,1)S(1)}, bf16[2,128,128]{2,1,0:T(8,128)(2,1)S(1)}, u32[]{:S(2)}, u32[]{:S(2)}) collective-permute-start(bf16[2,128,128]{2,1,0:T(8,128)(2,1)S(1)} %fusion.2), channel_id=1, source_target_pairs={{0,1},{1,0},{2,3},{3,2},{4,5},{5,4},{6,7},{7,6},{8,9},{9,8},{10,11... | collective-permute-start | bytes 196616 | tf_op jit(solution)/shard_map/ppermute | solution.py:168
  56.0 7.0 %copy-start.5 = (f32[256,128]{1,0:T(8,128)S(1)}, f32[256,128]{1,0:T(8,128)}, u32[]{:S(2)}) copy-start(f32[256,128]{1,0:T(8,128)} %get-tuple-element.21) | copy-start | bytes 393220
  68.5 27.0 %copy-start.3 = (bf16[4096,128]{1,0:T(8,128)(2,1)}, bf16[4096,128]{1,0:T(8,128)(2,1)S(1)}, u32[]{:S(2)}) copy-start(bf16[4096,128]{1,0:T(8,128)(2,1)S(1)} %collective-permute-done.1.refs_1_) | copy-start | bytes 3145732
  68.5 1.4 %collective-permute-start.6 = (f32[2,128,128]{2,1,0:T(8,128)S(1)}, f32[2,128,128]{2,1,0:T(8,128)S(1)}, u32[]{:S(2)}, u32[]{:S(2)}) collective-permute-start(f32[2,128,128]{2,1,0:T(8,128)S(1)} %dynamic-slice_bitcast_fusion), channel_id=1, source_target_pairs={{0,1},{1,0},{2,3},{3,2},{4,5},{5,4},{6,7},{7,6},{8,9},{9,8},{10,11... | collective-permute-start | bytes 393224 | tf_op jit(solution)/shard_map/ppermute | solution.py:168
  69.9 4.3 %collective-permute-start.7 = (f32[128,128]{1,0:T(8,128)S(1)}, f32[128,128]{1,0:T(8,128)S(1)}, u32[]{:S(2)}, u32[]{:S(2)}) collective-permute-start(f32[128,128]{1,0:T(8,128)S(1)} %dynamic-slice_bitcast_fusion.1), channel_id=1, source_target_pairs={{0,2},{1,3},{2,0},{3,1},{4,6},{5,7},{6,4},{7,5},{8,10},{9,11},{10,... | collective-permute-start | bytes 196616 | tf_op jit(solution)/shard_map/ppermute | solution.py:168
  74.3 4.3 %collective-permute-start.8 = (f32[128,128]{1,0:T(8,128)S(1)}, f32[128,128]{1,0:T(8,128)S(1)}, u32[]{:S(2)}, u32[]{:S(2)}) collective-permute-start(f32[128,128]{1,0:T(8,128)S(1)} %bitcast_add_fusion.1), channel_id=1, source_target_pairs={{0,32},{1,33},{2,34},{3,35},{4,36},{5,37},{6,38},{7,39},{8,40},{9,... | collective-permute-start | bytes 196616 | tf_op jit(solution)/shard_map/ppermute | solution.py:168
  78.7 5.6 %collective-permute-start.9 = (f32[128,128]{1,0:T(8,128)S(1)}, f32[128,128]{1,0:T(8,128)S(1)}, u32[]{:S(2)}, u32[]{:S(2)}) collective-permute-start(f32[128,128]{1,0:T(8,128)S(1)} %add.50), channel_id=1, source_target_pairs={{0,96},{1,97},{2,98},{3,99},{4,100},{5,101},{6,102},{7,103},{8,104... | collective-permute-start | bytes 196616 | tf_op jit(solution)/shard_map/ppermute | solution.py:168
  84.2 5.8 %collective-permute-start.10 = (f32[128,128]{1,0:T(8,128)S(1)}, f32[128,128]{1,0:T(8,128)S(1)}, u32[]{:S(2)}, u32[]{:S(2)}) collective-permute-start(f32[128,128]{1,0:T(8,128)S(1)} %add.51), channel_id=1, source_target_pairs={{0,16},{1,17},{2,18},{3,19},{4,20},{5,21},{6,22},{7,23},{8,24},{9,... | collective-permute-start | bytes 196616 | tf_op jit(solution)/shard_map/ppermute | solution.py:168
  90.1 5.3 %collective-permute-start.11 = (f32[128,128]{1,0:T(8,128)S(1)}, f32[128,128]{1,0:T(8,128)S(1)}, u32[]{:S(2)}, u32[]{:S(2)}) collective-permute-start(f32[128,128]{1,0:T(8,128)S(1)} %add.52), channel_id=1, source_target_pairs={{0,4},{1,5},{2,6},{3,7},{4,0},{5,1},{6,2},{7,3},{8,12},{9,13},{10,... | collective-permute-start | bytes 196616 | tf_op jit(solution)/shard_map/ppermute | solution.py:168
  95.5 5.6 %collective-permute-start.12 = (f32[128,128]{1,0:T(8,128)S(1)}, f32[128,128]{1,0:T(8,128)S(1)}, u32[]{:S(2)}, u32[]{:S(2)}) collective-permute-start(f32[128,128]{1,0:T(8,128)S(1)} %add.53), channel_id=1, source_target_pairs={{0,12},{1,13},{2,14},{3,15},{4,8},{5,9},{6,10},{7,11},{8,4},{9,5},... | collective-permute-start | bytes 196616 | tf_op jit(solution)/shard_map/ppermute | solution.py:168

commit v3 on v2

--- a/solution.py
+++ b/solution.py
@@ -13,7 +13,7 @@
 GROUP_CH = 16
 WIN = 2 * FLEN
 BLOCK = 1024
-VMEM_MB = 60
+VMEM_MB = 63
 F32, BF16 = jnp.float32, jnp.bfloat16
 
 
@@ -88,29 +88,37 @@
     return jnp.concatenate([group_sum(ar * br + ai * bi), group_sum(ai * br - ar * bi)], axis=1)
 
 
-def masked(flag, block):
-    return jnp.where(flag[...] > 0, block, jnp.zeros_like(block))
-
-
-def conv_kernel(flag, prev, cur, gate, h, fwd2, inv_b, gq):
-    x = spectrum(masked(flag, prev[...]), cur[...], fwd2[...])
+def masked(present, block):
+    return jnp.where(present, block, jnp.zeros_like(block))
+
+
+def has_previous():
+    return lax.axis_index("ctx") > 0
+
+
+def has_next():
+    return lax.axis_index("ctx") < lax.axis_size("ctx") - 1
+
+
+def conv_kernel(prev, cur, gate, h, fwd2, inv_b, gq):
+    x = spectrum(masked(has_previous(), prev[...]), cur[...], fwd2[...])
     gq[...] = (gate[...].astype(F32) * convolve(x, h[...], inv_b[...])).astype(BF16)
     return x
 
 
-def corr_kernel(flag, nxt, core, h, fwd2, inv_a, gg):
-    v = spectrum(core[...], masked(flag, nxt[...]), fwd2[...])
+def corr_kernel(nxt, core, h, fwd2, inv_a, gg):
+    v = spectrum(core[...], masked(has_next(), nxt[...]), fwd2[...])
     gg[...] = correlate(v, h[...], inv_a[...]).astype(BF16)
     return v
 
 
-def conv_taps_kernel(flag, prev, cur, gate, h, core, fwd2, inv_b, right, inv_a, gq, taps):
-    x = conv_kernel(flag, prev, cur, gate, h, fwd2, inv_b, gq)
+def conv_taps_kernel(prev, cur, gate, h, core, fwd2, inv_b, right, inv_a, gq, taps):
+    x = conv_kernel(prev, cur, gate, h, fwd2, inv_b, gq)
     taps[...] = invert_wide(cross(half_spectrum(core[...], right[...]), x), inv_a[...])
 
 
-def corr_taps_kernel(flag, nxt, core, h, cur, fwd2, inv_a, left, gg, taps):
-    v = corr_kernel(flag, nxt, core, h, fwd2, inv_a, gg)
+def corr_taps_kernel(nxt, core, h, cur, fwd2, inv_a, left, gg, taps):
+    v = corr_kernel(nxt, core, h, fwd2, inv_a, gg)
     taps[...] = invert_wide(cross(v, half_spectrum(cur[...], left[...])), inv_a[...])
 
 
@@ -125,31 +133,26 @@
 ANY = pl.BlockSpec(memory_space=pl.ANY)
 
 
-def run(kernel, flag, blocks, consts, out, start, size, carried=None, taps=False, cost=0):
-    args = [flag] + [a for a, _ in blocks] + list(consts)
-    specs = [whole(flag)] + [s for _, s in blocks] + [whole(c) for c in consts]
-    drop, aliases = None, {}
-    if carried is not None:
-        at = len(args)
-        aliases = {at: 0}
-        args.append(carried)
-        specs.append(ANY)
-        drop = at
-    shapes = [jax.ShapeDtypeStruct(out.shape, BF16)]
-    outs = [rows_at(start, FLEN, BLOCK)]
-    if taps:
-        shapes.append(jax.ShapeDtypeStruct((size // GROUP_CH, FLEN), F32))
-        outs.append(rows_at(0, FLEN, BLOCK // GROUP_CH))
+def run(kernel, blocks, consts, results, size, cost=0):
+    args = [a for a, _ in blocks] + list(consts)
+    specs = [s for _, s in blocks] + [whole(c) for c in consts]
+    used, aliases = len(args), {}
+    for i, (out, _, _) in enumerate(results):
+        if not isinstance(out, jax.ShapeDtypeStruct):
+            aliases[len(args)] = i
+            args.append(out)
+            specs.append(ANY)
+    given = len(args)
 
     def body(*refs):
-        kernel(*(r for i, r in enumerate(refs) if i != drop))
+        kernel(*refs[:used], *refs[given:])
 
     return pl.pallas_call(
         body,
-        out_shape=shapes,
+        out_shape=[jax.ShapeDtypeStruct(out.shape, out.dtype) for out, _, _ in results],
         grid=(size // BLOCK,),
         in_specs=specs,
-        out_specs=outs,
+        out_specs=[rows_at(start, FLEN, block) for _, start, block in results],
         input_output_aliases=aliases,
         compiler_params=pltpu.CompilerParams(vmem_limit_bytes=VMEM_MB * 1024 * 1024),
         cost_estimate=pl.CostEstimate(flops=cost * 10**9, bytes_accessed=cost * 10**7, transcendentals=0),
@@ -176,14 +179,20 @@
     return lax.dynamic_index_in_dim(a, i, axis, keepdims=False)
 
 
-def reduce_taps(x):
+def reduce_first(x):
     core, low = lax.axis_index("fsdp") % 2, lax.axis_index("fsdp") // 2
     x = pick(x, core, 1) + exchange(pick(x, 1 - core, 1), lambda c, f: (c, f ^ 1))
-    x = pick(x, low, 0) + exchange(pick(x, 1 - low, 0), lambda c, f: (c, f ^ 2))
+    own, other = pick(x, low, 0), pick(x, 1 - low, 0)
+    beside = exchange(other, lambda c, f: (c, f ^ 2))
+    opposite = exchange(own, lambda c, f: (c ^ 4, f))
+    across = exchange(other, lambda c, f: (c ^ 4, f ^ 2))
+    return own + beside + opposite + across
+
+
+def reduce_rest(x):
     for partner in (
         lambda c, f: (c ^ 8, f),
         lambda c, f: ((3 - c // 8) * 8 + c % 8, f),
-        lambda c, f: (c ^ 4, f),
         lambda c, f: (c ^ 1, f),
         lambda c, f: (c // 4 * 4 + 3 - c % 4, f),
     ):
@@ -197,8 +206,6 @@
     half = width // 2
     n_ctx = lax.axis_size("ctx")
     me = lax.axis_index("ctx")
-    has_prev = jnp.full((1, FLEN), me > 0, BF16)
-    has_next = jnp.full((1, FLEN), me < n_ctx - 1, BF16)
     fwd2, left, right, inv_a, inv_b = (jnp.asarray(t) for t in tables())
     up = [(i, (i + 1) % n_ctx) for i in range(n_ctx)]
     down = [(b, a) for a, b in up]
@@ -209,53 +216,59 @@
     at = lambda start: rows_at(start, FLEN, BLOCK)
 
     fsdp = lax.axis_index("fsdp")
-    far = exchange(filters, lambda c, f: (c, f ^ 2))
+    far = lax.optimization_barrier(exchange(filters, lambda c, f: (c, f ^ 2)))
     column = jnp.where(fsdp // 2 == 0, jnp.stack([filters, far]), jnp.stack([far, filters])).astype(BF16)
     near = exchange(column, lambda c, f: (c, f ^ 1))
     taps = jnp.where(fsdp % 2 == 0, jnp.stack([column, near], axis=1), jnp.stack([near, column], axis=1)).reshape(-1, FLEN)
     h = dot(jnp.concatenate([taps, taps], axis=1), left)
 
+    sent_a, _ = lax.optimization_barrier((rows(gated, 0, half), far))
     core_b = product(grad_out, query, half, half)
-    sent_a, core_b, _ = lax.optimization_barrier((rows(gated, 0, half), core_b, far))
+    sent_b, _ = lax.optimization_barrier((core_b, near))
     prev_a = lax.ppermute(sent_a, "ctx", up)
-    nxt_b = lax.ppermute(core_b, "ctx", down)
+    nxt_b = lax.ppermute(sent_b, "ctx", down)
     late = lax.optimization_barrier((gated, grad_out, query, core_b))[:3]
     core_a = product(late[1], late[2], 0, half)
     prev_b = lax.ppermute(rows(late[0], half, half), "ctx", up)
     nxt_a = lax.ppermute(core_a, "ctx", down)
 
-    gq, taps_a = run(
+    full = jax.ShapeDtypeStruct(gated.shape, BF16)
+    groups, gblock = width // GROUP_CH, BLOCK // GROUP_CH
+    gq, partial = run(
         conv_taps_kernel,
-        has_prev,
         [(prev_a, at(0)), (gated, at(0)), (grad_out, at(0)), (h, h_at(0)), (core_a, at(0))],
         (fwd2, inv_b, right, inv_a),
-        gated, 0, half, taps=True,
+        [(full, 0, BLOCK), (jax.ShapeDtypeStruct((groups, FLEN), F32), 0, gblock)],
+        half,
     )
-    has_next, _ = lax.optimization_barrier((has_next, taps_a))
-    gg, taps_b = run(
+    gg, partial = run(
         corr_taps_kernel,
-        has_next,
         [(nxt_b, at(0)), (core_b, at(0)), (h, h_at(half)), (gated, at(half))],
         (fwd2, inv_a, left),
-        gated, half, half, taps=True,
+        [(full, half, BLOCK), (partial, groups // 2, gblock)],
+        half,
     )
-    partial = jnp.stack([taps_a, taps_b]).reshape(2, 2, -1, FLEN)
+    partial = reduce_first(partial.reshape(2, 2, -1, FLEN))
     prev_b, nxt_a, partial = lax.optimization_barrier((prev_b, nxt_a, partial))
-    summed = reduce_taps(partial)
-    gq, = run(
-        conv_kernel,
-        has_prev,
-        [(prev_b, at(0)), (gated, at(half)), (grad_out, at(half)), (h, h_at(half))],
-        (fwd2, inv_b),
-        gated, half, half, carried=gq, cost=1,
-    )
-    gg, = run(
-        corr_kernel,
-        has_next,
-        [(nxt_a, at(0)), (core_a, at(0)), (h, h_at(0))],
-        (fwd2, inv_a),
-        gated, 0, half, carried=gg, cost=1,
-    )
+    summed = reduce_rest(partial)
+    size = half // 2
+    for start in (0, size):
+        gq, = run(
+            conv_kernel,
+            [(prev_b, at(start)), (gated, at(half + start)), (grad_out, at(half + start)), (h, h_at(half + start))],
+            (fwd2, inv_b),
+            [(gq, half + start, BLOCK)],
+            size,
+            cost=5,
+        )
+        gg, = run(
+            corr_kernel,
+            [(nxt_a, at(start)), (core_a, at(start)), (h, h_at(start))],
+            (fwd2, inv_a),
+            [(gg, start, BLOCK)],
+            size,
+            cost=5,
+        )
     count = lax.axis_size("fsdp") * n_ctx * FLEN * GROUP_CH
     grad_filters = summed * (1.0 / math.sqrt(count))
     return (gq[None], gg[None], grad_filters)

time: 102 us -> 86.7 us (0.85)
  waiting for transfers between devices: 45.7 us -> 23.5 us
  starting transfers between devices: 19 us -> 22.3 us
  Pallas kernels: 24.7 us -> 27.6 us
  local copies, waits for them, and re-layouts: 3.21 us -> 2.07 us
    ppermute x9 -> x10, waiting for transfers between devices: 22 us -> 7.29 us  [exchange(): return lax.ppermute(x, ('ctx', 'fsdp'), pairs)]
    ppermute x9 -> x10, starting transfers between devices: 2.64 us -> 10.6 us  [exchange(): return lax.ppermute(x, ('ctx', 'fsdp'), pairs)]
    ppermute x1, starting transfers between devices: 7.78 us -> 0.96 us  [per_device(): nxt_a = lax.ppermute(core_a, 'ctx', down)]
    ppermute x1, waiting for transfers between devices: 4.6 us -> 0.01 us  [per_device(): prev_b = lax.ppermute(rows(late[0], half, half), 'ctx', up)]
    pallas_call x4 -> x6, Pallas kernels: 24.7 us -> 27.6 us  [run(): pl.pallas_call(body, out_shape=[jax.ShapeDtypeStruct(out.shape, out.dtype...]
    ppermute x1, waiting for transfers between devices: 19.1 us -> 16.2 us  [per_device(): prev_a = lax.ppermute(sent_a, 'ctx', up)]
    ppermute x1, starting transfers between devices: 0.01 us -> 1.99 us  [per_device(): prev_a = lax.ppermute(sent_a, 'ctx', up)]
    ppermute x1, starting transfers between devices: 0.01 us -> 1.07 us  [per_device(): prev_b = lax.ppermute(rows(late[0], half, half), 'ctx', up)]
  transfers between devices with their start and end apart: 13 -> 14, of which waited for: 8 -> 7; matrix products, arithmetic and copies ran while one was open for 9% -> 11% of each run, Pallas kernels for 24% -> 32%
where the time goes in v3:
time: 86.7 us; the launch traced here: 85.5 us
  Pallas kernels  27.6 us (32%)
  waiting for transfers between devices  23.5 us (27%)
  starting transfers between devices  22.3 us (26%)
  other arithmetic  7.91 us (9%)
  local copies, waits for them, and re-layouts  2.07 us (2%)
  matrix products  1.23 us (1%)
    pallas_call x6, Pallas kernels, run(): pl.pallas_call(body, out_shape=[jax.ShapeDtypeStruct(out.shape, out.dtype...  27.6 us
    ppermute x1, waiting for transfers between devices, per_device(): prev_a = lax.ppermute(sent_a, 'ctx', up)  16.2 us
    ppermute x10, starting transfers between devices, exchange(): return lax.ppermute(x, ('ctx', 'fsdp'), pairs)  10.6 us
    ppermute x1, starting transfers between devices, per_device(): nxt_b = lax.ppermute(sent_b, 'ctx', down)  7.72 us
    ppermute x10, waiting for transfers between devices, exchange(): return lax.ppermute(x, ('ctx', 'fsdp'), pairs)  7.29 us
    convert_element_type x2, other arithmetic, per_device(): (rows(o, start, size).astype(F32) * rows(q, start, size).astype(F32)).ast...  5.27 us
    ppermute x1, starting transfers between devices, per_device(): prev_a = lax.ppermute(sent_a, 'ctx', up)  1.99 us
  transfers between devices with their start and end apart: 14, of which 7 were waited for; matrix products, arithmetic and copies ran while one was open for 11% of the time, Pallas kernels for 32%

profile of v3, /device:TPU:0, one launch (start us, length us, event | category | flops | bytes accessed | tf_op | source)
XLA Modules:
  0.0 85.5 jit_solution(17236655204414306151)
XLA Ops:
  0.7 1.0 %convert = bf16[128,128]{1,0:T(8,128)(2,1)S(1)} convert(f32[128,128]{1,0:T(8,128)} %param.12) | non-fusion elementwise | flops 16384 | bytes 98304
  1.6 1.7 %collective-permute-start.2 = (bf16[128,128]{1,0:T(8,128)(2,1)S(1)}, bf16[128,128]{1,0:T(8,128)(2,1)S(1)}, u32[]{:S(2)}, u32[]{:S(2)}) collective-permute-start(bf16[128,128]{1,0:T(8,128)(2,1)S(1)} %convert), channel_id=1, source_target_pairs={{0,2},{1,3},{2,0},{3,1},{4,6},{5,7},{6,4},{7,5},{8,10},{9,11},{10,... | collective-permute-start | bytes 98312 | tf_op jit(solution)/shard_map/ppermute | solution.py:171
  3.3 2.8 %fusion.refs_1_ = bf16[4096,128]{1,0:T(8,128)(2,1)} fusion(bf16[1,8192,128]{2,1,0:T(8,128)(2,1)} %param.9, bf16[1,8192,128]{2,1,0:T(8,128)(2,1)} %param.11), kind=kLoop, calls=%fused_computation.3 | loop fusion | flops 2097152 | bytes 3145728 | tf_op jit(solution)/shard_map/convert_element_type | solution.py:214
  6.3 2.0 %collective-permute-start.5 = (bf16[4096,128]{1,0:T(8,128)(2,1)S(1)}, bf16[4096,128]{1,0:T(8,128)(2,1)}, u32[]{:S(2)}, u32[]{:S(2)}) collective-permute-start(bf16[4096,128]{1,0:T(8,128)(2,1)S(1)} %slice_bitcast_fusion), channel_id=1, source_target_pairs={{0,4},{4,8},{8,12},{12,16},{16,20},{20,24},{24,28},{28,32},{32,36}... | collective-permute-start | bytes 3145736 | tf_op jit(solution)/shard_map/ppermute | solution.py:228
  8.3 7.7 %collective-permute-start.4 = (bf16[4096,128]{1,0:T(8,128)(2,1)}, bf16[4096,128]{1,0:T(8,128)(2,1)}, u32[]{:S(2)}, u32[]{:S(2)}) collective-permute-start(bf16[4096,128]{1,0:T(8,128)(2,1)} %fusion.refs_1_), channel_id=1, source_target_pairs={{4,0},{8,4},{12,8},{16,12},{20,16},{24,20},{28,24},{32,28},{36,32}... | collective-permute-start | bytes 3145736 | tf_op jit(solution)/shard_map/ppermute | solution.py:229
  16.0 2.5 %multiply_convert_fusion.refs_4_.refs_1_ = bf16[4096,128]{1,0:T(8,128)(2,1)} fusion(bf16[8192,128]{1,0:T(8,128)(2,1)} %bitcast.37, bf16[8192,128]{1,0:T(8,128)(2,1)S(1)} %bitcast.36), kind=kLoop, calls=%fused_computation | loop fusion | flops 2097152 | bytes 3145728 | tf_op jit(solution)/shard_map/convert_element_type | solution.py:214
  18.5 1.0 %collective-permute-start.1 = (bf16[4096,128]{1,0:T(8,128)(2,1)}, bf16[4096,128]{1,0:T(8,128)(2,1)}, u32[]{:S(2)}, u32[]{:S(2)}) collective-permute-start(bf16[4096,128]{1,0:T(8,128)(2,1)} %multiply_convert_fusion.refs_4_.refs_1_), channel_id=1, source_target_pairs={{4,0},{8,4},{12,8},{16,12},{20,16},{24,20},{28,24},{32,28},{36,32}... | collective-permute-start | bytes 3145736 | tf_op jit(solution)/shard_map/ppermute | solution.py:233
  19.5 1.0 %slice.25 = bf16[4096,128]{1,0:T(8,128)(2,1)} slice(bf16[8192,128]{1,0:T(8,128)(2,1)S(1)} %bitcast.32), slice={[4096:8192], [0:128]} | slice | bytes 2097152 | tf_op jit(solution)/shard_map/slice | solution.py:213
  20.5 1.1 %collective-permute-start = (bf16[4096,128]{1,0:T(8,128)(2,1)}, bf16[4096,128]{1,0:T(8,128)(2,1)}, u32[]{:S(2)}, u32[]{:S(2)}) collective-permute-start(bf16[4096,128]{1,0:T(8,128)(2,1)} %slice.25), channel_id=1, source_target_pairs={{0,4},{4,8},{8,12},{12,16},{16,20},{20,24},{24,28},{28,32},{32,36}... | collective-permute-start | bytes 3145736 | tf_op jit(solution)/shard_map/ppermute | solution.py:232
  21.9 1.0 %convolution_add_fusion.refs_3_.refs_2_ = f32[512,256]{1,0:T(8,128)} fusion(f32[512,256]{1,0:T(8,128)S(1)} %fusion.3, bf16[512,128]{1,0:T(8,128)(2,1)S(1)} %bitcast.39, bf16[128,256]{1,0:T(8,128)(2,1)S(1)} %copy-done.3), kind=kOutput, calls=%fused_computation.2 | convolution fusion | flops 33685504 | bytes 1245184 | tf_op jit(solution)/shard_map/dot_general | solution.py:42
  22.9 16.2 %collective-permute-done.5.refs_0_ = bf16[4096,128]{1,0:T(8,128)(2,1)} collective-permute-done((bf16[4096,128]{1,0:T(8,128)(2,1)S(1)}, bf16[4096,128]{1,0:T(8,128)(2,1)}, u32[]{:S(2)}, u32[]{:S(2)}) %collective-permute-start.5) | collective-permute-done | bytes 1048608 | tf_op jit(solution)/shard_map/ppermute | solution.py:228
  39.1 7.0 %conv_taps_kernel.1 = (bf16[8192,128]{1,0:T(8,128)(2,1)}, f32[512,128]{1,0:T(8,128)}) custom-call(bf16[4096,128]{1,0:T(8,128)(2,1)} %collective-permute-done.5.refs_0_, bf16[8192,128]{1,0:T(8,128)(2,1)} %bitcast.28, bf16[8192,128]{1,0:T(8,128)(2,1)} %bitcast.33, f32[512,256]{1,0:T(8,128)} %convolution_add_fusion.refs_3_.refs_2_, ...), custom_call_target="tpu_custom_call" | custom-call | tf_op jit(solution)/shard_map/conv_taps_kernel/pallas_call | solution.py:150
  46.1 6.9 %corr_taps_kernel.1 = (bf16[8192,128]{1,0:T(8,128)(2,1)}, f32[512,128]{1,0:T(8,128)}) custom-call(bf16[4096,128]{1,0:T(8,128)(2,1)} %collective-permute-done.4.refs_0_, bf16[4096,128]{1,0:T(8,128)(2,1)} %fusion.refs_1_, f32[512,256]{1,0:T(8,128)} %convolution_add_fusion.refs_3_.refs_2_, bf16[8192,128]{1,0:T(8,128)(2,1)} %bitcast.29, ...), custom_call_target="tpu_custom_call", output_to_operand_aliasing={{1}: (7, {})} | custom-call | tf_op jit(solution)/shard_map/corr_taps_kernel/pallas_call | solution.py:150
  54.1 1.3 %collective-permute-done.6 = f32[2,128,128]{2,1,0:T(8,128)S(1)} collective-permute-done((f32[2,128,128]{2,1,0:T(8,128)S(1)}, f32[2,128,128]{2,1,0:T(8,128)S(1)}, u32[]{:S(2)}, u32[]{:S(2)}) %collective-permute-start.6) | collective-permute-done | bytes 131104 | tf_op jit(solution)/shard_map/ppermute | solution.py:171
  57.4 3.7 %collective-permute-start.9 = (f32[128,128]{1,0:T(8,128)S(1)}, f32[128,128]{1,0:T(8,128)S(1)}, u32[]{:S(2)}, u32[]{:S(2)}) collective-permute-start(f32[128,128]{1,0:T(8,128)S(1)} %get-tuple-element.28), channel_id=1, source_target_pairs={{0,18},{1,19},{2,16},{3,17},{4,22},{5,23},{6,20},{7,21},{8,26},{9,... | collective-permute-start | bytes 196616 | tf_op jit(solution)/shard_map/ppermute | solution.py:171
  61.1 1.5 %collective-permute-done.7 = f32[128,128]{1,0:T(8,128)S(1)} collective-permute-done((f32[128,128]{1,0:T(8,128)S(1)}, f32[128,128]{1,0:T(8,128)S(1)}, u32[]{:S(2)}, u32[]{:S(2)}) %collective-permute-start.7) | collective-permute-done | bytes 65568 | tf_op jit(solution)/shard_map/ppermute | solution.py:171
  62.6 1.1 %collective-permute-done.8 = f32[128,128]{1,0:T(8,128)S(1)} collective-permute-done((f32[128,128]{1,0:T(8,128)S(1)}, f32[128,128]{1,0:T(8,128)S(1)}, u32[]{:S(2)}, u32[]{:S(2)}) %collective-permute-start.8) | collective-permute-done | bytes 65568 | tf_op jit(solution)/shard_map/ppermute | solution.py:171
  64.4 1.2 %collective-permute-start.10 = (f32[128,128]{1,0:T(8,128)S(1)}, f32[128,128]{1,0:T(8,128)S(1)}, u32[]{:S(2)}, u32[]{:S(2)}) collective-permute-start(f32[128,128]{1,0:T(8,128)S(1)} %add_add_fusion), channel_id=1, source_target_pairs={{0,32},{1,33},{2,34},{3,35},{4,36},{5,37},{6,38},{7,39},{8,40},{9,... | collective-permute-start | bytes 196616 | tf_op jit(solution)/shard_map/ppermute | solution.py:171
  65.6 3.4 %corr_kernel.2.refs_5_ = bf16[8192,128]{1,0:T(8,128)(2,1)} custom-call(bf16[4096,128]{1,0:T(8,128)(2,1)} %collective-permute-done.1.refs_0_, bf16[4096,128]{1,0:T(8,128)(2,1)} %multiply_convert_fusion.refs_4_.refs_1_, f32[512,256]{1,0:T(8,128)} %convolution_add_fusion.refs_3_.refs_2_, ...), custom_call_target="tpu_custom_call", output_to_operand_aliasing={{}: (5, {})} | custom-call | flops 5000000000 | bytes 50000000 | tf_op jit(solution)/shard_map/corr_kernel/pallas_call | solution.py:150
  69.0 2.5 %collective-permute-start.11 = (f32[128,128]{1,0:T(8,128)S(1)}, f32[128,128]{1,0:T(8,128)S(1)}, u32[]{:S(2)}, u32[]{:S(2)}) collective-permute-start(f32[128,128]{1,0:T(8,128)S(1)} %add.55), channel_id=1, source_target_pairs={{0,96},{1,97},{2,98},{3,99},{4,100},{5,101},{6,102},{7,103},{8,104... | collective-permute-start | bytes 196616 | tf_op jit(solution)/shard_map/ppermute | solution.py:171
  71.5 3.4 %corr_kernel.3 = bf16[8192,128]{1,0:T(8,128)(2,1)} custom-call(bf16[4096,128]{1,0:T(8,128)(2,1)} %collective-permute-done.1.refs_0_, bf16[4096,128]{1,0:T(8,128)(2,1)} %multiply_convert_fusion.refs_4_.refs_1_, f32[512,256]{1,0:T(8,128)} %convolution_add_fusion.refs_3_.refs_2_, ...), custom_call_target="tpu_custom_call", output_to_operand_aliasing={{}: (5, {})} | custom-call | flops 5000000000 | bytes 50000000 | tf_op jit(solution)/shard_map/corr_kernel/pallas_call | solution.py:150
  75.0 3.5 %conv_kernel.2.refs_6_ = bf16[8192,128]{1,0:T(8,128)(2,1)} custom-call(bf16[4096,128]{1,0:T(8,128)(2,1)} %collective-permute-done.refs_0_, bf16[8192,128]{1,0:T(8,128)(2,1)} %bitcast.30, bf16[8192,128]{1,0:T(8,128)(2,1)} %bitcast.34, f32[512,256]{1,0:T(8,128)} %convolution_add_fusion.refs_3_.refs_2_, ...), custom_call_target="tpu_custom_call", output_to_operand_aliasing={{}: (6, {})} | custom-call | flops 5000000000 | bytes 50000000 | tf_op jit(solution)/shard_map/conv_kernel/pallas_call | solution.py:150
  79.5 3.4 %conv_kernel.3 = bf16[8192,128]{1,0:T(8,128)(2,1)} custom-call(bf16[4096,128]{1,0:T(8,128)(2,1)} %collective-permute-done.refs_0_, bf16[8192,128]{1,0:T(8,128)(2,1)} %bitcast.31, bf16[8192,128]{1,0:T(8,128)(2,1)} %bitcast.35, f32[512,256]{1,0:T(8,128)} %convolution_add_fusion.refs_3_.refs_2_, ...), custom_call_target="tpu_custom_call", output_to_operand_aliasing={{}: (6, {})} | custom-call | flops 5000000000 | bytes 50000000 | tf_op jit(solution)/shard_map/conv_kernel/pallas_call | solution.py:150
  82.9 1.9 %collective-permute-done.13 = f32[128,128]{1,0:T(8,128)S(1)} collective-permute-done((f32[128,128]{1,0:T(8,128)S(1)}, f32[128,128]{1,0:T(8,128)S(1)}, u32[]{:S(2)}, u32[]{:S(2)}) %collective-permute-start.13) | collective-permute-done | bytes 65568 | tf_op jit(solution)/shard_map/ppermute | solution.py:171
  (38 shorter events, 5.8 us)
Async XLA Ops:
  0.6 5.5 %copy-start.2 = (f32[128,128]{1,0:T(8,128)S(1)}, f32[128,128]{1,0:T(8,128)}, u32[]{:S(2)}) copy-start(f32[128,128]{1,0:T(8,128)} %param.12) | copy-start | bytes 196612
  0.6 5.6 %copy-start = (bf16[1,8192,128]{2,1,0:T(8,128)(2,1)S(1)}, bf16[1,8192,128]{2,1,0:T(8,128)(2,1)}, u32[]{:S(2)}) copy-start(bf16[1,8192,128]{2,1,0:T(8,128)(2,1)} %param.10) | copy-start | bytes 6291460
  1.6 4.5 %collective-permute-start.2 = (bf16[128,128]{1,0:T(8,128)(2,1)S(1)}, bf16[128,128]{1,0:T(8,128)(2,1)S(1)}, u32[]{:S(2)}, u32[]{:S(2)}) collective-permute-start(bf16[128,128]{1,0:T(8,128)(2,1)S(1)} %convert), channel_id=1, source_target_pairs={{0,2},{1,3},{2,0},{3,1},{4,6},{5,7},{6,4},{7,5},{8,10},{9,11},{10,... | collective-permute-start | bytes 98312 | tf_op jit(solution)/shard_map/ppermute | solution.py:171
  6.1 9.9 %copy-start.1 = (bf16[1,8192,128]{2,1,0:T(8,128)(2,1)S(1)}, bf16[1,8192,128]{2,1,0:T(8,128)(2,1)}, u32[]{:S(2)}) copy-start(bf16[1,8192,128]{2,1,0:T(8,128)(2,1)} %param.11) | copy-start | bytes 6291460
  6.1 2.2 %collective-permute-start.3 = (bf16[2,128,128]{2,1,0:T(8,128)(2,1)S(1)}, bf16[2,128,128]{2,1,0:T(8,128)(2,1)S(1)}, u32[]{:S(2)}, u32[]{:S(2)}) collective-permute-start(bf16[2,128,128]{2,1,0:T(8,128)(2,1)S(1)} %fusion.1), channel_id=1, source_target_pairs={{0,1},{1,0},{2,3},{3,2},{4,5},{5,4},{6,7},{7,6},{8,9},{9,8},{10,11... | collective-permute-start | bytes 196616 | tf_op jit(solution)/shard_map/ppermute | solution.py:171
  6.3 15.3 %copy-start.4 = (bf16[128,256]{1,0:T(8,128)(2,1)S(1)}, bf16[128,256]{1,0:T(8,128)(2,1)}, u32[]{:S(2)}) copy-start(bf16[128,256]{1,0:T(8,128)(2,1)} %constant.69) | copy-start | bytes 196612
  6.3 32.8 %collective-permute-start.5 = (bf16[4096,128]{1,0:T(8,128)(2,1)S(1)}, bf16[4096,128]{1,0:T(8,128)(2,1)}, u32[]{:S(2)}, u32[]{:S(2)}) collective-permute-start(bf16[4096,128]{1,0:T(8,128)(2,1)S(1)} %slice_bitcast_fusion), channel_id=1, source_target_pairs={{0,4},{4,8},{8,12},{12,16},{16,20},{20,24},{24,28},{28,32},{32,36}... | collective-permute-start | bytes 3145736 | tf_op jit(solution)/shard_map/ppermute | solution.py:228
  8.3 37.8 %collective-permute-start.4 = (bf16[4096,128]{1,0:T(8,128)(2,1)}, bf16[4096,128]{1,0:T(8,128)(2,1)}, u32[]{:S(2)}, u32[]{:S(2)}) collective-permute-start(bf16[4096,128]{1,0:T(8,128)(2,1)} %fusion.refs_1_), channel_id=1, source_target_pairs={{4,0},{8,4},{12,8},{16,12},{20,16},{24,20},{28,24},{32,28},{36,32}... | collective-permute-start | bytes 3145736 | tf_op jit(solution)/shard_map/ppermute | solution.py:229
  18.5 3.3 %copy-start.3 = (bf16[128,256]{1,0:T(8,128)(2,1)S(1)}, bf16[128,256]{1,0:T(8,128)(2,1)}, u32[]{:S(2)}) copy-start(bf16[128,256]{1,0:T(8,128)(2,1)} %constant.70) | copy-start | bytes 196612
  18.5 45.9 %collective-permute-start.1 = (bf16[4096,128]{1,0:T(8,128)(2,1)}, bf16[4096,128]{1,0:T(8,128)(2,1)}, u32[]{:S(2)}, u32[]{:S(2)}) collective-permute-start(bf16[4096,128]{1,0:T(8,128)(2,1)} %multiply_convert_fusion.refs_4_.refs_1_), channel_id=1, source_target_pairs={{4,0},{8,4},{12,8},{16,12},{20,16},{24,20},{28,24},{32,28},{36,32}... | collective-permute-start | bytes 3145736 | tf_op jit(solution)/shard_map/ppermute | solution.py:233
  20.5 43.9 %collective-permute-start = (bf16[4096,128]{1,0:T(8,128)(2,1)}, bf16[4096,128]{1,0:T(8,128)(2,1)}, u32[]{:S(2)}, u32[]{:S(2)}) collective-permute-start(bf16[4096,128]{1,0:T(8,128)(2,1)} %slice.25), channel_id=1, source_target_pairs={{0,4},{4,8},{8,12},{12,16},{16,20},{20,24},{24,28},{28,32},{32,36}... | collective-permute-start | bytes 3145736 | tf_op jit(solution)/shard_map/ppermute | solution.py:232
  54.0 1.4 %collective-permute-start.6 = (f32[2,128,128]{2,1,0:T(8,128)S(1)}, f32[2,128,128]{2,1,0:T(8,128)S(1)}, u32[]{:S(2)}, u32[]{:S(2)}) collective-permute-start(f32[2,128,128]{2,1,0:T(8,128)S(1)} %dynamic-slice_bitcast_fusion), channel_id=1, source_target_pairs={{0,1},{1,0},{2,3},{3,2},{4,5},{5,4},{6,7},{7,6},{8,9},{9,8},{10,11... | collective-permute-start | bytes 393224 | tf_op jit(solution)/shard_map/ppermute | solution.py:171
  56.3 6.3 %collective-permute-start.7 = (f32[128,128]{1,0:T(8,128)S(1)}, f32[128,128]{1,0:T(8,128)S(1)}, u32[]{:S(2)}, u32[]{:S(2)}) collective-permute-start(f32[128,128]{1,0:T(8,128)S(1)} %get-tuple-element.28), channel_id=1, source_target_pairs={{0,2},{1,3},{2,0},{3,1},{4,6},{5,7},{6,4},{7,5},{8,10},{9,11},{10,... | collective-permute-start | bytes 196616 | tf_op jit(solution)/shard_map/ppermute | solution.py:171
  56.9 6.8 %collective-permute-start.8 = (f32[128,128]{1,0:T(8,128)S(1)}, f32[128,128]{1,0:T(8,128)S(1)}, u32[]{:S(2)}, u32[]{:S(2)}) collective-permute-start(f32[128,128]{1,0:T(8,128)S(1)} %get-tuple-element.27), channel_id=1, source_target_pairs={{0,16},{1,17},{2,18},{3,19},{4,20},{5,21},{6,22},{7,23},{8,24},{9,... | collective-permute-start | bytes 196616 | tf_op jit(solution)/shard_map/ppermute | solution.py:171
  57.4 7.0 %collective-permute-start.9 = (f32[128,128]{1,0:T(8,128)S(1)}, f32[128,128]{1,0:T(8,128)S(1)}, u32[]{:S(2)}, u32[]{:S(2)}) collective-permute-start(f32[128,128]{1,0:T(8,128)S(1)} %get-tuple-element.28), channel_id=1, source_target_pairs={{0,18},{1,19},{2,16},{3,17},{4,22},{5,23},{6,20},{7,21},{8,26},{9,... | collective-permute-start | bytes 196616 | tf_op jit(solution)/shard_map/ppermute | solution.py:171
  64.4 4.6 %collective-permute-start.10 = (f32[128,128]{1,0:T(8,128)S(1)}, f32[128,128]{1,0:T(8,128)S(1)}, u32[]{:S(2)}, u32[]{:S(2)}) collective-permute-start(f32[128,128]{1,0:T(8,128)S(1)} %add_add_fusion), channel_id=1, source_target_pairs={{0,32},{1,33},{2,34},{3,35},{4,36},{5,37},{6,38},{7,39},{8,40},{9,... | collective-permute-start | bytes 196616 | tf_op jit(solution)/shard_map/ppermute | solution.py:171
  69.0 5.9 %collective-permute-start.11 = (f32[128,128]{1,0:T(8,128)S(1)}, f32[128,128]{1,0:T(8,128)S(1)}, u32[]{:S(2)}, u32[]{:S(2)}) collective-permute-start(f32[128,128]{1,0:T(8,128)S(1)} %add.55), channel_id=1, source_target_pairs={{0,96},{1,97},{2,98},{3,99},{4,100},{5,101},{6,102},{7,103},{8,104... | collective-permute-start | bytes 196616 | tf_op jit(solution)/shard_map/ppermute | solution.py:171
  74.9 4.3 %collective-permute-start.12 = (f32[128,128]{1,0:T(8,128)S(1)}, f32[128,128]{1,0:T(8,128)S(1)}, u32[]{:S(2)}, u32[]{:S(2)}) collective-permute-start(f32[128,128]{1,0:T(8,128)S(1)} %add.56), channel_id=1, source_target_pairs={{0,4},{1,5},{2,6},{3,7},{4,0},{5,1},{6,2},{7,3},{8,12},{9,13},{10,... | collective-permute-start | bytes 196616 | tf_op jit(solution)/shard_map/ppermute | solution.py:171
  79.3 5.6 %collective-permute-start.13 = (f32[128,128]{1,0:T(8,128)S(1)}, f32[128,128]{1,0:T(8,128)S(1)}, u32[]{:S(2)}, u32[]{:S(2)}) collective-permute-start(f32[128,128]{1,0:T(8,128)S(1)} %add.57), channel_id=1, source_target_pairs={{0,12},{1,13},{2,14},{3,15},{4,8},{5,9},{6,10},{7,11},{8,4},{9,5},... | collective-permute-start | bytes 196616 | tf_op jit(solution)/shard_map/ppermute | solution.py:171

commit v4 on v3

--- a/solution.py
+++ b/solution.py
@@ -133,6 +133,17 @@
 ANY = pl.BlockSpec(memory_space=pl.ANY)
 
 
+def taps_kernel(column, near, left, h):
+    swapped = lax.axis_index("fsdp") % 2 > 0
+    table = left[...]
+    for low in range(2):
+        for core in range(2):
+            mine, other = column[low], near[low]
+            taps = jnp.where(swapped, other, mine) if core == 0 else jnp.where(swapped, mine, other)
+            at = (low * 2 + core) * FLEN
+            h[at : at + FLEN, :] = half_spectrum(taps.astype(BF16), table)
+
+
 def run(kernel, blocks, consts, results, size, cost=0):
     args = [a for a, _ in blocks] + list(consts)
     specs = [s for _, s in blocks] + [whole(c) for c in consts]
@@ -189,15 +200,14 @@
     return own + beside + opposite + across
 
 
+def around(x, partners):
+    others = [exchange(x, partner) for partner in partners]
+    return x + others[0] + others[1] + others[2]
+
+
 def reduce_rest(x):
-    for partner in (
-        lambda c, f: (c ^ 8, f),
-        lambda c, f: ((3 - c // 8) * 8 + c % 8, f),
-        lambda c, f: (c ^ 1, f),
-        lambda c, f: (c // 4 * 4 + 3 - c % 4, f),
-    ):
-        x = x + exchange(x, partner)
-    return x
+    x = around(x, [lambda c, f, step=step: ((c + 8 * step) % 32, f) for step in (1, 3, 2)])
+    return around(x, [lambda c, f, step=step: (c // 4 * 4 + (c + step) % 4, f) for step in (1, 3, 2)])
 
 
 def per_device(query, gated, grad_out, filters):
@@ -216,18 +226,19 @@
     at = lambda start: rows_at(start, FLEN, BLOCK)
 
     fsdp = lax.axis_index("fsdp")
-    far = lax.optimization_barrier(exchange(filters, lambda c, f: (c, f ^ 2)))
-    column = jnp.where(fsdp // 2 == 0, jnp.stack([filters, far]), jnp.stack([far, filters])).astype(BF16)
+    far = exchange(filters, lambda c, f: (c, f ^ 2))
+    column = jnp.where(fsdp // 2 == 0, jnp.stack([filters, far]), jnp.stack([far, filters]))
     near = exchange(column, lambda c, f: (c, f ^ 1))
-    taps = jnp.where(fsdp % 2 == 0, jnp.stack([column, near], axis=1), jnp.stack([near, column], axis=1)).reshape(-1, FLEN)
-    h = dot(jnp.concatenate([taps, taps], axis=1), left)
+    h = pl.pallas_call(
+        taps_kernel, out_shape=jax.ShapeDtypeStruct((width // GROUP_CH, WIN), F32), name="taps_spectra"
+    )(column, near, left)
 
     sent_a, _ = lax.optimization_barrier((rows(gated, 0, half), far))
     core_b = product(grad_out, query, half, half)
     sent_b, _ = lax.optimization_barrier((core_b, near))
     prev_a = lax.ppermute(sent_a, "ctx", up)
     nxt_b = lax.ppermute(sent_b, "ctx", down)
-    late = lax.optimization_barrier((gated, grad_out, query, core_b))[:3]
+    late = lax.optimization_barrier((gated, grad_out, query, core_b, near))[:3]
     core_a = product(late[1], late[2], 0, half)
     prev_b = lax.ppermute(rows(late[0], half, half), "ctx", up)
     nxt_a = lax.ppermute(core_a, "ctx", down)
@@ -249,26 +260,28 @@
         half,
     )
     partial = reduce_first(partial.reshape(2, 2, -1, FLEN))
-    prev_b, nxt_a, partial = lax.optimization_barrier((prev_b, nxt_a, partial))
-    summed = reduce_rest(partial)
-    size = half // 2
-    for start in (0, size):
-        gq, = run(
+    def conv(gq, start, size, cost):
+        return run(
             conv_kernel,
             [(prev_b, at(start)), (gated, at(half + start)), (grad_out, at(half + start)), (h, h_at(half + start))],
             (fwd2, inv_b),
             [(gq, half + start, BLOCK)],
             size,
-            cost=5,
-        )
-        gg, = run(
-            corr_kernel,
-            [(nxt_a, at(start)), (core_a, at(start)), (h, h_at(start))],
-            (fwd2, inv_a),
-            [(gg, start, BLOCK)],
-            size,
-            cost=5,
-        )
+            cost,
+        )[0]
+
+    gq = conv(gq, 0, half // 2, 0)
+    gq, nxt_a, partial = lax.optimization_barrier((gq, nxt_a, partial))
+    summed = reduce_rest(partial)
+    gq = conv(gq, half // 2, half // 2, 5)
+    gg, = run(
+        corr_kernel,
+        [(nxt_a, at(0)), (core_a, at(0)), (h, h_at(0))],
+        (fwd2, inv_a),
+        [(gg, 0, BLOCK)],
+        half,
+        5,
+    )
     count = lax.axis_size("fsdp") * n_ctx * FLEN * GROUP_CH
     grad_filters = summed * (1.0 / math.sqrt(count))
     return (gq[None], gg[None], grad_filters)

time: 86.7 us -> 84.3 us (0.972)
  starting transfers between devices: 22.3 us -> 32.2 us
  waiting for transfers between devices: 23.5 us -> 14.8 us
  other arithmetic: 7.91 us -> 5.7 us
  matrix products: 1.23 us -> 0 us
    ppermute x1, starting transfers between devices: 0.96 us -> 7.74 us  [per_device(): nxt_a = lax.ppermute(core_a, 'ctx', down)]
    ppermute x1, waiting for transfers between devices: 16.2 us -> 10.8 us  [per_device(): prev_a = lax.ppermute(sent_a, 'ctx', up)]
    ppermute x10 -> x12, starting transfers between devices: 10.6 us -> 14.2 us  [exchange(): return lax.ppermute(x, ('ctx', 'fsdp'), pairs)]
    ppermute x10 -> x12, waiting for transfers between devices: 7.29 us -> 3.64 us  [exchange(): return lax.ppermute(x, ('ctx', 'fsdp'), pairs)]
    pallas_call x0 -> x1, Pallas kernels: none -> 2.05 us  [per_device(): pl.pallas_call(taps_kernel, out_shape=jax.ShapeDtypeStruct((width // GROU...]
    pallas_call x6 -> x5, Pallas kernels: 27.6 us -> 26.1 us  [run(): pl.pallas_call(body, out_shape=[jax.ShapeDtypeStruct(out.shape, out.dtype...]
    dot_general x2 -> x0, matrix products: 1.23 us -> none  [dot(): return jnp.dot(a, b, preferred_element_type=F32)]
    convert_element_type x2, other arithmetic: 5.27 us -> 4.09 us  [per_device(): (rows(o, start, size).astype(F32) * rows(q, start, size).astype(F32)).ast...]
  transfers between devices with their start and end apart: 14 -> 16, of which waited for: 7 -> 4; matrix products, arithmetic and copies ran while one was open for 11% -> 8% of each run, Pallas kernels for 32% -> 34%
where the time goes in v4:
time: 84.3 us; the launch traced here: 83.7 us
  starting transfers between devices  32.2 us (38%)
  Pallas kernels  28.1 us (33%)
  waiting for transfers between devices  14.8 us (18%)
  other arithmetic  5.7 us (7%)
  local copies, waits for them, and re-layouts  2.07 us (2%)
    pallas_call x5, Pallas kernels, run(): pl.pallas_call(body, out_shape=[jax.ShapeDtypeStruct(out.shape, out.dtype...  26.1 us
    ppermute x12, starting transfers between devices, exchange(): return lax.ppermute(x, ('ctx', 'fsdp'), pairs)  14.2 us
    ppermute x1, waiting for transfers between devices, per_device(): prev_a = lax.ppermute(sent_a, 'ctx', up)  10.8 us
    ppermute x1, starting transfers between devices, per_device(): nxt_b = lax.ppermute(sent_b, 'ctx', down)  8.12 us
    ppermute x1, starting transfers between devices, per_device(): nxt_a = lax.ppermute(core_a, 'ctx', down)  7.74 us
    convert_element_type x2, other arithmetic, per_device(): (rows(o, start, size).astype(F32) * rows(q, start, size).astype(F32)).ast...  4.09 us
    ppermute x12, waiting for transfers between devices, exchange(): return lax.ppermute(x, ('ctx', 'fsdp'), pairs)  3.64 us
    ppermute x1, starting transfers between devices, per_device(): prev_a = lax.ppermute(sent_a, 'ctx', up)  2.06 us
  transfers between devices with their start and end apart: 16, of which 4 were waited for; matrix products, arithmetic and copies ran while one was open for 8% of the time, Pallas kernels for 34%

profile of v4, /device:TPU:0, one launch (start us, length us, event | category | flops | bytes accessed | tf_op | source)
XLA Modules:
  0.0 83.7 jit_solution(2811891177640596371)
XLA Ops:
  0.7 1.7 %collective-permute-start = (f32[128,128]{1,0:T(8,128)}, f32[128,128]{1,0:T(8,128)S(1)}, u32[]{:S(2)}, u32[]{:S(2)}) collective-permute-start(f32[128,128]{1,0:T(8,128)} %param.12), channel_id=1, source_target_pairs={{0,2},{1,3},{2,0},{3,1},{4,6},{5,7},{6,4},{7,5},{8,10},{9,11},{10,... | collective-permute-start | bytes 196616 | tf_op jit(solution)/shard_map/ppermute | solution.py:182
  2.4 2.8 %fusion.refs_1_ = bf16[4096,128]{1,0:T(8,128)(2,1)} fusion(bf16[1,8192,128]{2,1,0:T(8,128)(2,1)} %param.9, bf16[1,8192,128]{2,1,0:T(8,128)(2,1)} %param.11), kind=kLoop, calls=%fused_computation.2 | loop fusion | flops 2097152 | bytes 3145728 | tf_op jit(solution)/shard_map/convert_element_type | solution.py:224
  5.5 2.1 %collective-permute-start.3 = (bf16[4096,128]{1,0:T(8,128)(2,1)S(1)}, bf16[4096,128]{1,0:T(8,128)(2,1)}, u32[]{:S(2)}, u32[]{:S(2)}) collective-permute-start(bf16[4096,128]{1,0:T(8,128)(2,1)S(1)} %slice_bitcast_fusion), channel_id=1, source_target_pairs={{0,4},{4,8},{8,12},{12,16},{16,20},{20,24},{24,28},{28,32},{32,36}... | collective-permute-start | bytes 3145736 | tf_op jit(solution)/shard_map/ppermute | solution.py:239
  7.5 8.1 %collective-permute-start.5 = (bf16[4096,128]{1,0:T(8,128)(2,1)}, bf16[4096,128]{1,0:T(8,128)(2,1)}, u32[]{:S(2)}, u32[]{:S(2)}) collective-permute-start(bf16[4096,128]{1,0:T(8,128)(2,1)} %fusion.refs_1_), channel_id=1, source_target_pairs={{4,0},{8,4},{12,8},{16,12},{20,16},{24,20},{28,24},{32,28},{36,32}... | collective-permute-start | bytes 3145736 | tf_op jit(solution)/shard_map/ppermute | solution.py:240
  15.6 1.0 %slice.25 = bf16[4096,128]{1,0:T(8,128)(2,1)} slice(bf16[8192,128]{1,0:T(8,128)(2,1)S(1)} %bitcast.24), slice={[4096:8192], [0:128]} | slice | bytes 2097152 | tf_op jit(solution)/shard_map/slice | solution.py:223
  16.7 1.3 %multiply_convert_fusion.refs_4_.refs_1_ = bf16[4096,128]{1,0:T(8,128)(2,1)} fusion(bf16[8192,128]{1,0:T(8,128)(2,1)S(1)} %bitcast.29, bf16[8192,128]{1,0:T(8,128)(2,1)S(1)} %bitcast.28), kind=kLoop, calls=%fused_computation | loop fusion | flops 2097152 | bytes 3145728 | tf_op jit(solution)/shard_map/convert_element_type | solution.py:224
  18.0 7.7 %collective-permute-start.4 = (bf16[4096,128]{1,0:T(8,128)(2,1)}, bf16[4096,128]{1,0:T(8,128)(2,1)}, u32[]{:S(2)}, u32[]{:S(2)}) collective-permute-start(bf16[4096,128]{1,0:T(8,128)(2,1)} %multiply_convert_fusion.refs_4_.refs_1_), channel_id=1, source_target_pairs={{4,0},{8,4},{12,8},{16,12},{20,16},{24,20},{28,24},{32,28},{36,32}... | collective-permute-start | bytes 3145736 | tf_op jit(solution)/shard_map/ppermute | solution.py:244
  25.7 2.1 %taps_spectra.1.refs_3_.refs_2_ = f32[512,256]{1,0:T(8,128)} custom-call(f32[2,128,128]{2,1,0:T(8,128)} %copy-done.3, f32[2,128,128]{2,1,0:T(8,128)} %copy-done.4, bf16[256,256]{1,0:T(8,128)(2,1)} %constant.60.clone.left.refs_6_), custom_call_target="tpu_custom_call" | custom-call | tf_op jit(solution)/shard_map/taps_spectra/pallas_call | solution.py:232
  27.8 10.8 %collective-permute-done.3.refs_0_ = bf16[4096,128]{1,0:T(8,128)(2,1)} collective-permute-done((bf16[4096,128]{1,0:T(8,128)(2,1)S(1)}, bf16[4096,128]{1,0:T(8,128)(2,1)}, u32[]{:S(2)}, u32[]{:S(2)}) %collective-permute-start.3) | collective-permute-done | bytes 1048608 | tf_op jit(solution)/shard_map/ppermute | solution.py:239
  38.6 7.1 %conv_taps_kernel.1 = (bf16[8192,128]{1,0:T(8,128)(2,1)}, f32[512,128]{1,0:T(8,128)}) custom-call(bf16[4096,128]{1,0:T(8,128)(2,1)} %collective-permute-done.3.refs_0_, bf16[8192,128]{1,0:T(8,128)(2,1)} %bitcast.20, bf16[8192,128]{1,0:T(8,128)(2,1)} %bitcast.25, f32[512,256]{1,0:T(8,128)} %taps_spectra.1.refs_3_.refs_2_, ...), custom_call_target="tpu_custom_call" | custom-call | tf_op jit(solution)/shard_map/conv_taps_kernel/pallas_call | solution.py:161
  45.6 6.9 %corr_taps_kernel.1 = (bf16[8192,128]{1,0:T(8,128)(2,1)}, f32[512,128]{1,0:T(8,128)}) custom-call(bf16[4096,128]{1,0:T(8,128)(2,1)} %collective-permute-done.5.refs_0_, bf16[4096,128]{1,0:T(8,128)(2,1)} %fusion.refs_1_, f32[512,256]{1,0:T(8,128)} %taps_spectra.1.refs_3_.refs_2_, bf16[8192,128]{1,0:T(8,128)(2,1)} %bitcast.21, ...), custom_call_target="tpu_custom_call", output_to_operand_aliasing={{1}: (7, {})} | custom-call | tf_op jit(solution)/shard_map/corr_taps_kernel/pallas_call | solution.py:161
  52.6 0.9 %dynamic-slice_bitcast_fusion = f32[2,128,128]{2,1,0:T(8,128)S(1)} fusion(f32[2,2,128,128]{3,2,1,0:T(8,128)} %bitcast.31, s32[]{:T(128)S(6)} %select_n.39), kind=kLoop, calls=%fused_computation.6 | loop fusion | bytes 262148 | tf_op jit(solution)/shard_map/jit(dynamic_index_in_dim)/squeeze | solution.py:190
  53.6 1.3 %collective-permute-done.6 = f32[2,128,128]{2,1,0:T(8,128)S(1)} collective-permute-done((f32[2,128,128]{2,1,0:T(8,128)S(1)}, f32[2,128,128]{2,1,0:T(8,128)S(1)}, u32[]{:S(2)}, u32[]{:S(2)}) %collective-permute-start.6) | collective-permute-done | bytes 131104 | tf_op jit(solution)/shard_map/ppermute | solution.py:182
  54.9 0.9 %bitcast_add_fusion = f32[2,128,128]{2,1,0:T(8,128)S(1)} fusion(f32[2,128,128]{2,1,0:T(8,128)S(1)} %collective-permute-done.6, f32[2,2,128,128]{3,2,1,0:T(8,128)} %bitcast.32, s32[]{:T(128)S(6)} %select_n.38), kind=kLoop, calls=%fused_computation.5 | loop fusion | flops 32768 | bytes 393220 | tf_op jit(solution)/shard_map/add | solution.py:195
  55.8 0.8 collective-permute-start.7
  57.1 3.5 %collective-permute-start.9 = (f32[128,128]{1,0:T(8,128)S(1)}, f32[128,128]{1,0:T(8,128)S(1)}, u32[]{:S(2)}, u32[]{:S(2)}) collective-permute-start(f32[128,128]{1,0:T(8,128)S(1)} %get-tuple-element.28), channel_id=1, source_target_pairs={{0,18},{1,19},{2,16},{3,17},{4,22},{5,23},{6,20},{7,21},{8,26},{9,... | collective-permute-start | bytes 196616 | tf_op jit(solution)/shard_map/ppermute | solution.py:182
  61.0 3.4 %conv_kernel.2.refs_6_ = bf16[8192,128]{1,0:T(8,128)(2,1)} custom-call(bf16[4096,128]{1,0:T(8,128)(2,1)} %collective-permute-done.2.refs_0_, bf16[8192,128]{1,0:T(8,128)(2,1)} %bitcast.22, bf16[8192,128]{1,0:T(8,128)(2,1)} %bitcast.26, f32[512,256]{1,0:T(8,128)} %taps_spectra.1.refs_3_.refs_2_, ...), custom_call_target="tpu_custom_call", output_to_operand_aliasing={{}: (6, {})} | custom-call | tf_op jit(solution)/shard_map/conv_kernel/pallas_call | solution.py:161
  64.5 0.7 collective-permute-start.10
  65.2 2.6 %collective-permute-start.11 = (f32[128,128]{1,0:T(8,128)S(1)}, f32[128,128]{1,0:T(8,128)S(1)}, u32[]{:S(2)}, u32[]{:S(2)}) collective-permute-start(f32[128,128]{1,0:T(8,128)S(1)} %add_add_fusion.1), channel_id=1, source_target_pairs={{0,96},{1,97},{2,98},{3,99},{4,100},{5,101},{6,102},{7,103},{8,104... | collective-permute-start | bytes 196616 | tf_op jit(solution)/shard_map/ppermute | solution.py:182
  67.8 1.0 %collective-permute-start.12 = (f32[128,128]{1,0:T(8,128)S(1)}, f32[128,128]{1,0:T(8,128)S(1)}, u32[]{:S(2)}, u32[]{:S(2)}) collective-permute-start(f32[128,128]{1,0:T(8,128)S(1)} %add_add_fusion.1), channel_id=1, source_target_pairs={{0,64},{1,65},{2,66},{3,67},{4,68},{5,69},{6,70},{7,71},{8,72},{9,... | collective-permute-start | bytes 196616 | tf_op jit(solution)/shard_map/ppermute | solution.py:182
  68.8 5.2 %corr_kernel.1 = bf16[8192,128]{1,0:T(8,128)(2,1)} custom-call(bf16[4096,128]{1,0:T(8,128)(2,1)} %collective-permute-done.4.refs_0_, bf16[4096,128]{1,0:T(8,128)(2,1)} %multiply_convert_fusion.refs_4_.refs_1_, f32[512,256]{1,0:T(8,128)} %taps_spectra.1.refs_3_.refs_2_, ...), custom_call_target="tpu_custom_call", output_to_operand_aliasing={{}: (5, {})} | custom-call | flops 5000000000 | bytes 50000000 | tf_op jit(solution)/shard_map/corr_kernel/pallas_call | solution.py:161
  74.1 3.2 %collective-permute-start.14 = (f32[128,128]{1,0:T(8,128)S(1)}, f32[128,128]{1,0:T(8,128)S(1)}, u32[]{:S(2)}, u32[]{:S(2)}) collective-permute-start(f32[128,128]{1,0:T(8,128)S(1)} %add_add_fusion), channel_id=1, source_target_pairs={{0,12},{1,13},{2,14},{3,15},{4,0},{5,1},{6,2},{7,3},{8,4},{9,5},{1... | collective-permute-start | bytes 196616 | tf_op jit(solution)/shard_map/ppermute | solution.py:182
  77.3 3.5 %conv_kernel.3 = bf16[8192,128]{1,0:T(8,128)(2,1)} custom-call(bf16[4096,128]{1,0:T(8,128)(2,1)} %collective-permute-done.2.refs_0_, bf16[8192,128]{1,0:T(8,128)(2,1)} %bitcast.23, bf16[8192,128]{1,0:T(8,128)(2,1)} %bitcast.27, f32[512,256]{1,0:T(8,128)} %taps_spectra.1.refs_3_.refs_2_, ...), custom_call_target="tpu_custom_call", output_to_operand_aliasing={{}: (6, {})} | custom-call | flops 5000000000 | bytes 50000000 | tf_op jit(solution)/shard_map/conv_kernel/pallas_call | solution.py:161
  80.8 2.3 %collective-permute-done.15 = f32[128,128]{1,0:T(8,128)S(1)} collective-permute-done((f32[128,128]{1,0:T(8,128)S(1)}, f32[128,128]{1,0:T(8,128)S(1)}, u32[]{:S(2)}, u32[]{:S(2)}) %collective-permute-start.15) | collective-permute-done | bytes 65568 | tf_op jit(solution)/shard_map/ppermute | solution.py:182
  (37 shorter events, 2.0 us)
Async XLA Ops:
  0.6 4.6 %copy-start.5 = (f32[128,128]{1,0:T(8,128)S(1)}, f32[128,128]{1,0:T(8,128)}, u32[]{:S(2)}) copy-start(f32[128,128]{1,0:T(8,128)} %param.12) | copy-start | bytes 196612
  0.6 4.7 %copy-start = (bf16[1,8192,128]{2,1,0:T(8,128)(2,1)S(1)}, bf16[1,8192,128]{2,1,0:T(8,128)(2,1)}, u32[]{:S(2)}) copy-start(bf16[1,8192,128]{2,1,0:T(8,128)(2,1)} %param.10) | copy-start | bytes 6291460
  0.7 4.6 %collective-permute-start = (f32[128,128]{1,0:T(8,128)}, f32[128,128]{1,0:T(8,128)S(1)}, u32[]{:S(2)}, u32[]{:S(2)}) collective-permute-start(f32[128,128]{1,0:T(8,128)} %param.12), channel_id=1, source_target_pairs={{0,2},{1,3},{2,0},{3,1},{4,6},{5,7},{6,4},{7,5},{8,10},{9,11},{10,... | collective-permute-start | bytes 196616 | tf_op jit(solution)/shard_map/ppermute | solution.py:182
  5.2 11.4 %copy-start.3 = (f32[2,128,128]{2,1,0:T(8,128)}, f32[2,128,128]{2,1,0:T(8,128)S(1)}, u32[]{:S(2)}) copy-start(f32[2,128,128]{2,1,0:T(8,128)S(1)} %maximum_select_fusion.column) | copy-start | bytes 393220
  5.2 11.4 %copy-start.1 = (bf16[1,8192,128]{2,1,0:T(8,128)(2,1)S(1)}, bf16[1,8192,128]{2,1,0:T(8,128)(2,1)}, u32[]{:S(2)}) copy-start(bf16[1,8192,128]{2,1,0:T(8,128)(2,1)} %param.11) | copy-start | bytes 6291460
  5.3 11.4 %copy-start.2 = (bf16[1,8192,128]{2,1,0:T(8,128)(2,1)S(1)}, bf16[1,8192,128]{2,1,0:T(8,128)(2,1)}, u32[]{:S(2)}) copy-start(bf16[1,8192,128]{2,1,0:T(8,128)(2,1)} %param.9) | copy-start | bytes 6291460
  5.3 2.2 %collective-permute-start.1 = (f32[2,128,128]{2,1,0:T(8,128)S(1)}, f32[2,128,128]{2,1,0:T(8,128)S(1)}, u32[]{:S(2)}, u32[]{:S(2)}) collective-permute-start(f32[2,128,128]{2,1,0:T(8,128)S(1)} %maximum_select_fusion.column), channel_id=1, source_target_pairs={{0,1},{1,0},{2,3},{3,2},{4,5},{5,4},{6,7},{7,6},{8,9},{9,8},{10,11... | collective-permute-start | bytes 393224 | tf_op jit(solution)/shard_map/ppermute | solution.py:182
  5.5 33.1 %collective-permute-start.3 = (bf16[4096,128]{1,0:T(8,128)(2,1)S(1)}, bf16[4096,128]{1,0:T(8,128)(2,1)}, u32[]{:S(2)}, u32[]{:S(2)}) collective-permute-start(bf16[4096,128]{1,0:T(8,128)(2,1)S(1)} %slice_bitcast_fusion), channel_id=1, source_target_pairs={{0,4},{4,8},{8,12},{12,16},{16,20},{20,24},{24,28},{28,32},{32,36}... | collective-permute-start | bytes 3145736 | tf_op jit(solution)/shard_map/ppermute | solution.py:239
  7.5 10.5 %copy-start.4 = (f32[2,128,128]{2,1,0:T(8,128)}, f32[2,128,128]{2,1,0:T(8,128)S(1)}, u32[]{:S(2)}) copy-start(f32[2,128,128]{2,1,0:T(8,128)S(1)} %collective-permute-done.1.near) | copy-start | bytes 393220
  7.5 38.1 %collective-permute-start.5 = (bf16[4096,128]{1,0:T(8,128)(2,1)}, bf16[4096,128]{1,0:T(8,128)(2,1)}, u32[]{:S(2)}, u32[]{:S(2)}) collective-permute-start(bf16[4096,128]{1,0:T(8,128)(2,1)} %fusion.refs_1_), channel_id=1, source_target_pairs={{4,0},{8,4},{12,8},{16,12},{20,16},{24,20},{28,24},{32,28},{36,32}... | collective-permute-start | bytes 3145736 | tf_op jit(solution)/shard_map/ppermute | solution.py:240
  16.7 44.3 %collective-permute-start.2 = (bf16[4096,128]{1,0:T(8,128)(2,1)}, bf16[4096,128]{1,0:T(8,128)(2,1)}, u32[]{:S(2)}, u32[]{:S(2)}) collective-permute-start(bf16[4096,128]{1,0:T(8,128)(2,1)} %slice.25), channel_id=1, source_target_pairs={{0,4},{4,8},{8,12},{12,16},{16,20},{20,24},{24,28},{28,32},{32,36}... | collective-permute-start | bytes 3145736 | tf_op jit(solution)/shard_map/ppermute | solution.py:243
  18.0 46.5 %collective-permute-start.4 = (bf16[4096,128]{1,0:T(8,128)(2,1)}, bf16[4096,128]{1,0:T(8,128)(2,1)}, u32[]{:S(2)}, u32[]{:S(2)}) collective-permute-start(bf16[4096,128]{1,0:T(8,128)(2,1)} %multiply_convert_fusion.refs_4_.refs_1_), channel_id=1, source_target_pairs={{4,0},{8,4},{12,8},{16,12},{20,16},{24,20},{28,24},{32,28},{36,32}... | collective-permute-start | bytes 3145736 | tf_op jit(solution)/shard_map/ppermute | solution.py:244
  53.5 1.4 %collective-permute-start.6 = (f32[2,128,128]{2,1,0:T(8,128)S(1)}, f32[2,128,128]{2,1,0:T(8,128)S(1)}, u32[]{:S(2)}, u32[]{:S(2)}) collective-permute-start(f32[2,128,128]{2,1,0:T(8,128)S(1)} %dynamic-slice_bitcast_fusion), channel_id=1, source_target_pairs={{0,1},{1,0},{2,3},{3,2},{4,5},{5,4},{6,7},{7,6},{8,9},{9,8},{10,11... | collective-permute-start | bytes 393224 | tf_op jit(solution)/shard_map/ppermute | solution.py:182
  55.8 8.6 %collective-permute-start.7 = (f32[128,128]{1,0:T(8,128)S(1)}, f32[128,128]{1,0:T(8,128)S(1)}, u32[]{:S(2)}, u32[]{:S(2)}) collective-permute-start(f32[128,128]{1,0:T(8,128)S(1)} %get-tuple-element.28), channel_id=1, source_target_pairs={{0,2},{1,3},{2,0},{3,1},{4,6},{5,7},{6,4},{7,5},{8,10},{9,11},{10,... | collective-permute-start | bytes 196616 | tf_op jit(solution)/shard_map/ppermute | solution.py:182
  56.6 7.8 %collective-permute-start.8 = (f32[128,128]{1,0:T(8,128)S(1)}, f32[128,128]{1,0:T(8,128)S(1)}, u32[]{:S(2)}, u32[]{:S(2)}) collective-permute-start(f32[128,128]{1,0:T(8,128)S(1)} %get-tuple-element.27), channel_id=1, source_target_pairs={{0,16},{1,17},{2,18},{3,19},{4,20},{5,21},{6,22},{7,23},{8,24},{9,... | collective-permute-start | bytes 196616 | tf_op jit(solution)/shard_map/ppermute | solution.py:182
  57.1 7.4 %collective-permute-start.9 = (f32[128,128]{1,0:T(8,128)S(1)}, f32[128,128]{1,0:T(8,128)S(1)}, u32[]{:S(2)}, u32[]{:S(2)}) collective-permute-start(f32[128,128]{1,0:T(8,128)S(1)} %get-tuple-element.28), channel_id=1, source_target_pairs={{0,18},{1,19},{2,16},{3,17},{4,22},{5,23},{6,20},{7,21},{8,26},{9,... | collective-permute-start | bytes 196616 | tf_op jit(solution)/shard_map/ppermute | solution.py:182
  64.5 9.5 %collective-permute-start.10 = (f32[128,128]{1,0:T(8,128)S(1)}, f32[128,128]{1,0:T(8,128)S(1)}, u32[]{:S(2)}, u32[]{:S(2)}) collective-permute-start(f32[128,128]{1,0:T(8,128)S(1)} %add_add_fusion.1), channel_id=1, source_target_pairs={{0,32},{1,33},{2,34},{3,35},{4,36},{5,37},{6,38},{7,39},{8,40},{9,... | collective-permute-start | bytes 196616 | tf_op jit(solution)/shard_map/ppermute | solution.py:182
  65.2 8.8 %collective-permute-start.11 = (f32[128,128]{1,0:T(8,128)S(1)}, f32[128,128]{1,0:T(8,128)S(1)}, u32[]{:S(2)}, u32[]{:S(2)}) collective-permute-start(f32[128,128]{1,0:T(8,128)S(1)} %add_add_fusion.1), channel_id=1, source_target_pairs={{0,96},{1,97},{2,98},{3,99},{4,100},{5,101},{6,102},{7,103},{8,104... | collective-permute-start | bytes 196616 | tf_op jit(solution)/shard_map/ppermute | solution.py:182
  67.8 6.2 %collective-permute-start.12 = (f32[128,128]{1,0:T(8,128)S(1)}, f32[128,128]{1,0:T(8,128)S(1)}, u32[]{:S(2)}, u32[]{:S(2)}) collective-permute-start(f32[128,128]{1,0:T(8,128)S(1)} %add_add_fusion.1), channel_id=1, source_target_pairs={{0,64},{1,65},{2,66},{3,67},{4,68},{5,69},{6,70},{7,71},{8,72},{9,... | collective-permute-start | bytes 196616 | tf_op jit(solution)/shard_map/ppermute | solution.py:182
  74.0 6.8 %collective-permute-start.13 = (f32[128,128]{1,0:T(8,128)S(1)}, f32[128,128]{1,0:T(8,128)S(1)}, u32[]{:S(2)}, u32[]{:S(2)}) collective-permute-start(f32[128,128]{1,0:T(8,128)S(1)} %add_add_fusion), channel_id=1, source_target_pairs={{0,4},{1,5},{2,6},{3,7},{4,8},{5,9},{6,10},{7,11},{8,12},{9,13},{1... | collective-permute-start | bytes 196616 | tf_op jit(solution)/shard_map/ppermute | solution.py:182
  74.1 6.7 %collective-permute-start.14 = (f32[128,128]{1,0:T(8,128)S(1)}, f32[128,128]{1,0:T(8,128)S(1)}, u32[]{:S(2)}, u32[]{:S(2)}) collective-permute-start(f32[128,128]{1,0:T(8,128)S(1)} %add_add_fusion), channel_id=1, source_target_pairs={{0,12},{1,13},{2,14},{3,15},{4,0},{5,1},{6,2},{7,3},{8,4},{9,5},{1... | collective-permute-start | bytes 196616 | tf_op jit(solution)/shard_map/ppermute | solution.py:182
  77.3 5.8 %collective-permute-start.15 = (f32[128,128]{1,0:T(8,128)S(1)}, f32[128,128]{1,0:T(8,128)S(1)}, u32[]{:S(2)}, u32[]{:S(2)}) collective-permute-start(f32[128,128]{1,0:T(8,128)S(1)} %add_add_fusion), channel_id=1, source_target_pairs={{0,8},{1,9},{2,10},{3,11},{4,12},{5,13},{6,14},{7,15},{8,0},{9,1},... | collective-permute-start | bytes 196616 | tf_op jit(solution)/shard_map/ppermute | solution.py:182

commit v5 on v4

--- a/solution.py
+++ b/solution.py
@@ -12,7 +12,7 @@
 FLEN = 128
 GROUP_CH = 16
 WIN = 2 * FLEN
-BLOCK = 1024
+BLOCK = 2048
 VMEM_MB = 63
 F32, BF16 = jnp.float32, jnp.bfloat16
 
@@ -228,14 +228,14 @@
     fsdp = lax.axis_index("fsdp")
     far = exchange(filters, lambda c, f: (c, f ^ 2))
     column = jnp.where(fsdp // 2 == 0, jnp.stack([filters, far]), jnp.stack([far, filters]))
+    core_b = product(grad_out, query, half, half)
+    sent_b, column = lax.optimization_barrier((core_b, column))
     near = exchange(column, lambda c, f: (c, f ^ 1))
     h = pl.pallas_call(
         taps_kernel, out_shape=jax.ShapeDtypeStruct((width // GROUP_CH, WIN), F32), name="taps_spectra"
     )(column, near, left)
 
     sent_a, _ = lax.optimization_barrier((rows(gated, 0, half), far))
-    core_b = product(grad_out, query, half, half)
-    sent_b, _ = lax.optimization_barrier((core_b, near))
     prev_a = lax.ppermute(sent_a, "ctx", up)
     nxt_b = lax.ppermute(sent_b, "ctx", down)
     late = lax.optimization_barrier((gated, grad_out, query, core_b, near))[:3]
@@ -260,20 +260,16 @@
         half,
     )
     partial = reduce_first(partial.reshape(2, 2, -1, FLEN))
-    def conv(gq, start, size, cost):
-        return run(
-            conv_kernel,
-            [(prev_b, at(start)), (gated, at(half + start)), (grad_out, at(half + start)), (h, h_at(half + start))],
-            (fwd2, inv_b),
-            [(gq, half + start, BLOCK)],
-            size,
-            cost,
-        )[0]
-
-    gq = conv(gq, 0, half // 2, 0)
-    gq, nxt_a, partial = lax.optimization_barrier((gq, nxt_a, partial))
+    prev_b, nxt_a, partial = lax.optimization_barrier((prev_b, nxt_a, partial))
     summed = reduce_rest(partial)
-    gq = conv(gq, half // 2, half // 2, 5)
+    gq, = run(
+        conv_kernel,
+        [(prev_b, at(0)), (gated, at(half)), (grad_out, at(half)), (h, h_at(half))],
+        (fwd2, inv_b),
+        [(gq, half, BLOCK)],
+        half,
+        5,
+    )
     gg, = run(
         corr_kernel,
         [(nxt_a, at(0)), (core_a, at(0)), (h, h_at(0))],

time: 84.3 us -> 82.9 us (0.983)
  waiting for transfers between devices: 14.8 us -> 22.4 us
  starting transfers between devices: 32.2 us -> 26 us
  Pallas kernels: 28.1 us -> 24.4 us
  other arithmetic: 5.7 us -> 6.93 us
    ppermute x1, starting transfers between devices: 7.74 us -> 1.94 us  [per_device(): nxt_a = lax.ppermute(core_a, 'ctx', down)]
    ppermute x1, waiting for transfers between devices: 10.8 us -> 16.3 us  [per_device(): prev_a = lax.ppermute(sent_a, 'ctx', up)]
    pallas_call x5 -> x4, Pallas kernels: 26.1 us -> 22.4 us  [run(): pl.pallas_call(body, out_shape=[jax.ShapeDtypeStruct(out.shape, out.dtype...]
    ppermute x12, waiting for transfers between devices: 3.64 us -> 6.08 us  [exchange(): return lax.ppermute(x, ('ctx', 'fsdp'), pairs)]
    convert_element_type x2, other arithmetic: 4.09 us -> 5.32 us  [per_device(): (rows(o, start, size).astype(F32) * rows(q, start, size).astype(F32)).ast...]
    ppermute x1, starting transfers between devices: 8.12 us -> 7.03 us  [per_device(): nxt_b = lax.ppermute(sent_b, 'ctx', down)]
  transfers between devices with their start and end apart: 16 -> 16, of which waited for: 4 -> 6; matrix products, arithmetic and copies ran while one was open for 8% -> 10% of each run, Pallas kernels for 34% -> 30%
where the time goes in v5:
time: 82.9 us; the launch traced here: 82.6 us
  starting transfers between devices  26 us (31%)
  Pallas kernels  24.4 us (29%)
  waiting for transfers between devices  22.4 us (27%)
  other arithmetic  6.93 us (8%)
  local copies, waits for them, and re-layouts  2.08 us (3%)
    pallas_call x4, Pallas kernels, run(): pl.pallas_call(body, out_shape=[jax.ShapeDtypeStruct(out.shape, out.dtype...  22.4 us
    ppermute x1, waiting for transfers between devices, per_device(): prev_a = lax.ppermute(sent_a, 'ctx', up)  16.3 us
    ppermute x12, starting transfers between devices, exchange(): return lax.ppermute(x, ('ctx', 'fsdp'), pairs)  14.8 us
    ppermute x1, starting transfers between devices, per_device(): nxt_b = lax.ppermute(sent_b, 'ctx', down)  7.03 us
    ppermute x12, waiting for transfers between devices, exchange(): return lax.ppermute(x, ('ctx', 'fsdp'), pairs)  6.08 us
    convert_element_type x2, other arithmetic, per_device(): (rows(o, start, size).astype(F32) * rows(q, start, size).astype(F32)).ast...  5.32 us
    ppermute x1, starting transfers between devices, per_device(): prev_a = lax.ppermute(sent_a, 'ctx', up)  2.07 us
    pallas_call x1, Pallas kernels, per_device(): pl.pallas_call(taps_kernel, out_shape=jax.ShapeDtypeStruct((width // GROU...  2.05 us
  transfers between devices with their start and end apart: 16, of which 6 were waited for; matrix products, arithmetic and copies ran while one was open for 10% of the time, Pallas kernels for 30%

profile of v5, /device:TPU:0, one launch (start us, length us, event | category | flops | bytes accessed | tf_op | source)
XLA Modules:
  0.0 82.6 jit_solution(6982356016453227451)
XLA Ops:
  0.7 1.7 %collective-permute-start = (f32[128,128]{1,0:T(8,128)}, f32[128,128]{1,0:T(8,128)S(1)}, u32[]{:S(2)}, u32[]{:S(2)}) collective-permute-start(f32[128,128]{1,0:T(8,128)} %param.12), channel_id=1, source_target_pairs={{0,2},{1,3},{2,0},{3,1},{4,6},{5,7},{6,4},{7,5},{8,10},{9,11},{10,... | collective-permute-start | bytes 196616 | tf_op jit(solution)/shard_map/ppermute | solution.py:182
  2.4 2.8 %fusion.refs_1_ = bf16[4096,128]{1,0:T(8,128)(2,1)} fusion(bf16[1,8192,128]{2,1,0:T(8,128)(2,1)} %param.9, bf16[1,8192,128]{2,1,0:T(8,128)(2,1)} %param.11), kind=kLoop, calls=%fused_computation.2 | loop fusion | flops 2097152 | bytes 3145728 | tf_op jit(solution)/shard_map/convert_element_type | solution.py:224
  5.4 2.1 %collective-permute-start.5 = (bf16[4096,128]{1,0:T(8,128)(2,1)S(1)}, bf16[4096,128]{1,0:T(8,128)(2,1)}, u32[]{:S(2)}, u32[]{:S(2)}) collective-permute-start(bf16[4096,128]{1,0:T(8,128)(2,1)S(1)} %slice_bitcast_fusion), channel_id=1, source_target_pairs={{0,4},{4,8},{8,12},{12,16},{16,20},{20,24},{24,28},{28,32},{32,36}... | collective-permute-start | bytes 3145736 | tf_op jit(solution)/shard_map/ppermute | solution.py:239
  7.5 7.0 %collective-permute-start.4 = (bf16[4096,128]{1,0:T(8,128)(2,1)}, bf16[4096,128]{1,0:T(8,128)(2,1)}, u32[]{:S(2)}, u32[]{:S(2)}) collective-permute-start(bf16[4096,128]{1,0:T(8,128)(2,1)} %fusion.refs_1_), channel_id=1, source_target_pairs={{4,0},{8,4},{12,8},{16,12},{20,16},{24,20},{28,24},{32,28},{36,32}... | collective-permute-start | bytes 3145736 | tf_op jit(solution)/shard_map/ppermute | solution.py:240
  14.5 2.5 %multiply_convert_fusion.refs_4_.refs_1_ = bf16[4096,128]{1,0:T(8,128)(2,1)} fusion(bf16[8192,128]{1,0:T(8,128)(2,1)} %bitcast.27, bf16[8192,128]{1,0:T(8,128)(2,1)S(1)} %bitcast.26), kind=kLoop, calls=%fused_computation | loop fusion | flops 2097152 | bytes 3145728 | tf_op jit(solution)/shard_map/convert_element_type | solution.py:224
  17.1 1.9 %collective-permute-start.3 = (bf16[4096,128]{1,0:T(8,128)(2,1)}, bf16[4096,128]{1,0:T(8,128)(2,1)}, u32[]{:S(2)}, u32[]{:S(2)}) collective-permute-start(bf16[4096,128]{1,0:T(8,128)(2,1)} %multiply_convert_fusion.refs_4_.refs_1_), channel_id=1, source_target_pairs={{4,0},{8,4},{12,8},{16,12},{20,16},{24,20},{28,24},{32,28},{36,32}... | collective-permute-start | bytes 3145736 | tf_op jit(solution)/shard_map/ppermute | solution.py:244
  19.0 1.1 %slice.25 = bf16[4096,128]{1,0:T(8,128)(2,1)} slice(bf16[8192,128]{1,0:T(8,128)(2,1)S(1)} %bitcast.23), slice={[4096:8192], [0:128]} | slice | bytes 2097152 | tf_op jit(solution)/shard_map/slice | solution.py:223
  20.2 2.1 %taps_spectra.1.refs_3_.refs_2_ = f32[512,256]{1,0:T(8,128)} custom-call(f32[2,128,128]{2,1,0:T(8,128)} %copy-done.2, f32[2,128,128]{2,1,0:T(8,128)} %copy-done.3, bf16[256,256]{1,0:T(8,128)(2,1)} %constant.60.clone.left.refs_6_), custom_call_target="tpu_custom_call" | custom-call | tf_op jit(solution)/shard_map/taps_spectra/pallas_call | solution.py:234
  22.2 16.3 %collective-permute-done.5.refs_0_ = bf16[4096,128]{1,0:T(8,128)(2,1)} collective-permute-done((bf16[4096,128]{1,0:T(8,128)(2,1)S(1)}, bf16[4096,128]{1,0:T(8,128)(2,1)}, u32[]{:S(2)}, u32[]{:S(2)}) %collective-permute-start.5) | collective-permute-done | bytes 1048608 | tf_op jit(solution)/shard_map/ppermute | solution.py:239
  38.6 6.7 %conv_taps_kernel.1 = (bf16[8192,128]{1,0:T(8,128)(2,1)}, f32[512,128]{1,0:T(8,128)}) custom-call(bf16[4096,128]{1,0:T(8,128)(2,1)} %collective-permute-done.5.refs_0_, bf16[8192,128]{1,0:T(8,128)(2,1)} %bitcast.20, bf16[8192,128]{1,0:T(8,128)(2,1)} %bitcast.24, f32[512,256]{1,0:T(8,128)} %taps_spectra.1.refs_3_.refs_2_, ...), custom_call_target="tpu_custom_call" | custom-call | tf_op jit(solution)/shard_map/conv_taps_kernel/pallas_call | solution.py:161
  45.2 6.4 %corr_taps_kernel.1 = (bf16[8192,128]{1,0:T(8,128)(2,1)}, f32[512,128]{1,0:T(8,128)}) custom-call(bf16[4096,128]{1,0:T(8,128)(2,1)} %collective-permute-done.4.refs_0_, bf16[4096,128]{1,0:T(8,128)(2,1)} %fusion.refs_1_, f32[512,256]{1,0:T(8,128)} %taps_spectra.1.refs_3_.refs_2_, bf16[8192,128]{1,0:T(8,128)(2,1)} %bitcast.21, ...), custom_call_target="tpu_custom_call", output_to_operand_aliasing={{1}: (7, {})} | custom-call | tf_op jit(solution)/shard_map/corr_taps_kernel/pallas_call | solution.py:161
  51.7 0.9 %dynamic-slice_bitcast_fusion = f32[2,128,128]{2,1,0:T(8,128)S(1)} fusion(f32[2,2,128,128]{3,2,1,0:T(8,128)} %bitcast.28, s32[]{:T(128)S(6)} %select_n.39), kind=kLoop, calls=%fused_computation.6 | loop fusion | bytes 262148 | tf_op jit(solution)/shard_map/jit(dynamic_index_in_dim)/squeeze | solution.py:190
  52.7 1.3 %collective-permute-done.6 = f32[2,128,128]{2,1,0:T(8,128)S(1)} collective-permute-done((f32[2,128,128]{2,1,0:T(8,128)S(1)}, f32[2,128,128]{2,1,0:T(8,128)S(1)}, u32[]{:S(2)}, u32[]{:S(2)}) %collective-permute-start.6) | collective-permute-done | bytes 131104 | tf_op jit(solution)/shard_map/ppermute | solution.py:182
  54.0 0.9 %bitcast_add_fusion = f32[2,128,128]{2,1,0:T(8,128)S(1)} fusion(f32[2,128,128]{2,1,0:T(8,128)S(1)} %collective-permute-done.6, f32[2,2,128,128]{3,2,1,0:T(8,128)} %bitcast.29, s32[]{:T(128)S(6)} %select_n.38), kind=kLoop, calls=%fused_computation.5 | loop fusion | flops 32768 | bytes 393220 | tf_op jit(solution)/shard_map/add | solution.py:195
  56.2 3.5 %collective-permute-start.9 = (f32[128,128]{1,0:T(8,128)S(1)}, f32[128,128]{1,0:T(8,128)S(1)}, u32[]{:S(2)}, u32[]{:S(2)}) collective-permute-start(f32[128,128]{1,0:T(8,128)S(1)} %get-tuple-element.30), channel_id=1, source_target_pairs={{0,18},{1,19},{2,16},{3,17},{4,22},{5,23},{6,20},{7,21},{8,26},{9,... | collective-permute-start | bytes 196616 | tf_op jit(solution)/shard_map/ppermute | solution.py:182
  59.7 2.3 %collective-permute-done.7 = f32[128,128]{1,0:T(8,128)S(1)} collective-permute-done((f32[128,128]{1,0:T(8,128)S(1)}, f32[128,128]{1,0:T(8,128)S(1)}, u32[]{:S(2)}, u32[]{:S(2)}) %collective-permute-start.7) | collective-permute-done | bytes 65568 | tf_op jit(solution)/shard_map/ppermute | solution.py:182
  62.0 1.2 %collective-permute-done.8 = f32[128,128]{1,0:T(8,128)S(1)} collective-permute-done((f32[128,128]{1,0:T(8,128)S(1)}, f32[128,128]{1,0:T(8,128)S(1)}, u32[]{:S(2)}, u32[]{:S(2)}) %collective-permute-start.8) | collective-permute-done | bytes 65568 | tf_op jit(solution)/shard_map/ppermute | solution.py:182
  63.5 1.3 %collective-permute-start.10 = (f32[128,128]{1,0:T(8,128)S(1)}, f32[128,128]{1,0:T(8,128)S(1)}, u32[]{:S(2)}, u32[]{:S(2)}) collective-permute-start(f32[128,128]{1,0:T(8,128)S(1)} %add_add_fusion.1), channel_id=1, source_target_pairs={{0,32},{1,33},{2,34},{3,35},{4,36},{5,37},{6,38},{7,39},{8,40},{9,... | collective-permute-start | bytes 196616 | tf_op jit(solution)/shard_map/ppermute | solution.py:182
  64.7 2.0 %collective-permute-start.11 = (f32[128,128]{1,0:T(8,128)S(1)}, f32[128,128]{1,0:T(8,128)S(1)}, u32[]{:S(2)}, u32[]{:S(2)}) collective-permute-start(f32[128,128]{1,0:T(8,128)S(1)} %add_add_fusion.1), channel_id=1, source_target_pairs={{0,96},{1,97},{2,98},{3,99},{4,100},{5,101},{6,102},{7,103},{8,104... | collective-permute-start | bytes 196616 | tf_op jit(solution)/shard_map/ppermute | solution.py:182
  66.8 1.5 %collective-permute-start.12 = (f32[128,128]{1,0:T(8,128)S(1)}, f32[128,128]{1,0:T(8,128)S(1)}, u32[]{:S(2)}, u32[]{:S(2)}) collective-permute-start(f32[128,128]{1,0:T(8,128)S(1)} %add_add_fusion.1), channel_id=1, source_target_pairs={{0,64},{1,65},{2,66},{3,67},{4,68},{5,69},{6,70},{7,71},{8,72},{9,... | collective-permute-start | bytes 196616 | tf_op jit(solution)/shard_map/ppermute | solution.py:182
  68.3 4.5 %corr_kernel.1 = bf16[8192,128]{1,0:T(8,128)(2,1)} custom-call(bf16[4096,128]{1,0:T(8,128)(2,1)} %collective-permute-done.3.refs_0_, bf16[4096,128]{1,0:T(8,128)(2,1)} %multiply_convert_fusion.refs_4_.refs_1_, f32[512,256]{1,0:T(8,128)} %taps_spectra.1.refs_3_.refs_2_, ...), custom_call_target="tpu_custom_call", output_to_operand_aliasing={{}: (5, {})} | custom-call | flops 5000000000 | bytes 50000000 | tf_op jit(solution)/shard_map/corr_kernel/pallas_call | solution.py:161
  73.0 3.2 %collective-permute-start.14 = (f32[128,128]{1,0:T(8,128)S(1)}, f32[128,128]{1,0:T(8,128)S(1)}, u32[]{:S(2)}, u32[]{:S(2)}) collective-permute-start(f32[128,128]{1,0:T(8,128)S(1)} %add_add_fusion), channel_id=1, source_target_pairs={{0,12},{1,13},{2,14},{3,15},{4,0},{5,1},{6,2},{7,3},{8,4},{9,5},{1... | collective-permute-start | bytes 196616 | tf_op jit(solution)/shard_map/ppermute | solution.py:182
  76.2 4.7 %conv_kernel.1 = bf16[8192,128]{1,0:T(8,128)(2,1)} custom-call(bf16[4096,128]{1,0:T(8,128)(2,1)} %collective-permute-done.2.refs_0_, bf16[8192,128]{1,0:T(8,128)(2,1)} %bitcast.22, bf16[8192,128]{1,0:T(8,128)(2,1)} %bitcast.25, f32[512,256]{1,0:T(8,128)} %taps_spectra.1.refs_3_.refs_2_, ...), custom_call_target="tpu_custom_call", output_to_operand_aliasing={{}: (6, {})} | custom-call | flops 5000000000 | bytes 50000000 | tf_op jit(solution)/shard_map/conv_kernel/pallas_call | solution.py:161
  80.9 1.0 %collective-permute-done.15 = f32[128,128]{1,0:T(8,128)S(1)} collective-permute-done((f32[128,128]{1,0:T(8,128)S(1)}, f32[128,128]{1,0:T(8,128)S(1)}, u32[]{:S(2)}, u32[]{:S(2)}) %collective-permute-start.15) | collective-permute-done | bytes 65568 | tf_op jit(solution)/shard_map/ppermute | solution.py:182
  (34 shorter events, 2.7 us)
Async XLA Ops:
  0.6 4.6 %copy-start.4 = (f32[128,128]{1,0:T(8,128)S(1)}, f32[128,128]{1,0:T(8,128)}, u32[]{:S(2)}) copy-start(f32[128,128]{1,0:T(8,128)} %param.12) | copy-start | bytes 196612
  0.6 4.7 %copy-start = (bf16[1,8192,128]{2,1,0:T(8,128)(2,1)S(1)}, bf16[1,8192,128]{2,1,0:T(8,128)(2,1)}, u32[]{:S(2)}) copy-start(bf16[1,8192,128]{2,1,0:T(8,128)(2,1)} %param.10) | copy-start | bytes 6291460
  0.7 4.6 %collective-permute-start = (f32[128,128]{1,0:T(8,128)}, f32[128,128]{1,0:T(8,128)S(1)}, u32[]{:S(2)}, u32[]{:S(2)}) collective-permute-start(f32[128,128]{1,0:T(8,128)} %param.12), channel_id=1, source_target_pairs={{0,2},{1,3},{2,0},{3,1},{4,6},{5,7},{6,4},{7,5},{8,10},{9,11},{10,... | collective-permute-start | bytes 196616 | tf_op jit(solution)/shard_map/ppermute | solution.py:182
  5.2 9.4 %copy-start.1 = (bf16[1,8192,128]{2,1,0:T(8,128)(2,1)S(1)}, bf16[1,8192,128]{2,1,0:T(8,128)(2,1)}, u32[]{:S(2)}) copy-start(bf16[1,8192,128]{2,1,0:T(8,128)(2,1)} %param.11) | copy-start | bytes 6291460
  5.2 11.8 %copy-start.2 = (f32[2,128,128]{2,1,0:T(8,128)}, f32[2,128,128]{2,1,0:T(8,128)S(1)}, u32[]{:S(2)}) copy-start(f32[2,128,128]{2,1,0:T(8,128)S(1)} %maximum_select_fusion.column) | copy-start | bytes 393220
  5.2 9.3 %collective-permute-start.1 = (f32[2,128,128]{2,1,0:T(8,128)S(1)}, f32[2,128,128]{2,1,0:T(8,128)S(1)}, u32[]{:S(2)}, u32[]{:S(2)}) collective-permute-start(f32[2,128,128]{2,1,0:T(8,128)S(1)} %maximum_select_fusion.column), channel_id=1, source_target_pairs={{0,1},{1,0},{2,3},{3,2},{4,5},{5,4},{6,7},{7,6},{8,9},{9,8},{10,11... | collective-permute-start | bytes 393224 | tf_op jit(solution)/shard_map/ppermute | solution.py:182
  5.4 33.1 %collective-permute-start.5 = (bf16[4096,128]{1,0:T(8,128)(2,1)S(1)}, bf16[4096,128]{1,0:T(8,128)(2,1)}, u32[]{:S(2)}, u32[]{:S(2)}) collective-permute-start(bf16[4096,128]{1,0:T(8,128)(2,1)S(1)} %slice_bitcast_fusion), channel_id=1, source_target_pairs={{0,4},{4,8},{8,12},{12,16},{16,20},{20,24},{24,28},{28,32},{32,36}... | collective-permute-start | bytes 3145736 | tf_op jit(solution)/shard_map/ppermute | solution.py:239
  7.5 37.7 %collective-permute-start.4 = (bf16[4096,128]{1,0:T(8,128)(2,1)}, bf16[4096,128]{1,0:T(8,128)(2,1)}, u32[]{:S(2)}, u32[]{:S(2)}) collective-permute-start(bf16[4096,128]{1,0:T(8,128)(2,1)} %fusion.refs_1_), channel_id=1, source_target_pairs={{4,0},{8,4},{12,8},{16,12},{20,16},{24,20},{28,24},{32,28},{36,32}... | collective-permute-start | bytes 3145736 | tf_op jit(solution)/shard_map/ppermute | solution.py:240
  14.5 5.5 %copy-start.3 = (f32[2,128,128]{2,1,0:T(8,128)}, f32[2,128,128]{2,1,0:T(8,128)S(1)}, u32[]{:S(2)}) copy-start(f32[2,128,128]{2,1,0:T(8,128)S(1)} %collective-permute-done.1.near) | copy-start | bytes 393220
  17.1 46.4 %collective-permute-start.3 = (bf16[4096,128]{1,0:T(8,128)(2,1)}, bf16[4096,128]{1,0:T(8,128)(2,1)}, u32[]{:S(2)}, u32[]{:S(2)}) collective-permute-start(bf16[4096,128]{1,0:T(8,128)(2,1)} %multiply_convert_fusion.refs_4_.refs_1_), channel_id=1, source_target_pairs={{4,0},{8,4},{12,8},{16,12},{20,16},{24,20},{28,24},{32,28},{36,32}... | collective-permute-start | bytes 3145736 | tf_op jit(solution)/shard_map/ppermute | solution.py:244
  20.1 43.4 %collective-permute-start.2 = (bf16[4096,128]{1,0:T(8,128)(2,1)}, bf16[4096,128]{1,0:T(8,128)(2,1)}, u32[]{:S(2)}, u32[]{:S(2)}) collective-permute-start(bf16[4096,128]{1,0:T(8,128)(2,1)} %slice.25), channel_id=1, source_target_pairs={{0,4},{4,8},{8,12},{12,16},{16,20},{20,24},{24,28},{28,32},{32,36}... | collective-permute-start | bytes 3145736 | tf_op jit(solution)/shard_map/ppermute | solution.py:243
  52.6 1.4 %collective-permute-start.6 = (f32[2,128,128]{2,1,0:T(8,128)S(1)}, f32[2,128,128]{2,1,0:T(8,128)S(1)}, u32[]{:S(2)}, u32[]{:S(2)}) collective-permute-start(f32[2,128,128]{2,1,0:T(8,128)S(1)} %dynamic-slice_bitcast_fusion), channel_id=1, source_target_pairs={{0,1},{1,0},{2,3},{3,2},{4,5},{5,4},{6,7},{7,6},{8,9},{9,8},{10,11... | collective-permute-start | bytes 393224 | tf_op jit(solution)/shard_map/ppermute | solution.py:182
  55.0 7.1 %collective-permute-start.7 = (f32[128,128]{1,0:T(8,128)S(1)}, f32[128,128]{1,0:T(8,128)S(1)}, u32[]{:S(2)}, u32[]{:S(2)}) collective-permute-start(f32[128,128]{1,0:T(8,128)S(1)} %get-tuple-element.30), channel_id=1, source_target_pairs={{0,2},{1,3},{2,0},{3,1},{4,6},{5,7},{6,4},{7,5},{8,10},{9,11},{10,... | collective-permute-start | bytes 196616 | tf_op jit(solution)/shard_map/ppermute | solution.py:182
  55.7 7.5 %collective-permute-start.8 = (f32[128,128]{1,0:T(8,128)S(1)}, f32[128,128]{1,0:T(8,128)S(1)}, u32[]{:S(2)}, u32[]{:S(2)}) collective-permute-start(f32[128,128]{1,0:T(8,128)S(1)} %get-tuple-element.29), channel_id=1, source_target_pairs={{0,16},{1,17},{2,18},{3,19},{4,20},{5,21},{6,22},{7,23},{8,24},{9,... | collective-permute-start | bytes 196616 | tf_op jit(solution)/shard_map/ppermute | solution.py:182
  56.2 7.2 %collective-permute-start.9 = (f32[128,128]{1,0:T(8,128)S(1)}, f32[128,128]{1,0:T(8,128)S(1)}, u32[]{:S(2)}, u32[]{:S(2)}) collective-permute-start(f32[128,128]{1,0:T(8,128)S(1)} %get-tuple-element.30), channel_id=1, source_target_pairs={{0,18},{1,19},{2,16},{3,17},{4,22},{5,23},{6,20},{7,21},{8,26},{9,... | collective-permute-start | bytes 196616 | tf_op jit(solution)/shard_map/ppermute | solution.py:182
  63.5 9.4 %collective-permute-start.10 = (f32[128,128]{1,0:T(8,128)S(1)}, f32[128,128]{1,0:T(8,128)S(1)}, u32[]{:S(2)}, u32[]{:S(2)}) collective-permute-start(f32[128,128]{1,0:T(8,128)S(1)} %add_add_fusion.1), channel_id=1, source_target_pairs={{0,32},{1,33},{2,34},{3,35},{4,36},{5,37},{6,38},{7,39},{8,40},{9,... | collective-permute-start | bytes 196616 | tf_op jit(solution)/shard_map/ppermute | solution.py:182
  64.7 8.1 %collective-permute-start.11 = (f32[128,128]{1,0:T(8,128)S(1)}, f32[128,128]{1,0:T(8,128)S(1)}, u32[]{:S(2)}, u32[]{:S(2)}) collective-permute-start(f32[128,128]{1,0:T(8,128)S(1)} %add_add_fusion.1), channel_id=1, source_target_pairs={{0,96},{1,97},{2,98},{3,99},{4,100},{5,101},{6,102},{7,103},{8,104... | collective-permute-start | bytes 196616 | tf_op jit(solution)/shard_map/ppermute | solution.py:182
  66.8 6.1 %collective-permute-start.12 = (f32[128,128]{1,0:T(8,128)S(1)}, f32[128,128]{1,0:T(8,128)S(1)}, u32[]{:S(2)}, u32[]{:S(2)}) collective-permute-start(f32[128,128]{1,0:T(8,128)S(1)} %add_add_fusion.1), channel_id=1, source_target_pairs={{0,64},{1,65},{2,66},{3,67},{4,68},{5,69},{6,70},{7,71},{8,72},{9,... | collective-permute-start | bytes 196616 | tf_op jit(solution)/shard_map/ppermute | solution.py:182
  72.9 8.0 %collective-permute-start.13 = (f32[128,128]{1,0:T(8,128)S(1)}, f32[128,128]{1,0:T(8,128)S(1)}, u32[]{:S(2)}, u32[]{:S(2)}) collective-permute-start(f32[128,128]{1,0:T(8,128)S(1)} %add_add_fusion), channel_id=1, source_target_pairs={{0,4},{1,5},{2,6},{3,7},{4,8},{5,9},{6,10},{7,11},{8,12},{9,13},{1... | collective-permute-start | bytes 196616 | tf_op jit(solution)/shard_map/ppermute | solution.py:182
  73.0 8.0 %collective-permute-start.14 = (f32[128,128]{1,0:T(8,128)S(1)}, f32[128,128]{1,0:T(8,128)S(1)}, u32[]{:S(2)}, u32[]{:S(2)}) collective-permute-start(f32[128,128]{1,0:T(8,128)S(1)} %add_add_fusion), channel_id=1, source_target_pairs={{0,12},{1,13},{2,14},{3,15},{4,0},{5,1},{6,2},{7,3},{8,4},{9,5},{1... | collective-permute-start | bytes 196616 | tf_op jit(solution)/shard_map/ppermute | solution.py:182
  76.2 5.8 %collective-permute-start.15 = (f32[128,128]{1,0:T(8,128)S(1)}, f32[128,128]{1,0:T(8,128)S(1)}, u32[]{:S(2)}, u32[]{:S(2)}) collective-permute-start(f32[128,128]{1,0:T(8,128)S(1)} %add_add_fusion), channel_id=1, source_target_pairs={{0,8},{1,9},{2,10},{3,11},{4,12},{5,13},{6,14},{7,15},{8,0},{9,1},... | collective-permute-start | bytes 196616 | tf_op jit(solution)/shard_map/ppermute | solution.py:182

commit v6 on v5

--- a/solution.py
+++ b/solution.py
@@ -206,8 +206,8 @@
 
 
 def reduce_rest(x):
-    x = around(x, [lambda c, f, step=step: ((c + 8 * step) % 32, f) for step in (1, 3, 2)])
-    return around(x, [lambda c, f, step=step: (c // 4 * 4 + (c + step) % 4, f) for step in (1, 3, 2)])
+    x = around(x, [lambda c, f, step=step: (c // 4 * 4 + (c + step) % 4, f) for step in (1, 3, 2)])
+    return around(x, [lambda c, f, step=step: ((c + 8 * step) % 32, f) for step in (1, 3, 2)])
 
 
 def per_device(query, gated, grad_out, filters):

time: 82.9 us -> 83.1 us (level)
  transfers between devices with their start and end apart: 16 -> 16, of which waited for: 6 -> 6; matrix products, arithmetic and copies ran while one was open for 10% -> 10% of each run, Pallas kernels for 30% -> 29%
where the time goes in v6:
time: 83.1 us; the launch traced here: 82.8 us
  starting transfers between devices  26 us (31%)
  Pallas kernels  24.4 us (29%)
  waiting for transfers between devices  22.6 us (27%)
  other arithmetic  6.93 us (8%)
  local copies, waits for them, and re-layouts  2.08 us (3%)
    pallas_call x4, Pallas kernels, run(): pl.pallas_call(body, out_shape=[jax.ShapeDtypeStruct(out.shape, out.dtype...  22.3 us
    ppermute x1, waiting for transfers between devices, per_device(): prev_a = lax.ppermute(sent_a, 'ctx', up)  16.3 us
    ppermute x12, starting transfers between devices, exchange(): return lax.ppermute(x, ('ctx', 'fsdp'), pairs)  14.8 us
    ppermute x1, starting transfers between devices, per_device(): nxt_b = lax.ppermute(sent_b, 'ctx', down)  7.03 us
    ppermute x12, waiting for transfers between devices, exchange(): return lax.ppermute(x, ('ctx', 'fsdp'), pairs)  6.29 us
    convert_element_type x2, other arithmetic, per_device(): (rows(o, start, size).astype(F32) * rows(q, start, size).astype(F32)).ast...  5.32 us
    ppermute x1, starting transfers between devices, per_device(): prev_a = lax.ppermute(sent_a, 'ctx', up)  2.07 us
    pallas_call x1, Pallas kernels, per_device(): pl.pallas_call(taps_kernel, out_shape=jax.ShapeDtypeStruct((width // GROU...  2.05 us
  transfers between devices with their start and end apart: 16, of which 6 were waited for; matrix products, arithmetic and copies ran while one was open for 10% of the time, Pallas kernels for 29%

profile of v6, /device:TPU:0, one launch (start us, length us, event | category | flops | bytes accessed | tf_op | source)
XLA Modules:
  0.0 82.8 jit_solution(15547003335704758438)
XLA Ops:
  0.7 1.7 %collective-permute-start = (f32[128,128]{1,0:T(8,128)}, f32[128,128]{1,0:T(8,128)S(1)}, u32[]{:S(2)}, u32[]{:S(2)}) collective-permute-start(f32[128,128]{1,0:T(8,128)} %param.12), channel_id=1, source_target_pairs={{0,2},{1,3},{2,0},{3,1},{4,6},{5,7},{6,4},{7,5},{8,10},{9,11},{10,... | collective-permute-start | bytes 196616 | tf_op jit(solution)/shard_map/ppermute | solution.py:182
  2.4 2.8 %fusion.refs_1_ = bf16[4096,128]{1,0:T(8,128)(2,1)} fusion(bf16[1,8192,128]{2,1,0:T(8,128)(2,1)} %param.9, bf16[1,8192,128]{2,1,0:T(8,128)(2,1)} %param.11), kind=kLoop, calls=%fused_computation.2 | loop fusion | flops 2097152 | bytes 3145728 | tf_op jit(solution)/shard_map/convert_element_type | solution.py:224
  5.4 2.1 %collective-permute-start.5 = (bf16[4096,128]{1,0:T(8,128)(2,1)S(1)}, bf16[4096,128]{1,0:T(8,128)(2,1)}, u32[]{:S(2)}, u32[]{:S(2)}) collective-permute-start(bf16[4096,128]{1,0:T(8,128)(2,1)S(1)} %slice_bitcast_fusion), channel_id=1, source_target_pairs={{0,4},{4,8},{8,12},{12,16},{16,20},{20,24},{24,28},{28,32},{32,36}... | collective-permute-start | bytes 3145736 | tf_op jit(solution)/shard_map/ppermute | solution.py:239
  7.5 7.0 %collective-permute-start.4 = (bf16[4096,128]{1,0:T(8,128)(2,1)}, bf16[4096,128]{1,0:T(8,128)(2,1)}, u32[]{:S(2)}, u32[]{:S(2)}) collective-permute-start(bf16[4096,128]{1,0:T(8,128)(2,1)} %fusion.refs_1_), channel_id=1, source_target_pairs={{4,0},{8,4},{12,8},{16,12},{20,16},{24,20},{28,24},{32,28},{36,32}... | collective-permute-start | bytes 3145736 | tf_op jit(solution)/shard_map/ppermute | solution.py:240
  14.5 2.5 %multiply_convert_fusion.refs_4_.refs_1_ = bf16[4096,128]{1,0:T(8,128)(2,1)} fusion(bf16[8192,128]{1,0:T(8,128)(2,1)} %bitcast.27, bf16[8192,128]{1,0:T(8,128)(2,1)S(1)} %bitcast.26), kind=kLoop, calls=%fused_computation | loop fusion | flops 2097152 | bytes 3145728 | tf_op jit(solution)/shard_map/convert_element_type | solution.py:224
  17.1 1.9 %collective-permute-start.3 = (bf16[4096,128]{1,0:T(8,128)(2,1)}, bf16[4096,128]{1,0:T(8,128)(2,1)}, u32[]{:S(2)}, u32[]{:S(2)}) collective-permute-start(bf16[4096,128]{1,0:T(8,128)(2,1)} %multiply_convert_fusion.refs_4_.refs_1_), channel_id=1, source_target_pairs={{4,0},{8,4},{12,8},{16,12},{20,16},{24,20},{28,24},{32,28},{36,32}... | collective-permute-start | bytes 3145736 | tf_op jit(solution)/shard_map/ppermute | solution.py:244
  19.0 1.1 %slice.25 = bf16[4096,128]{1,0:T(8,128)(2,1)} slice(bf16[8192,128]{1,0:T(8,128)(2,1)S(1)} %bitcast.23), slice={[4096:8192], [0:128]} | slice | bytes 2097152 | tf_op jit(solution)/shard_map/slice | solution.py:223
  20.2 2.1 %taps_spectra.1.refs_3_.refs_2_ = f32[512,256]{1,0:T(8,128)} custom-call(f32[2,128,128]{2,1,0:T(8,128)} %copy-done.2, f32[2,128,128]{2,1,0:T(8,128)} %copy-done.3, bf16[256,256]{1,0:T(8,128)(2,1)} %constant.60.clone.left.refs_6_), custom_call_target="tpu_custom_call" | custom-call | tf_op jit(solution)/shard_map/taps_spectra/pallas_call | solution.py:234
  22.2 16.3 %collective-permute-done.5.refs_0_ = bf16[4096,128]{1,0:T(8,128)(2,1)} collective-permute-done((bf16[4096,128]{1,0:T(8,128)(2,1)S(1)}, bf16[4096,128]{1,0:T(8,128)(2,1)}, u32[]{:S(2)}, u32[]{:S(2)}) %collective-permute-start.5) | collective-permute-done | bytes 1048608 | tf_op jit(solution)/shard_map/ppermute | solution.py:239
  38.6 6.7 %conv_taps_kernel.1 = (bf16[8192,128]{1,0:T(8,128)(2,1)}, f32[512,128]{1,0:T(8,128)}) custom-call(bf16[4096,128]{1,0:T(8,128)(2,1)} %collective-permute-done.5.refs_0_, bf16[8192,128]{1,0:T(8,128)(2,1)} %bitcast.20, bf16[8192,128]{1,0:T(8,128)(2,1)} %bitcast.24, f32[512,256]{1,0:T(8,128)} %taps_spectra.1.refs_3_.refs_2_, ...), custom_call_target="tpu_custom_call" | custom-call | tf_op jit(solution)/shard_map/conv_taps_kernel/pallas_call | solution.py:161
  45.2 6.4 %corr_taps_kernel.1 = (bf16[8192,128]{1,0:T(8,128)(2,1)}, f32[512,128]{1,0:T(8,128)}) custom-call(bf16[4096,128]{1,0:T(8,128)(2,1)} %collective-permute-done.4.refs_0_, bf16[4096,128]{1,0:T(8,128)(2,1)} %fusion.refs_1_, f32[512,256]{1,0:T(8,128)} %taps_spectra.1.refs_3_.refs_2_, bf16[8192,128]{1,0:T(8,128)(2,1)} %bitcast.21, ...), custom_call_target="tpu_custom_call", output_to_operand_aliasing={{1}: (7, {})} | custom-call | tf_op jit(solution)/shard_map/corr_taps_kernel/pallas_call | solution.py:161
  51.7 0.9 %dynamic-slice_bitcast_fusion = f32[2,128,128]{2,1,0:T(8,128)S(1)} fusion(f32[2,2,128,128]{3,2,1,0:T(8,128)} %bitcast.28, s32[]{:T(128)S(6)} %select_n.39), kind=kLoop, calls=%fused_computation.6 | loop fusion | bytes 262148 | tf_op jit(solution)/shard_map/jit(dynamic_index_in_dim)/squeeze | solution.py:190
  52.7 1.3 %collective-permute-done.6 = f32[2,128,128]{2,1,0:T(8,128)S(1)} collective-permute-done((f32[2,128,128]{2,1,0:T(8,128)S(1)}, f32[2,128,128]{2,1,0:T(8,128)S(1)}, u32[]{:S(2)}, u32[]{:S(2)}) %collective-permute-start.6) | collective-permute-done | bytes 131104 | tf_op jit(solution)/shard_map/ppermute | solution.py:182
  54.0 0.9 %bitcast_add_fusion = f32[2,128,128]{2,1,0:T(8,128)S(1)} fusion(f32[2,128,128]{2,1,0:T(8,128)S(1)} %collective-permute-done.6, f32[2,2,128,128]{3,2,1,0:T(8,128)} %bitcast.29, s32[]{:T(128)S(6)} %select_n.38), kind=kLoop, calls=%fused_computation.5 | loop fusion | flops 32768 | bytes 393220 | tf_op jit(solution)/shard_map/add | solution.py:195
  56.2 3.5 %collective-permute-start.9 = (f32[128,128]{1,0:T(8,128)S(1)}, f32[128,128]{1,0:T(8,128)S(1)}, u32[]{:S(2)}, u32[]{:S(2)}) collective-permute-start(f32[128,128]{1,0:T(8,128)S(1)} %get-tuple-element.30), channel_id=1, source_target_pairs={{0,18},{1,19},{2,16},{3,17},{4,22},{5,23},{6,20},{7,21},{8,26},{9,... | collective-permute-start | bytes 196616 | tf_op jit(solution)/shard_map/ppermute | solution.py:182
  59.7 2.3 %collective-permute-done.7 = f32[128,128]{1,0:T(8,128)S(1)} collective-permute-done((f32[128,128]{1,0:T(8,128)S(1)}, f32[128,128]{1,0:T(8,128)S(1)}, u32[]{:S(2)}, u32[]{:S(2)}) %collective-permute-start.7) | collective-permute-done | bytes 65568 | tf_op jit(solution)/shard_map/ppermute | solution.py:182
  62.0 1.2 %collective-permute-done.8 = f32[128,128]{1,0:T(8,128)S(1)} collective-permute-done((f32[128,128]{1,0:T(8,128)S(1)}, f32[128,128]{1,0:T(8,128)S(1)}, u32[]{:S(2)}, u32[]{:S(2)}) %collective-permute-start.8) | collective-permute-done | bytes 65568 | tf_op jit(solution)/shard_map/ppermute | solution.py:182
  63.5 3.2 %collective-permute-start.11 = (f32[128,128]{1,0:T(8,128)S(1)}, f32[128,128]{1,0:T(8,128)S(1)}, u32[]{:S(2)}, u32[]{:S(2)}) collective-permute-start(f32[128,128]{1,0:T(8,128)S(1)} %add_add_fusion.1), channel_id=1, source_target_pairs={{0,12},{1,13},{2,14},{3,15},{4,0},{5,1},{6,2},{7,3},{8,4},{9,5},{1... | collective-permute-start | bytes 196616 | tf_op jit(solution)/shard_map/ppermute | solution.py:182
  66.8 4.5 %corr_kernel.1 = bf16[8192,128]{1,0:T(8,128)(2,1)} custom-call(bf16[4096,128]{1,0:T(8,128)(2,1)} %collective-permute-done.3.refs_0_, bf16[4096,128]{1,0:T(8,128)(2,1)} %multiply_convert_fusion.refs_4_.refs_1_, f32[512,256]{1,0:T(8,128)} %taps_spectra.1.refs_3_.refs_2_, ...), custom_call_target="tpu_custom_call", output_to_operand_aliasing={{}: (5, {})} | custom-call | flops 5000000000 | bytes 50000000 | tf_op jit(solution)/shard_map/corr_kernel/pallas_call | solution.py:161
  71.3 1.2 %collective-permute-done.12 = f32[128,128]{1,0:T(8,128)S(1)} collective-permute-done((f32[128,128]{1,0:T(8,128)S(1)}, f32[128,128]{1,0:T(8,128)S(1)}, u32[]{:S(2)}, u32[]{:S(2)}) %collective-permute-start.12) | collective-permute-done | bytes 65568 | tf_op jit(solution)/shard_map/ppermute | solution.py:182
  72.6 1.3 %collective-permute-start.13 = (f32[128,128]{1,0:T(8,128)S(1)}, f32[128,128]{1,0:T(8,128)S(1)}, u32[]{:S(2)}, u32[]{:S(2)}) collective-permute-start(f32[128,128]{1,0:T(8,128)S(1)} %add_add_fusion), channel_id=1, source_target_pairs={{0,32},{1,33},{2,34},{3,35},{4,36},{5,37},{6,38},{7,39},{8,40},{9,... | collective-permute-start | bytes 196616 | tf_op jit(solution)/shard_map/ppermute | solution.py:182
  73.8 2.0 %collective-permute-start.14 = (f32[128,128]{1,0:T(8,128)S(1)}, f32[128,128]{1,0:T(8,128)S(1)}, u32[]{:S(2)}, u32[]{:S(2)}) collective-permute-start(f32[128,128]{1,0:T(8,128)S(1)} %add_add_fusion), channel_id=1, source_target_pairs={{0,96},{1,97},{2,98},{3,99},{4,100},{5,101},{6,102},{7,103},{8,104... | collective-permute-start | bytes 196616 | tf_op jit(solution)/shard_map/ppermute | solution.py:182
  75.9 1.5 %collective-permute-start.15 = (f32[128,128]{1,0:T(8,128)S(1)}, f32[128,128]{1,0:T(8,128)S(1)}, u32[]{:S(2)}, u32[]{:S(2)}) collective-permute-start(f32[128,128]{1,0:T(8,128)S(1)} %add_add_fusion), channel_id=1, source_target_pairs={{0,64},{1,65},{2,66},{3,67},{4,68},{5,69},{6,70},{7,71},{8,72},{9,... | collective-permute-start | bytes 196616 | tf_op jit(solution)/shard_map/ppermute | solution.py:182
  77.4 4.7 %conv_kernel.1 = bf16[8192,128]{1,0:T(8,128)(2,1)} custom-call(bf16[4096,128]{1,0:T(8,128)(2,1)} %collective-permute-done.2.refs_0_, bf16[8192,128]{1,0:T(8,128)(2,1)} %bitcast.22, bf16[8192,128]{1,0:T(8,128)(2,1)} %bitcast.25, f32[512,256]{1,0:T(8,128)} %taps_spectra.1.refs_3_.refs_2_, ...), custom_call_target="tpu_custom_call", output_to_operand_aliasing={{}: (6, {})} | custom-call | flops 5000000000 | bytes 50000000 | tf_op jit(solution)/shard_map/conv_kernel/pallas_call | solution.py:161
  (34 shorter events, 2.7 us)
Async XLA Ops:
  0.6 4.6 %copy-start.4 = (f32[128,128]{1,0:T(8,128)S(1)}, f32[128,128]{1,0:T(8,128)}, u32[]{:S(2)}) copy-start(f32[128,128]{1,0:T(8,128)} %param.12) | copy-start | bytes 196612
  0.6 4.7 %copy-start = (bf16[1,8192,128]{2,1,0:T(8,128)(2,1)S(1)}, bf16[1,8192,128]{2,1,0:T(8,128)(2,1)}, u32[]{:S(2)}) copy-start(bf16[1,8192,128]{2,1,0:T(8,128)(2,1)} %param.10) | copy-start | bytes 6291460
  0.7 4.6 %collective-permute-start = (f32[128,128]{1,0:T(8,128)}, f32[128,128]{1,0:T(8,128)S(1)}, u32[]{:S(2)}, u32[]{:S(2)}) collective-permute-start(f32[128,128]{1,0:T(8,128)} %param.12), channel_id=1, source_target_pairs={{0,2},{1,3},{2,0},{3,1},{4,6},{5,7},{6,4},{7,5},{8,10},{9,11},{10,... | collective-permute-start | bytes 196616 | tf_op jit(solution)/shard_map/ppermute | solution.py:182
  5.2 9.4 %copy-start.1 = (bf16[1,8192,128]{2,1,0:T(8,128)(2,1)S(1)}, bf16[1,8192,128]{2,1,0:T(8,128)(2,1)}, u32[]{:S(2)}) copy-start(bf16[1,8192,128]{2,1,0:T(8,128)(2,1)} %param.11) | copy-start | bytes 6291460
  5.2 11.8 %copy-start.2 = (f32[2,128,128]{2,1,0:T(8,128)}, f32[2,128,128]{2,1,0:T(8,128)S(1)}, u32[]{:S(2)}) copy-start(f32[2,128,128]{2,1,0:T(8,128)S(1)} %maximum_select_fusion.column) | copy-start | bytes 393220
  5.2 9.3 %collective-permute-start.1 = (f32[2,128,128]{2,1,0:T(8,128)S(1)}, f32[2,128,128]{2,1,0:T(8,128)S(1)}, u32[]{:S(2)}, u32[]{:S(2)}) collective-permute-start(f32[2,128,128]{2,1,0:T(8,128)S(1)} %maximum_select_fusion.column), channel_id=1, source_target_pairs={{0,1},{1,0},{2,3},{3,2},{4,5},{5,4},{6,7},{7,6},{8,9},{9,8},{10,11... | collective-permute-start | bytes 393224 | tf_op jit(solution)/shard_map/ppermute | solution.py:182
  5.4 33.1 %collective-permute-start.5 = (bf16[4096,128]{1,0:T(8,128)(2,1)S(1)}, bf16[4096,128]{1,0:T(8,128)(2,1)}, u32[]{:S(2)}, u32[]{:S(2)}) collective-permute-start(bf16[4096,128]{1,0:T(8,128)(2,1)S(1)} %slice_bitcast_fusion), channel_id=1, source_target_pairs={{0,4},{4,8},{8,12},{12,16},{16,20},{20,24},{24,28},{28,32},{32,36}... | collective-permute-start | bytes 3145736 | tf_op jit(solution)/shard_map/ppermute | solution.py:239
  7.5 37.7 %collective-permute-start.4 = (bf16[4096,128]{1,0:T(8,128)(2,1)}, bf16[4096,128]{1,0:T(8,128)(2,1)}, u32[]{:S(2)}, u32[]{:S(2)}) collective-permute-start(bf16[4096,128]{1,0:T(8,128)(2,1)} %fusion.refs_1_), channel_id=1, source_target_pairs={{4,0},{8,4},{12,8},{16,12},{20,16},{24,20},{28,24},{32,28},{36,32}... | collective-permute-start | bytes 3145736 | tf_op jit(solution)/shard_map/ppermute | solution.py:240
  14.5 5.5 %copy-start.3 = (f32[2,128,128]{2,1,0:T(8,128)}, f32[2,128,128]{2,1,0:T(8,128)S(1)}, u32[]{:S(2)}) copy-start(f32[2,128,128]{2,1,0:T(8,128)S(1)} %collective-permute-done.1.near) | copy-start | bytes 393220
  17.1 46.4 %collective-permute-start.3 = (bf16[4096,128]{1,0:T(8,128)(2,1)}, bf16[4096,128]{1,0:T(8,128)(2,1)}, u32[]{:S(2)}, u32[]{:S(2)}) collective-permute-start(bf16[4096,128]{1,0:T(8,128)(2,1)} %multiply_convert_fusion.refs_4_.refs_1_), channel_id=1, source_target_pairs={{4,0},{8,4},{12,8},{16,12},{20,16},{24,20},{28,24},{32,28},{36,32}... | collective-permute-start | bytes 3145736 | tf_op jit(solution)/shard_map/ppermute | solution.py:244
  20.1 43.4 %collective-permute-start.2 = (bf16[4096,128]{1,0:T(8,128)(2,1)}, bf16[4096,128]{1,0:T(8,128)(2,1)}, u32[]{:S(2)}, u32[]{:S(2)}) collective-permute-start(bf16[4096,128]{1,0:T(8,128)(2,1)} %slice.25), channel_id=1, source_target_pairs={{0,4},{4,8},{8,12},{12,16},{16,20},{20,24},{24,28},{28,32},{32,36}... | collective-permute-start | bytes 3145736 | tf_op jit(solution)/shard_map/ppermute | solution.py:243
  52.6 1.4 %collective-permute-start.6 = (f32[2,128,128]{2,1,0:T(8,128)S(1)}, f32[2,128,128]{2,1,0:T(8,128)S(1)}, u32[]{:S(2)}, u32[]{:S(2)}) collective-permute-start(f32[2,128,128]{2,1,0:T(8,128)S(1)} %dynamic-slice_bitcast_fusion), channel_id=1, source_target_pairs={{0,1},{1,0},{2,3},{3,2},{4,5},{5,4},{6,7},{7,6},{8,9},{9,8},{10,11... | collective-permute-start | bytes 393224 | tf_op jit(solution)/shard_map/ppermute | solution.py:182
  55.0 7.1 %collective-permute-start.7 = (f32[128,128]{1,0:T(8,128)S(1)}, f32[128,128]{1,0:T(8,128)S(1)}, u32[]{:S(2)}, u32[]{:S(2)}) collective-permute-start(f32[128,128]{1,0:T(8,128)S(1)} %get-tuple-element.30), channel_id=1, source_target_pairs={{0,2},{1,3},{2,0},{3,1},{4,6},{5,7},{6,4},{7,5},{8,10},{9,11},{10,... | collective-permute-start | bytes 196616 | tf_op jit(solution)/shard_map/ppermute | solution.py:182
  55.7 7.5 %collective-permute-start.8 = (f32[128,128]{1,0:T(8,128)S(1)}, f32[128,128]{1,0:T(8,128)S(1)}, u32[]{:S(2)}, u32[]{:S(2)}) collective-permute-start(f32[128,128]{1,0:T(8,128)S(1)} %get-tuple-element.29), channel_id=1, source_target_pairs={{0,16},{1,17},{2,18},{3,19},{4,20},{5,21},{6,22},{7,23},{8,24},{9,... | collective-permute-start | bytes 196616 | tf_op jit(solution)/shard_map/ppermute | solution.py:182
  56.2 7.2 %collective-permute-start.9 = (f32[128,128]{1,0:T(8,128)S(1)}, f32[128,128]{1,0:T(8,128)S(1)}, u32[]{:S(2)}, u32[]{:S(2)}) collective-permute-start(f32[128,128]{1,0:T(8,128)S(1)} %get-tuple-element.30), channel_id=1, source_target_pairs={{0,18},{1,19},{2,16},{3,17},{4,22},{5,23},{6,20},{7,21},{8,26},{9,... | collective-permute-start | bytes 196616 | tf_op jit(solution)/shard_map/ppermute | solution.py:182
  63.5 7.8 %collective-permute-start.10 = (f32[128,128]{1,0:T(8,128)S(1)}, f32[128,128]{1,0:T(8,128)S(1)}, u32[]{:S(2)}, u32[]{:S(2)}) collective-permute-start(f32[128,128]{1,0:T(8,128)S(1)} %add_add_fusion.1), channel_id=1, source_target_pairs={{0,4},{1,5},{2,6},{3,7},{4,8},{5,9},{6,10},{7,11},{8,12},{9,13},{1... | collective-permute-start | bytes 196616 | tf_op jit(solution)/shard_map/ppermute | solution.py:182
  63.5 7.8 %collective-permute-start.11 = (f32[128,128]{1,0:T(8,128)S(1)}, f32[128,128]{1,0:T(8,128)S(1)}, u32[]{:S(2)}, u32[]{:S(2)}) collective-permute-start(f32[128,128]{1,0:T(8,128)S(1)} %add_add_fusion.1), channel_id=1, source_target_pairs={{0,12},{1,13},{2,14},{3,15},{4,0},{5,1},{6,2},{7,3},{8,4},{9,5},{1... | collective-permute-start | bytes 196616 | tf_op jit(solution)/shard_map/ppermute | solution.py:182
  66.8 5.8 %collective-permute-start.12 = (f32[128,128]{1,0:T(8,128)S(1)}, f32[128,128]{1,0:T(8,128)S(1)}, u32[]{:S(2)}, u32[]{:S(2)}) collective-permute-start(f32[128,128]{1,0:T(8,128)S(1)} %add_add_fusion.1), channel_id=1, source_target_pairs={{0,8},{1,9},{2,10},{3,11},{4,12},{5,13},{6,14},{7,15},{8,0},{9,1},... | collective-permute-start | bytes 196616 | tf_op jit(solution)/shard_map/ppermute | solution.py:182
  72.6 9.6 %collective-permute-start.13 = (f32[128,128]{1,0:T(8,128)S(1)}, f32[128,128]{1,0:T(8,128)S(1)}, u32[]{:S(2)}, u32[]{:S(2)}) collective-permute-start(f32[128,128]{1,0:T(8,128)S(1)} %add_add_fusion), channel_id=1, source_target_pairs={{0,32},{1,33},{2,34},{3,35},{4,36},{5,37},{6,38},{7,39},{8,40},{9,... | collective-permute-start | bytes 196616 | tf_op jit(solution)/shard_map/ppermute | solution.py:182
  73.8 8.3 %collective-permute-start.14 = (f32[128,128]{1,0:T(8,128)S(1)}, f32[128,128]{1,0:T(8,128)S(1)}, u32[]{:S(2)}, u32[]{:S(2)}) collective-permute-start(f32[128,128]{1,0:T(8,128)S(1)} %add_add_fusion), channel_id=1, source_target_pairs={{0,96},{1,97},{2,98},{3,99},{4,100},{5,101},{6,102},{7,103},{8,104... | collective-permute-start | bytes 196616 | tf_op jit(solution)/shard_map/ppermute | solution.py:182
  75.9 6.3 %collective-permute-start.15 = (f32[128,128]{1,0:T(8,128)S(1)}, f32[128,128]{1,0:T(8,128)S(1)}, u32[]{:S(2)}, u32[]{:S(2)}) collective-permute-start(f32[128,128]{1,0:T(8,128)S(1)} %add_add_fusion), channel_id=1, source_target_pairs={{0,64},{1,65},{2,66},{3,67},{4,68},{5,69},{6,70},{7,71},{8,72},{9,... | collective-permute-start | bytes 196616 | tf_op jit(solution)/shard_map/ppermute | solution.py:182

commit v7 on v4

--- a/solution.py
+++ b/solution.py
@@ -12,7 +12,7 @@
 FLEN = 128
 GROUP_CH = 16
 WIN = 2 * FLEN
-BLOCK = 1024
+BLOCK = 2048
 VMEM_MB = 63
 F32, BF16 = jnp.float32, jnp.bfloat16
 
@@ -144,7 +144,7 @@
             h[at : at + FLEN, :] = half_spectrum(taps.astype(BF16), table)
 
 
-def run(kernel, blocks, consts, results, size, cost=0):
+def run(kernel, blocks, consts, results, size, cost=0, block=BLOCK):
     args = [a for a, _ in blocks] + list(consts)
     specs = [s for _, s in blocks] + [whole(c) for c in consts]
     used, aliases = len(args), {}
@@ -161,9 +161,9 @@
     return pl.pallas_call(
         body,
         out_shape=[jax.ShapeDtypeStruct(out.shape, out.dtype) for out, _, _ in results],
-        grid=(size // BLOCK,),
+        grid=(size // block,),
         in_specs=specs,
-        out_specs=[rows_at(start, FLEN, block) for _, start, block in results],
+        out_specs=[rows_at(start, FLEN, n) for _, start, n in results],
         input_output_aliases=aliases,
         compiler_params=pltpu.CompilerParams(vmem_limit_bytes=VMEM_MB * 1024 * 1024),
         cost_estimate=pl.CostEstimate(flops=cost * 10**9, bytes_accessed=cost * 10**7, transcendentals=0),
@@ -228,14 +228,14 @@
     fsdp = lax.axis_index("fsdp")
     far = exchange(filters, lambda c, f: (c, f ^ 2))
     column = jnp.where(fsdp // 2 == 0, jnp.stack([filters, far]), jnp.stack([far, filters]))
+    core_b = product(grad_out, query, half, half)
+    sent_b, column = lax.optimization_barrier((core_b, column))
     near = exchange(column, lambda c, f: (c, f ^ 1))
     h = pl.pallas_call(
         taps_kernel, out_shape=jax.ShapeDtypeStruct((width // GROUP_CH, WIN), F32), name="taps_spectra"
     )(column, near, left)
 
     sent_a, _ = lax.optimization_barrier((rows(gated, 0, half), far))
-    core_b = product(grad_out, query, half, half)
-    sent_b, _ = lax.optimization_barrier((core_b, near))
     prev_a = lax.ppermute(sent_a, "ctx", up)
     nxt_b = lax.ppermute(sent_b, "ctx", down)
     late = lax.optimization_barrier((gated, grad_out, query, core_b, near))[:3]
@@ -261,19 +261,23 @@
     )
     partial = reduce_first(partial.reshape(2, 2, -1, FLEN))
     def conv(gq, start, size, cost):
+        n = 1024
+        part = lambda first: rows_at(first, FLEN, n)
         return run(
             conv_kernel,
-            [(prev_b, at(start)), (gated, at(half + start)), (grad_out, at(half + start)), (h, h_at(half + start))],
+            [(prev_b, part(start)), (gated, part(half + start)), (grad_out, part(half + start)),
+             (h, rows_at((half + start) // GROUP_CH, WIN, n // GROUP_CH))],
             (fwd2, inv_b),
-            [(gq, half + start, BLOCK)],
+            [(gq, half + start, n)],
             size,
             cost,
+            n,
         )[0]
 
-    gq = conv(gq, 0, half // 2, 0)
+    gq = conv(gq, 0, 1024, 0)
     gq, nxt_a, partial = lax.optimization_barrier((gq, nxt_a, partial))
     summed = reduce_rest(partial)
-    gq = conv(gq, half // 2, half // 2, 5)
+    gq = conv(gq, 1024, half - 1024, 5)
     gg, = run(
         corr_kernel,
         [(nxt_a, at(0)), (core_a, at(0)), (h, h_at(0))],

time: 84.3 us -> 82.9 us (0.983)
  Pallas kernels: 28.1 us -> 27 us
  waiting for transfers between devices: 14.8 us -> 15.7 us
    pallas_call x5, Pallas kernels: 26.1 us -> 24.9 us  [run(): pl.pallas_call(body, out_shape=[jax.ShapeDtypeStruct(out.shape, out.dtype...]
    ppermute x12, waiting for transfers between devices: 3.64 us -> 2.47 us  [exchange(): return lax.ppermute(x, ('ctx', 'fsdp'), pairs)]
    ppermute x1, starting transfers between devices: 8.12 us -> 7.03 us  [per_device(): nxt_b = lax.ppermute(sent_b, 'ctx', down)]
    ppermute x1, waiting for transfers between devices: 10.8 us -> 11.9 us  [per_device(): prev_a = lax.ppermute(sent_a, 'ctx', up)]
    ppermute x1, waiting for transfers between devices: 0.36 us -> 1.27 us  [per_device(): prev_b = lax.ppermute(rows(late[0], half, half), 'ctx', up)]
  transfers between devices with their start and end apart: 16 -> 16, of which waited for: 4 -> 4; matrix products, arithmetic and copies ran while one was open for 8% -> 9% of each run, Pallas kernels for 34% -> 33%
where the time goes in v7:
time: 82.9 us; the launch traced here: 82.6 us
  starting transfers between devices  31.4 us (38%)
  Pallas kernels  27 us (33%)
  waiting for transfers between devices  15.7 us (19%)
  other arithmetic  5.7 us (7%)
  local copies, waits for them, and re-layouts  2.08 us (3%)
  between operations  0.83 us (1%)
    pallas_call x5, Pallas kernels, run(): pl.pallas_call(body, out_shape=[jax.ShapeDtypeStruct(out.shape, out.dtype...  24.9 us
    ppermute x12, starting transfers between devices, exchange(): return lax.ppermute(x, ('ctx', 'fsdp'), pairs)  14.6 us
    ppermute x1, waiting for transfers between devices, per_device(): prev_a = lax.ppermute(sent_a, 'ctx', up)  11.9 us
    ppermute x1, starting transfers between devices, per_device(): nxt_a = lax.ppermute(core_a, 'ctx', down)  7.74 us
    ppermute x1, starting transfers between devices, per_device(): nxt_b = lax.ppermute(sent_b, 'ctx', down)  7.03 us
    convert_element_type x2, other arithmetic, per_device(): (rows(o, start, size).astype(F32) * rows(q, start, size).astype(F32)).ast...  4.09 us
    ppermute x12, waiting for transfers between devices, exchange(): return lax.ppermute(x, ('ctx', 'fsdp'), pairs)  2.47 us
    ppermute x1, starting transfers between devices, per_device(): prev_a = lax.ppermute(sent_a, 'ctx', up)  2.06 us
  transfers between devices with their start and end apart: 16, of which 4 were waited for; matrix products, arithmetic and copies ran while one was open for 9% of the time, Pallas kernels for 33%

profile of v7, /device:TPU:0, one launch (start us, length us, event | category | flops | bytes accessed | tf_op | source)
XLA Modules:
  0.0 82.6 jit_solution(13272220234135747632)
XLA Ops:
  0.7 1.7 %collective-permute-start = (f32[128,128]{1,0:T(8,128)}, f32[128,128]{1,0:T(8,128)S(1)}, u32[]{:S(2)}, u32[]{:S(2)}) collective-permute-start(f32[128,128]{1,0:T(8,128)} %param.12), channel_id=1, source_target_pairs={{0,2},{1,3},{2,0},{3,1},{4,6},{5,7},{6,4},{7,5},{8,10},{9,11},{10,... | collective-permute-start | bytes 196616 | tf_op jit(solution)/shard_map/ppermute | solution.py:182
  2.4 2.8 %fusion.refs_1_ = bf16[4096,128]{1,0:T(8,128)(2,1)} fusion(bf16[1,8192,128]{2,1,0:T(8,128)(2,1)} %param.9, bf16[1,8192,128]{2,1,0:T(8,128)(2,1)} %param.11), kind=kLoop, calls=%fused_computation.2 | loop fusion | flops 2097152 | bytes 3145728 | tf_op jit(solution)/shard_map/convert_element_type | solution.py:224
  5.5 2.1 %collective-permute-start.3 = (bf16[4096,128]{1,0:T(8,128)(2,1)S(1)}, bf16[4096,128]{1,0:T(8,128)(2,1)}, u32[]{:S(2)}, u32[]{:S(2)}) collective-permute-start(bf16[4096,128]{1,0:T(8,128)(2,1)S(1)} %slice_bitcast_fusion), channel_id=1, source_target_pairs={{0,4},{4,8},{8,12},{12,16},{16,20},{20,24},{24,28},{28,32},{32,36}... | collective-permute-start | bytes 3145736 | tf_op jit(solution)/shard_map/ppermute | solution.py:239
  7.5 7.0 %collective-permute-start.5 = (bf16[4096,128]{1,0:T(8,128)(2,1)}, bf16[4096,128]{1,0:T(8,128)(2,1)}, u32[]{:S(2)}, u32[]{:S(2)}) collective-permute-start(bf16[4096,128]{1,0:T(8,128)(2,1)} %fusion.refs_1_), channel_id=1, source_target_pairs={{4,0},{8,4},{12,8},{16,12},{20,16},{24,20},{28,24},{32,28},{36,32}... | collective-permute-start | bytes 3145736 | tf_op jit(solution)/shard_map/ppermute | solution.py:240
  14.5 1.0 %slice.25 = bf16[4096,128]{1,0:T(8,128)(2,1)} slice(bf16[8192,128]{1,0:T(8,128)(2,1)S(1)} %bitcast.24), slice={[4096:8192], [0:128]} | slice | bytes 2097152 | tf_op jit(solution)/shard_map/slice | solution.py:223
  15.6 1.3 %multiply_convert_fusion.refs_4_.refs_1_ = bf16[4096,128]{1,0:T(8,128)(2,1)} fusion(bf16[8192,128]{1,0:T(8,128)(2,1)S(1)} %bitcast.29, bf16[8192,128]{1,0:T(8,128)(2,1)S(1)} %bitcast.28), kind=kLoop, calls=%fused_computation | loop fusion | flops 2097152 | bytes 3145728 | tf_op jit(solution)/shard_map/convert_element_type | solution.py:224
  16.9 7.7 %collective-permute-start.4 = (bf16[4096,128]{1,0:T(8,128)(2,1)}, bf16[4096,128]{1,0:T(8,128)(2,1)}, u32[]{:S(2)}, u32[]{:S(2)}) collective-permute-start(bf16[4096,128]{1,0:T(8,128)(2,1)} %multiply_convert_fusion.refs_4_.refs_1_), channel_id=1, source_target_pairs={{4,0},{8,4},{12,8},{16,12},{20,16},{24,20},{28,24},{32,28},{36,32}... | collective-permute-start | bytes 3145736 | tf_op jit(solution)/shard_map/ppermute | solution.py:244
  24.6 2.1 %taps_spectra.1.refs_3_.refs_2_ = f32[512,256]{1,0:T(8,128)} custom-call(f32[2,128,128]{2,1,0:T(8,128)} %copy-done.3, f32[2,128,128]{2,1,0:T(8,128)} %copy-done.4, bf16[256,256]{1,0:T(8,128)(2,1)} %constant.60.clone.left.refs_6_), custom_call_target="tpu_custom_call" | custom-call | tf_op jit(solution)/shard_map/taps_spectra/pallas_call | solution.py:234
  26.7 11.9 %collective-permute-done.3.refs_0_ = bf16[4096,128]{1,0:T(8,128)(2,1)} collective-permute-done((bf16[4096,128]{1,0:T(8,128)(2,1)S(1)}, bf16[4096,128]{1,0:T(8,128)(2,1)}, u32[]{:S(2)}, u32[]{:S(2)}) %collective-permute-start.3) | collective-permute-done | bytes 1048608 | tf_op jit(solution)/shard_map/ppermute | solution.py:239
  38.6 6.7 %conv_taps_kernel.1 = (bf16[8192,128]{1,0:T(8,128)(2,1)}, f32[512,128]{1,0:T(8,128)}) custom-call(bf16[4096,128]{1,0:T(8,128)(2,1)} %collective-permute-done.3.refs_0_, bf16[8192,128]{1,0:T(8,128)(2,1)} %bitcast.20, bf16[8192,128]{1,0:T(8,128)(2,1)} %bitcast.25, f32[512,256]{1,0:T(8,128)} %taps_spectra.1.refs_3_.refs_2_, ...), custom_call_target="tpu_custom_call" | custom-call | tf_op jit(solution)/shard_map/conv_taps_kernel/pallas_call | solution.py:161
  45.2 6.5 %corr_taps_kernel.1 = (bf16[8192,128]{1,0:T(8,128)(2,1)}, f32[512,128]{1,0:T(8,128)}) custom-call(bf16[4096,128]{1,0:T(8,128)(2,1)} %collective-permute-done.5.refs_0_, bf16[4096,128]{1,0:T(8,128)(2,1)} %fusion.refs_1_, f32[512,256]{1,0:T(8,128)} %taps_spectra.1.refs_3_.refs_2_, bf16[8192,128]{1,0:T(8,128)(2,1)} %bitcast.21, ...), custom_call_target="tpu_custom_call", output_to_operand_aliasing={{1}: (7, {})} | custom-call | tf_op jit(solution)/shard_map/corr_taps_kernel/pallas_call | solution.py:161
  51.7 0.9 %dynamic-slice_bitcast_fusion = f32[2,128,128]{2,1,0:T(8,128)S(1)} fusion(f32[2,2,128,128]{3,2,1,0:T(8,128)} %bitcast.31, s32[]{:T(128)S(6)} %select_n.39), kind=kLoop, calls=%fused_computation.6 | loop fusion | bytes 262148 | tf_op jit(solution)/shard_map/jit(dynamic_index_in_dim)/squeeze | solution.py:190
  52.7 1.3 %collective-permute-done.6 = f32[2,128,128]{2,1,0:T(8,128)S(1)} collective-permute-done((f32[2,128,128]{2,1,0:T(8,128)S(1)}, f32[2,128,128]{2,1,0:T(8,128)S(1)}, u32[]{:S(2)}, u32[]{:S(2)}) %collective-permute-start.6) | collective-permute-done | bytes 131104 | tf_op jit(solution)/shard_map/ppermute | solution.py:182
  54.0 0.9 %bitcast_add_fusion = f32[2,128,128]{2,1,0:T(8,128)S(1)} fusion(f32[2,128,128]{2,1,0:T(8,128)S(1)} %collective-permute-done.6, f32[2,2,128,128]{3,2,1,0:T(8,128)} %bitcast.32, s32[]{:T(128)S(6)} %select_n.38), kind=kLoop, calls=%fused_computation.5 | loop fusion | flops 32768 | bytes 393220 | tf_op jit(solution)/shard_map/add | solution.py:195
  56.2 3.5 %collective-permute-start.9 = (f32[128,128]{1,0:T(8,128)S(1)}, f32[128,128]{1,0:T(8,128)S(1)}, u32[]{:S(2)}, u32[]{:S(2)}) collective-permute-start(f32[128,128]{1,0:T(8,128)S(1)} %get-tuple-element.30), channel_id=1, source_target_pairs={{0,18},{1,19},{2,16},{3,17},{4,22},{5,23},{6,20},{7,21},{8,26},{9,... | collective-permute-start | bytes 196616 | tf_op jit(solution)/shard_map/ppermute | solution.py:182
  59.8 1.3 %collective-permute-done.2.refs_0_ = bf16[4096,128]{1,0:T(8,128)(2,1)} collective-permute-done((bf16[4096,128]{1,0:T(8,128)(2,1)}, bf16[4096,128]{1,0:T(8,128)(2,1)}, u32[]{:S(2)}, u32[]{:S(2)}) %collective-permute-start.2) | collective-permute-done | bytes 1048608 | tf_op jit(solution)/shard_map/ppermute | solution.py:243
  61.0 2.6 %conv_kernel.2.refs_6_ = bf16[8192,128]{1,0:T(8,128)(2,1)} custom-call(bf16[4096,128]{1,0:T(8,128)(2,1)} %collective-permute-done.2.refs_0_, bf16[8192,128]{1,0:T(8,128)(2,1)} %bitcast.22, bf16[8192,128]{1,0:T(8,128)(2,1)} %bitcast.26, f32[512,256]{1,0:T(8,128)} %taps_spectra.1.refs_3_.refs_2_, ...), custom_call_target="tpu_custom_call", output_to_operand_aliasing={{}: (6, {})} | custom-call | tf_op jit(solution)/shard_map/conv_kernel/pallas_call | solution.py:161
  63.7 1.0 %collective-permute-start.10 = (f32[128,128]{1,0:T(8,128)S(1)}, f32[128,128]{1,0:T(8,128)S(1)}, u32[]{:S(2)}, u32[]{:S(2)}) collective-permute-start(f32[128,128]{1,0:T(8,128)S(1)} %add_add_fusion.1), channel_id=1, source_target_pairs={{0,32},{1,33},{2,34},{3,35},{4,36},{5,37},{6,38},{7,39},{8,40},{9,... | collective-permute-start | bytes 196616 | tf_op jit(solution)/shard_map/ppermute | solution.py:182
  64.8 2.3 %collective-permute-start.11 = (f32[128,128]{1,0:T(8,128)S(1)}, f32[128,128]{1,0:T(8,128)S(1)}, u32[]{:S(2)}, u32[]{:S(2)}) collective-permute-start(f32[128,128]{1,0:T(8,128)S(1)} %add_add_fusion.1), channel_id=1, source_target_pairs={{0,96},{1,97},{2,98},{3,99},{4,100},{5,101},{6,102},{7,103},{8,104... | collective-permute-start | bytes 196616 | tf_op jit(solution)/shard_map/ppermute | solution.py:182
  67.0 1.3 %collective-permute-start.12 = (f32[128,128]{1,0:T(8,128)S(1)}, f32[128,128]{1,0:T(8,128)S(1)}, u32[]{:S(2)}, u32[]{:S(2)}) collective-permute-start(f32[128,128]{1,0:T(8,128)S(1)} %add_add_fusion.1), channel_id=1, source_target_pairs={{0,64},{1,65},{2,66},{3,67},{4,68},{5,69},{6,70},{7,71},{8,72},{9,... | collective-permute-start | bytes 196616 | tf_op jit(solution)/shard_map/ppermute | solution.py:182
  68.3 4.5 %corr_kernel.1 = bf16[8192,128]{1,0:T(8,128)(2,1)} custom-call(bf16[4096,128]{1,0:T(8,128)(2,1)} %collective-permute-done.4.refs_0_, bf16[4096,128]{1,0:T(8,128)(2,1)} %multiply_convert_fusion.refs_4_.refs_1_, f32[512,256]{1,0:T(8,128)} %taps_spectra.1.refs_3_.refs_2_, ...), custom_call_target="tpu_custom_call", output_to_operand_aliasing={{}: (5, {})} | custom-call | flops 5000000000 | bytes 50000000 | tf_op jit(solution)/shard_map/corr_kernel/pallas_call | solution.py:161
  73.0 3.2 %collective-permute-start.14 = (f32[128,128]{1,0:T(8,128)S(1)}, f32[128,128]{1,0:T(8,128)S(1)}, u32[]{:S(2)}, u32[]{:S(2)}) collective-permute-start(f32[128,128]{1,0:T(8,128)S(1)} %add_add_fusion), channel_id=1, source_target_pairs={{0,12},{1,13},{2,14},{3,15},{4,0},{5,1},{6,2},{7,3},{8,4},{9,5},{1... | collective-permute-start | bytes 196616 | tf_op jit(solution)/shard_map/ppermute | solution.py:182
  76.2 4.6 %conv_kernel.3 = bf16[8192,128]{1,0:T(8,128)(2,1)} custom-call(bf16[4096,128]{1,0:T(8,128)(2,1)} %collective-permute-done.2.refs_0_, bf16[8192,128]{1,0:T(8,128)(2,1)} %bitcast.23, bf16[8192,128]{1,0:T(8,128)(2,1)} %bitcast.27, f32[512,256]{1,0:T(8,128)} %taps_spectra.1.refs_3_.refs_2_, ...), custom_call_target="tpu_custom_call", output_to_operand_aliasing={{}: (6, {})} | custom-call | flops 5000000000 | bytes 50000000 | tf_op jit(solution)/shard_map/conv_kernel/pallas_call | solution.py:161
  80.8 1.1 %collective-permute-done.15 = f32[128,128]{1,0:T(8,128)S(1)} collective-permute-done((f32[128,128]{1,0:T(8,128)S(1)}, f32[128,128]{1,0:T(8,128)S(1)}, u32[]{:S(2)}, u32[]{:S(2)}) %collective-permute-start.15) | collective-permute-done | bytes 65568 | tf_op jit(solution)/shard_map/ppermute | solution.py:182
  (37 shorter events, 2.3 us)
Async XLA Ops:
  0.6 4.6 %copy-start.5 = (f32[128,128]{1,0:T(8,128)S(1)}, f32[128,128]{1,0:T(8,128)}, u32[]{:S(2)}) copy-start(f32[128,128]{1,0:T(8,128)} %param.12) | copy-start | bytes 196612
  0.6 4.7 %copy-start = (bf16[1,8192,128]{2,1,0:T(8,128)(2,1)S(1)}, bf16[1,8192,128]{2,1,0:T(8,128)(2,1)}, u32[]{:S(2)}) copy-start(bf16[1,8192,128]{2,1,0:T(8,128)(2,1)} %param.10) | copy-start | bytes 6291460
  0.7 4.6 %collective-permute-start = (f32[128,128]{1,0:T(8,128)}, f32[128,128]{1,0:T(8,128)S(1)}, u32[]{:S(2)}, u32[]{:S(2)}) collective-permute-start(f32[128,128]{1,0:T(8,128)} %param.12), channel_id=1, source_target_pairs={{0,2},{1,3},{2,0},{3,1},{4,6},{5,7},{6,4},{7,5},{8,10},{9,11},{10,... | collective-permute-start | bytes 196616 | tf_op jit(solution)/shard_map/ppermute | solution.py:182
  5.2 10.4 %copy-start.3 = (f32[2,128,128]{2,1,0:T(8,128)}, f32[2,128,128]{2,1,0:T(8,128)S(1)}, u32[]{:S(2)}) copy-start(f32[2,128,128]{2,1,0:T(8,128)S(1)} %maximum_select_fusion.column) | copy-start | bytes 393220
  5.2 10.3 %copy-start.1 = (bf16[1,8192,128]{2,1,0:T(8,128)(2,1)S(1)}, bf16[1,8192,128]{2,1,0:T(8,128)(2,1)}, u32[]{:S(2)}) copy-start(bf16[1,8192,128]{2,1,0:T(8,128)(2,1)} %param.11) | copy-start | bytes 6291460
  5.3 10.3 %copy-start.2 = (bf16[1,8192,128]{2,1,0:T(8,128)(2,1)S(1)}, bf16[1,8192,128]{2,1,0:T(8,128)(2,1)}, u32[]{:S(2)}) copy-start(bf16[1,8192,128]{2,1,0:T(8,128)(2,1)} %param.9) | copy-start | bytes 6291460
  5.3 9.3 %collective-permute-start.1 = (f32[2,128,128]{2,1,0:T(8,128)S(1)}, f32[2,128,128]{2,1,0:T(8,128)S(1)}, u32[]{:S(2)}, u32[]{:S(2)}) collective-permute-start(f32[2,128,128]{2,1,0:T(8,128)S(1)} %maximum_select_fusion.column), channel_id=1, source_target_pairs={{0,1},{1,0},{2,3},{3,2},{4,5},{5,4},{6,7},{7,6},{8,9},{9,8},{10,11... | collective-permute-start | bytes 393224 | tf_op jit(solution)/shard_map/ppermute | solution.py:182
  5.5 33.1 %collective-permute-start.3 = (bf16[4096,128]{1,0:T(8,128)(2,1)S(1)}, bf16[4096,128]{1,0:T(8,128)(2,1)}, u32[]{:S(2)}, u32[]{:S(2)}) collective-permute-start(bf16[4096,128]{1,0:T(8,128)(2,1)S(1)} %slice_bitcast_fusion), channel_id=1, source_target_pairs={{0,4},{4,8},{8,12},{12,16},{16,20},{20,24},{24,28},{28,32},{32,36}... | collective-permute-start | bytes 3145736 | tf_op jit(solution)/shard_map/ppermute | solution.py:239
  7.5 37.7 %collective-permute-start.5 = (bf16[4096,128]{1,0:T(8,128)(2,1)}, bf16[4096,128]{1,0:T(8,128)(2,1)}, u32[]{:S(2)}, u32[]{:S(2)}) collective-permute-start(bf16[4096,128]{1,0:T(8,128)(2,1)} %fusion.refs_1_), channel_id=1, source_target_pairs={{4,0},{8,4},{12,8},{16,12},{20,16},{24,20},{28,24},{32,28},{36,32}... | collective-permute-start | bytes 3145736 | tf_op jit(solution)/shard_map/ppermute | solution.py:240
  14.5 2.3 %copy-start.4 = (f32[2,128,128]{2,1,0:T(8,128)}, f32[2,128,128]{2,1,0:T(8,128)S(1)}, u32[]{:S(2)}) copy-start(f32[2,128,128]{2,1,0:T(8,128)S(1)} %collective-permute-done.1.near) | copy-start | bytes 393220
  15.6 45.5 %collective-permute-start.2 = (bf16[4096,128]{1,0:T(8,128)(2,1)}, bf16[4096,128]{1,0:T(8,128)(2,1)}, u32[]{:S(2)}, u32[]{:S(2)}) collective-permute-start(bf16[4096,128]{1,0:T(8,128)(2,1)} %slice.25), channel_id=1, source_target_pairs={{0,4},{4,8},{8,12},{12,16},{16,20},{20,24},{24,28},{28,32},{32,36}... | collective-permute-start | bytes 3145736 | tf_op jit(solution)/shard_map/ppermute | solution.py:243
  16.9 46.9 %collective-permute-start.4 = (bf16[4096,128]{1,0:T(8,128)(2,1)}, bf16[4096,128]{1,0:T(8,128)(2,1)}, u32[]{:S(2)}, u32[]{:S(2)}) collective-permute-start(bf16[4096,128]{1,0:T(8,128)(2,1)} %multiply_convert_fusion.refs_4_.refs_1_), channel_id=1, source_target_pairs={{4,0},{8,4},{12,8},{16,12},{20,16},{24,20},{28,24},{32,28},{36,32}... | collective-permute-start | bytes 3145736 | tf_op jit(solution)/shard_map/ppermute | solution.py:244
  52.6 1.4 %collective-permute-start.6 = (f32[2,128,128]{2,1,0:T(8,128)S(1)}, f32[2,128,128]{2,1,0:T(8,128)S(1)}, u32[]{:S(2)}, u32[]{:S(2)}) collective-permute-start(f32[2,128,128]{2,1,0:T(8,128)S(1)} %dynamic-slice_bitcast_fusion), channel_id=1, source_target_pairs={{0,1},{1,0},{2,3},{3,2},{4,5},{5,4},{6,7},{7,6},{8,9},{9,8},{10,11... | collective-permute-start | bytes 393224 | tf_op jit(solution)/shard_map/ppermute | solution.py:182
  55.0 8.7 %collective-permute-start.7 = (f32[128,128]{1,0:T(8,128)S(1)}, f32[128,128]{1,0:T(8,128)S(1)}, u32[]{:S(2)}, u32[]{:S(2)}) collective-permute-start(f32[128,128]{1,0:T(8,128)S(1)} %get-tuple-element.30), channel_id=1, source_target_pairs={{0,2},{1,3},{2,0},{3,1},{4,6},{5,7},{6,4},{7,5},{8,10},{9,11},{10,... | collective-permute-start | bytes 196616 | tf_op jit(solution)/shard_map/ppermute | solution.py:182
  55.7 7.9 %collective-permute-start.8 = (f32[128,128]{1,0:T(8,128)S(1)}, f32[128,128]{1,0:T(8,128)S(1)}, u32[]{:S(2)}, u32[]{:S(2)}) collective-permute-start(f32[128,128]{1,0:T(8,128)S(1)} %get-tuple-element.29), channel_id=1, source_target_pairs={{0,16},{1,17},{2,18},{3,19},{4,20},{5,21},{6,22},{7,23},{8,24},{9,... | collective-permute-start | bytes 196616 | tf_op jit(solution)/shard_map/ppermute | solution.py:182
  56.2 7.5 %collective-permute-start.9 = (f32[128,128]{1,0:T(8,128)S(1)}, f32[128,128]{1,0:T(8,128)S(1)}, u32[]{:S(2)}, u32[]{:S(2)}) collective-permute-start(f32[128,128]{1,0:T(8,128)S(1)} %get-tuple-element.30), channel_id=1, source_target_pairs={{0,18},{1,19},{2,16},{3,17},{4,22},{5,23},{6,20},{7,21},{8,26},{9,... | collective-permute-start | bytes 196616 | tf_op jit(solution)/shard_map/ppermute | solution.py:182
  63.7 9.1 %collective-permute-start.10 = (f32[128,128]{1,0:T(8,128)S(1)}, f32[128,128]{1,0:T(8,128)S(1)}, u32[]{:S(2)}, u32[]{:S(2)}) collective-permute-start(f32[128,128]{1,0:T(8,128)S(1)} %add_add_fusion.1), channel_id=1, source_target_pairs={{0,32},{1,33},{2,34},{3,35},{4,36},{5,37},{6,38},{7,39},{8,40},{9,... | collective-permute-start | bytes 196616 | tf_op jit(solution)/shard_map/ppermute | solution.py:182
  64.8 8.1 %collective-permute-start.11 = (f32[128,128]{1,0:T(8,128)S(1)}, f32[128,128]{1,0:T(8,128)S(1)}, u32[]{:S(2)}, u32[]{:S(2)}) collective-permute-start(f32[128,128]{1,0:T(8,128)S(1)} %add_add_fusion.1), channel_id=1, source_target_pairs={{0,96},{1,97},{2,98},{3,99},{4,100},{5,101},{6,102},{7,103},{8,104... | collective-permute-start | bytes 196616 | tf_op jit(solution)/shard_map/ppermute | solution.py:182
  67.0 5.8 %collective-permute-start.12 = (f32[128,128]{1,0:T(8,128)S(1)}, f32[128,128]{1,0:T(8,128)S(1)}, u32[]{:S(2)}, u32[]{:S(2)}) collective-permute-start(f32[128,128]{1,0:T(8,128)S(1)} %add_add_fusion.1), channel_id=1, source_target_pairs={{0,64},{1,65},{2,66},{3,67},{4,68},{5,69},{6,70},{7,71},{8,72},{9,... | collective-permute-start | bytes 196616 | tf_op jit(solution)/shard_map/ppermute | solution.py:182
  72.9 7.9 %collective-permute-start.13 = (f32[128,128]{1,0:T(8,128)S(1)}, f32[128,128]{1,0:T(8,128)S(1)}, u32[]{:S(2)}, u32[]{:S(2)}) collective-permute-start(f32[128,128]{1,0:T(8,128)S(1)} %add_add_fusion), channel_id=1, source_target_pairs={{0,4},{1,5},{2,6},{3,7},{4,8},{5,9},{6,10},{7,11},{8,12},{9,13},{1... | collective-permute-start | bytes 196616 | tf_op jit(solution)/shard_map/ppermute | solution.py:182
  73.0 7.9 %collective-permute-start.14 = (f32[128,128]{1,0:T(8,128)S(1)}, f32[128,128]{1,0:T(8,128)S(1)}, u32[]{:S(2)}, u32[]{:S(2)}) collective-permute-start(f32[128,128]{1,0:T(8,128)S(1)} %add_add_fusion), channel_id=1, source_target_pairs={{0,12},{1,13},{2,14},{3,15},{4,0},{5,1},{6,2},{7,3},{8,4},{9,5},{1... | collective-permute-start | bytes 196616 | tf_op jit(solution)/shard_map/ppermute | solution.py:182
  76.2 5.8 %collective-permute-start.15 = (f32[128,128]{1,0:T(8,128)S(1)}, f32[128,128]{1,0:T(8,128)S(1)}, u32[]{:S(2)}, u32[]{:S(2)}) collective-permute-start(f32[128,128]{1,0:T(8,128)S(1)} %add_add_fusion), channel_id=1, source_target_pairs={{0,8},{1,9},{2,10},{3,11},{4,12},{5,13},{6,14},{7,15},{8,0},{9,1},... | collective-permute-start | bytes 196616 | tf_op jit(solution)/shard_map/ppermute | solution.py:182
